TPU v7x, 32 devices: a whole 2x2x4 slice. The times are simulated.
32 devices in a mesh: dp: 8 (over z, x), seq: 4 (over y, core).
Axes of the slice: x: 2, y: 2, z: 4, core: 2. Of those that a mesh axis runs over, the one named last changes fastest.
Arguments:
- inputs: bfloat16 [8, 1024, 768], P('dp', 'seq'), may hold values from -6 to 6
- w_query: bfloat16 [768, 768], replicated, may hold values from -0.21875 to 0.21875
- query_bias: bfloat16 [768], replicated, may hold values from -4 to 4
- w_key: bfloat16 [768, 768], replicated, may hold values from -0.21875 to 0.21875
- w_value: bfloat16 [768, 768], replicated, may hold values from -0.21875 to 0.21875
- value_bias: bfloat16 [768], replicated, may hold values from -0.75 to 0.75
- w_proj: bfloat16 [768, 768], replicated, may hold values from -3 to 3
- proj_bias: bfloat16 [768], replicated, may hold values from -4 to 4
- ln1_gain: bfloat16 [768], replicated, may hold values from 0.5 to 1.5
- ln1_bias: bfloat16 [768], replicated, may hold values from -4 to 4
- w_up: bfloat16 [768, 3072], replicated, may hold values from -0.21875 to 0.21875
- up_bias: bfloat16 [3072], replicated, may hold values from -4 to 4
- w_down: bfloat16 [3072, 768], replicated, may hold values from -0.109375 to 0.109375
- down_bias: bfloat16 [768], replicated, may hold values from -4 to 4
- ln2_gain: bfloat16 [768], replicated, may hold values from 0.5 to 1.5
- ln2_bias: bfloat16 [768], replicated, may hold values from -4 to 4
- long_group: int32 [8], P('dp'), may hold values from 0 to 1, as said below
- random_blocks: int32 [8, 16, 3], P('dp', 'seq'), may hold values from 1 to 14, as said below
- out_grad: bfloat16 [8, 1024, 768], P('dp', 'seq'), may hold values from -6 to 6
Outputs:
- layer_out: bfloat16 [8, 1024, 768], P('dp', 'seq')
- input_grad: float32 [8, 1024, 768], P('dp', 'seq')
- grad_w_query: float32 [768, 768], P('seq')
- grad_w_key: float32 [768, 768], P('seq')
- grad_w_value: float32 [768, 768], P('seq')
- grad_w_proj: float32 [768, 768], P('seq')
- grad_w_up: float32 [768, 3072], P('seq')
- grad_w_down: float32 [3072, 768], P('seq')
- grad_query_bias: float32 [768], replicated
- grad_value_bias: float32 [768], replicated
- grad_proj_bias: float32 [768], replicated
- grad_ln1_gain: float32 [768], replicated
- grad_ln1_bias: float32 [768], replicated
- grad_up_bias: float32 [3072], replicated
- grad_down_bias: float32 [768], replicated
- grad_ln2_gain: float32 [768], replicated
- grad_ln2_bias: float32 [768], replicated
Inputs may be any that keep to these rules, and one draw needn't show every extreme that they name: `long_group`: 1 marks a group holding one sequence of 1024 tokens, 0 a group holding 2 sequences of 512 tokens. `random_blocks`: for a block at relative position p of its sequence of n blocks, the 3 entries are distinct positions of the same sequence, none of them 0, n - 1, p - 1, p or p + 1; the entries of global blocks are not used.
All inputs are finite; a program needn't handle non-finite values.
Results may differ from a plain program's by a relative error of at most 0.018.
Values may be sent and summed in bfloat16 or wider, within the bound.
No kernel may reach another device: no remote copies, remote signals or barrier semaphores. Data moves between devices by JAX's collectives and lax.ppermute only.
A program may use at most 192 MiB of HBM per device.

v0:
```python
import jax
import jax.numpy as jnp
from jax import lax
from jax.experimental import pallas as pl
from jax.experimental.pallas import tpu as pltpu
from jax.sharding import PartitionSpec as P

D = 768
HEADS = 12
HEAD = 64
FF = 3072
BLOCK = 64
RAND = 3
SLOTS = 2
SLOT_TOK = 128
T_DEV = 256
PER_SLOT = SLOT_TOK // BLOCK
PER_DEV = T_DEV // BLOCK

LN_EPS = 1e-05
MASKED = -1e30
F32 = jnp.float32
BF16 = jnp.bfloat16
MIB = 2**20

NN = (((1,), (0,)), ((), ()))
NT = (((1,), (1,)), ((), ()))
TN = (((0,), (0,)), ((), ()))


def dot(left, right, dims=NN):
    return lax.dot_general(left, right, dims, preferred_element_type=F32)


def seq_coords(blocks, is_long):
    device = blocks // PER_DEV
    within = blocks % PER_DEV
    slot_id = jnp.where(is_long, 0, within // PER_SLOT)
    position = jnp.where(is_long, blocks, device * PER_SLOT + within % PER_SLOT)
    return (slot_id, position)


def block_bias(device, chosen, is_long, n_seq):
    total_blocks = PER_DEV * n_seq
    last_pos = jnp.where(is_long, total_blocks, total_blocks // SLOTS) - 1
    own_slot, own_pos = seq_coords(device * PER_DEV + jnp.arange(PER_DEV), is_long)
    columns = jnp.arange(total_blocks)
    key_ids = (device ^ (columns // PER_DEV)) * PER_DEV + columns % PER_DEV
    key_slot, key_pos = seq_coords(key_ids, is_long)
    same = own_slot[:, None] == key_slot[None, :]
    ends = (key_pos == 0) | (key_pos == last_pos)
    near = jnp.abs(own_pos[:, None] - key_pos[None, :]) <= 1
    drawn = jnp.any(chosen[:, :, None] == key_pos[None, None, :], axis=1)
    is_global = (own_pos == 0) | (own_pos == last_pos)
    keep = same & (is_global[:, None] | ends[None, :] | near | drawn)
    return jnp.where(keep, 0.0, MASKED).astype(F32)


def joined(refs):
    return jnp.concatenate([ref[...] for ref in refs])


def attn_fwd_kernel(q_ref, bias_ref, *refs, parts):
    k_refs, v_refs, (mixed_ref, lse_ref) = refs[:parts], refs[parts : 2 * parts], refs[2 * parts :]
    query, key, value, bias = q_ref[...], joined(k_refs), joined(v_refs), bias_ref[...]
    rows, keys = query.shape[0], key.shape[0]
    first = lax.broadcasted_iota(jnp.int32, (rows, 2 * HEAD), 1) < HEAD
    outs, lses = [], []
    for head in range(2):
        own = jnp.where(first == (head == 0), query, jnp.zeros_like(query))
        scores = dot(own, key, NT).reshape(PER_DEV, BLOCK, keys) + bias[:, None, :]
        scores = scores.reshape(rows, keys)
        peak = jnp.max(scores, axis=1, keepdims=True)
        weight = jnp.exp(scores - peak)
        total = jnp.sum(weight, axis=1, keepdims=True)
        outs.append(dot((weight * (1.0 / total)).astype(BF16), value))
        lses.append(peak + jnp.log(total))
    mixed_ref[...] = jnp.where(first, outs[0], outs[1]).astype(BF16)
    lse_ref[...] = jnp.where(first, lses[0], lses[1])


def attn_bwd_kernel(q_ref, bias_ref, g_ref, lse_ref, *refs, parts):
    k_refs, v_refs, (dq_ref, dk_ref, dv_ref) = (
        refs[:parts],
        refs[parts : 2 * parts],
        refs[2 * parts :],
    )
    query, key, value, bias, grad = (
        q_ref[...],
        joined(k_refs),
        joined(v_refs),
        bias_ref[...],
        g_ref[...],
    )
    rows, keys = query.shape[0], key.shape[0]
    first = lax.broadcasted_iota(jnp.int32, (rows, 2 * HEAD), 1) < HEAD
    d_query, d_key, d_value = [], None, None
    for head in range(2):
        mine = first == (head == 0)
        own = jnp.where(mine, query, jnp.zeros_like(query))
        own_grad = jnp.where(mine, grad, jnp.zeros_like(grad))
        scores = dot(own, key, NT).reshape(PER_DEV, BLOCK, keys) + bias[:, None, :]
        probs = jnp.exp(scores.reshape(rows, keys) - lse_ref[:, HEAD * head : HEAD * head + 1])
        d_probs = dot(own_grad, value, NT)
        delta = jnp.sum(probs * d_probs, axis=1, keepdims=True)
        d_scores = (probs * (d_probs - delta)).astype(BF16)
        d_query.append(dot(d_scores, key))
        key_term = dot(d_scores, own, TN)
        value_term = dot(probs.astype(BF16), own_grad, TN)
        d_key = key_term if d_key is None else d_key + key_term
        d_value = value_term if d_value is None else d_value + value_term
    dq_ref[...] = jnp.where(first, d_query[0], d_query[1]).astype(BF16)
    dk_ref[...] = d_key.astype(BF16)
    dv_ref[...] = d_value.astype(BF16)


def cost(microseconds):
    return pl.CostEstimate(flops=int(microseconds * 1.1e9), bytes_accessed=0, transcendentals=0)


def head_pair(rows):
    return pl.BlockSpec((rows, 2 * HEAD), lambda i: (0, i))


def whole(shape):
    return pl.BlockSpec(shape, lambda *_: (0,) * len(shape))


def attn_fwd(query, bias, keys, values):
    rows = query.shape[0]
    return pl.pallas_call(
        lambda *refs: attn_fwd_kernel(*refs, parts=len(keys)),
        grid=(HEADS // 2,),
        in_specs=[head_pair(rows), whole(bias.shape)] + [head_pair(rows)] * (2 * len(keys)),
        out_specs=[head_pair(rows), head_pair(rows)],
        out_shape=[
            jax.ShapeDtypeStruct((rows, D), BF16),
            jax.ShapeDtypeStruct((rows, D), F32),
        ],
        compiler_params=pltpu.CompilerParams(vmem_limit_bytes=16 * MIB),
        cost_estimate=cost(10),
        name="attn_fwd",
    )(query, bias, *keys, *values)


def attn_bwd(query, bias, keys, values, grad, lse):
    rows = query.shape[0]
    count = rows * len(keys)
    return pl.pallas_call(
        lambda *refs: attn_bwd_kernel(*refs, parts=len(keys)),
        grid=(HEADS // 2,),
        in_specs=[head_pair(rows), whole(bias.shape), head_pair(rows), head_pair(rows)]
        + [head_pair(rows)] * (2 * len(keys)),
        out_specs=[head_pair(rows), head_pair(count), head_pair(count)],
        out_shape=[
            jax.ShapeDtypeStruct((rows, D), BF16),
            jax.ShapeDtypeStruct((count, D), BF16),
            jax.ShapeDtypeStruct((count, D), BF16),
        ],
        compiler_params=pltpu.CompilerParams(vmem_limit_bytes=24 * MIB),
        cost_estimate=cost(0.01),
        name="attn_bwd",
    )(query, bias, grad, lse, *keys, *values)


LANES = 384
QUARTERS = 4


def slot_of(quarter):
    return 2 * (quarter % 2) + quarter // 2


def half_share_kernel(place_ref, *refs, plan, low):
    keep_ref, send_ref, stage, turned = refs[4 * len(plan) :]
    top, low_own, x_own, z_own = (place_ref[i] for i in range(4))
    offset = 0
    for index, (rows, cols) in enumerate(plan):
        sides = (refs[4 * index : 4 * index + 2], refs[4 * index + 2 : 4 * index + 4])
        half = rows // 2
        share = half // low
        strip = min(half, LANES)
        piece_rows = share // QUARTERS
        for start in range(0, half, strip):
            lanes = pl.ds(pl.multiple_of(top * half + start, 128), strip)
            for side, (left, _) in enumerate(sides):
                turned[0:strip, side * T_DEV : (side + 1) * T_DEV] = left[:, lanes].T
            for block in range(cols // D):
                grad = sum(
                    dot(
                        turned[0:strip, side * T_DEV : (side + 1) * T_DEV],
                        right[:, block * D : (block + 1) * D],
                    )
                    for side, (_, right) in enumerate(sides)
                )
                for part in range(D // LANES):
                    column = block * D + part * LANES
                    side_x = column // (cols // 2)
                    slot = offset + (column % (cols // 2)) // LANES * piece_rows
                    for row in range(0, strip, piece_rows):
                        at = start + row
                        low_other = at // share
                        quarter = at % share // piece_rows
                        stage[
                            low_other ^ low_own,
                            side_x ^ x_own,
                            slot_of(quarter ^ z_own),
                            slot : slot + piece_rows,
                            :,
                        ] = grad[
                            row : row + piece_rows, part * LANES : (part + 1) * LANES
                        ].astype(BF16)
        offset += piece_rows * (cols // 2 // LANES)
    keep_ref[...] = stage[0 : low // 2]
    send_ref[...] = stage[low // 2 : low]


VMEM_SPEC = pl.BlockSpec(memory_space=pltpu.VMEM)
SMEM_SPEC = pl.BlockSpec(memory_space=pltpu.SMEM)


def half_share_grads(place, weights, n_seq, name):
    low = n_seq // 2
    plan = [(w[0].shape[1], w[1].shape[1]) for w in weights]
    piece_rows = sum(r // n_seq // QUARTERS * (c // 2 // LANES) for r, c in plan)
    shape = (2, QUARTERS, piece_rows, LANES)
    return pl.pallas_call(
        lambda *refs: half_share_kernel(*refs, plan=plan, low=low),
        in_specs=[SMEM_SPEC] + [VMEM_SPEC] * (4 * len(weights)),
        out_specs=[VMEM_SPEC] * 2,
        out_shape=[jax.ShapeDtypeStruct((low // 2, *shape), BF16)] * 2,
        scratch_shapes=[pltpu.VMEM((low, *shape), BF16), pltpu.VMEM((LANES, 2 * T_DEV), BF16)],
        compiler_params=pltpu.CompilerParams(vmem_limit_bytes=20 * MIB),
        cost_estimate=cost(0.01),
        name=name,
    )(place, *[array for weight in weights for array in weight])


def full_share_kernel(place_ref, dq_ref, dk_ref, dv_ref, sums_ref, *refs, n_seq):
    tokens, (keep_ref, send_ref, small_ref, stage, turned) = refs[:n_seq], refs[n_seq:]
    small_ref[2:, :] = sums_ref[2:, :]
    small_ref[0:1, :] = jnp.sum(dq_ref[...].astype(F32), axis=0, keepdims=True) * 0.125
    small_ref[1:2, :] = jnp.sum(dv_ref[...].astype(F32), axis=0, keepdims=True)
    top, low_own, x_own, z_own = (place_ref[i] for i in range(4))
    seq_own = top * (n_seq // 2) + low_own
    share = D // n_seq
    piece_rows = share // QUARTERS
    for start in range(0, D, LANES):
        for index, part in enumerate(tokens):
            turned[:, index * T_DEV : (index + 1) * T_DEV] = part[:, start : start + LANES].T
        for index, right in enumerate((dq_ref, dk_ref, dv_ref)):
            if index == 0:
                grad = dot(turned[:, 0:T_DEV], right[...]) * 0.125
            else:
                grad = dot(turned[...], right[...])
            for part in range(D // LANES):
                for row in range(0, LANES, piece_rows):
                    at = start + row
                    relative = (at // share) ^ seq_own
                    stage[
                        relative % 2 * (n_seq // 2) + relative // 2,
                        part ^ x_own,
                        slot_of((at % share // piece_rows) ^ z_own),
                        index * piece_rows : (index + 1) * piece_rows,
                        :,
                    ] = grad[row : row + piece_rows, part * LANES : (part + 1) * LANES].astype(BF16)
    keep_ref[...] = stage[0 : n_seq // 2]
    send_ref[...] = stage[n_seq // 2 : n_seq]


def full_share_grads(place, tokens, d_query, d_key, d_value, sums):
    n_seq = len(tokens)
    piece_rows = 3 * (D // n_seq // QUARTERS)
    shape = (2, QUARTERS, piece_rows, LANES)
    return pl.pallas_call(
        lambda *refs: full_share_kernel(*refs, n_seq=n_seq),
        in_specs=[SMEM_SPEC] + [VMEM_SPEC] * (4 + n_seq),
        out_specs=[VMEM_SPEC] * 3,
        out_shape=[jax.ShapeDtypeStruct((n_seq // 2, *shape), BF16)] * 2
        + [jax.ShapeDtypeStruct(sums.shape, F32)],
        scratch_shapes=[
            pltpu.VMEM((n_seq, *shape), BF16),
            pltpu.VMEM((LANES, n_seq * T_DEV), BF16),
        ],
        compiler_params=pltpu.CompilerParams(vmem_limit_bytes=20 * MIB),
        cost_estimate=cost(0.01),
        name="grads_qkv",
    )(place, d_query, d_key, d_value, sums, *tokens)


def assemble_kernel(place_ref, *refs, plan):
    outs = refs[len(refs) - len(plan) :]
    x_own, z_own = place_ref[2], place_ref[3]
    index = 0
    for ref in refs[: len(refs) - len(plan)]:
        for slot in range(ref.shape[0]):
            relative, column = index % QUARTERS, index // QUARTERS
            quarter = slot_of(relative) ^ z_own
            offset = 0
            for out, (rows, cols) in zip(outs, plan):
                height = rows // QUARTERS
                at = pl.ds(pl.multiple_of(quarter * height, 8), height)
                for part in range(cols // 2 // LANES):
                    lanes = pl.ds(
                        pl.multiple_of((column ^ x_own) * (cols // 2) + part * LANES, 128), LANES
                    )
                    out[at, lanes] = ref[slot, offset : offset + height, :].astype(F32)
                    offset += height
            index += 1


def assemble(place, pieces, plan, name):
    return pl.pallas_call(
        lambda *refs: assemble_kernel(*refs, plan=plan),
        in_specs=[SMEM_SPEC] + [VMEM_SPEC] * len(pieces),
        out_specs=[VMEM_SPEC] * len(plan),
        out_shape=[jax.ShapeDtypeStruct(shape, F32) for shape in plan],
        compiler_params=pltpu.CompilerParams(vmem_limit_bytes=12 * MIB),
        cost_estimate=cost(0.01),
        name=name,
    )(place, *pieces)


def swap(value, axis, mask):
    size = lax.axis_size(axis)
    return lax.ppermute(value, axis, [(i, i ^ mask) for i in range(size)])


def summed(terms):
    total = terms[0].astype(F32)
    for term in terms[1:]:
        total = total + term.astype(F32)
    return total.astype(BF16)


class Order:
    def __init__(self):
        self.last = ()

    def after(self, *arrays):
        return lax.optimization_barrier((*arrays, *self.last))[: len(arrays)]

    def mark(self, *arrays):
        self.last = arrays


def exchange(order, sends, swaps):
    order.mark(*sends)
    return [swap(send, axis, mask) for send, (axis, mask) in zip(sends, swaps)]


def sum_seq(order, keep, send, seq_masks):
    got = exchange(order, [send], [("seq", seq_masks[0])])
    yield
    terms = [keep, *order.after(*got)]
    for mask in seq_masks[1:]:
        half = terms[0].shape[0] // 2
        got = exchange(order, [summed([t[half:] for t in terms])], [("seq", mask)])
        yield
        terms = [t[:half] for t in terms] + list(order.after(*got))
    return [t[0] for t in terms]


def sum_dp_rest(order, piece):
    step = 2 * QUARTERS
    while step < lax.axis_size("dp"):
        got = exchange(order, [piece], [("dp", step)])
        yield
        piece = summed([piece, *order.after(*got)])
        step *= 2
    return piece


def gather_dp(order, own):
    for mask in (4, 2):
        got = exchange(order, [own], [("dp", mask)])
        yield
        own = jnp.concatenate([own, *order.after(*got)])
    got = exchange(order, [own], [("dp", 1)])
    yield
    (other,) = order.after(*got)
    return [own, other]


def columns_first(order, keep, send, seq_masks):
    terms = yield from sum_seq(order, keep, send, seq_masks)
    got = exchange(order, [summed([t[1] for t in terms])], [("dp", 1)])
    yield
    terms = [t[0] for t in terms] + list(order.after(*got))
    for mask in (2, 4):
        half = terms[0].shape[0] // 2
        got = exchange(order, [summed([t[half:] for t in terms])], [("dp", mask)])
        yield
        terms = [t[:half] for t in terms] + list(order.after(*got))
    piece = yield from sum_dp_rest(order, summed(terms))
    return (yield from gather_dp(order, piece))


def halves_first(order, keep, send, seq_masks):
    terms = yield from sum_seq(order, keep, send, seq_masks)
    half = QUARTERS // 2
    got = exchange(order, [summed([t[:, half:] for t in terms])], [("dp", 2)])
    yield
    terms = [t[:, :half] for t in terms] + list(order.after(*got))
    got = exchange(order, [summed([t[1] for t in terms])], [("dp", 1)])
    yield
    terms = [t[0] for t in terms] + list(order.after(*got))
    got = exchange(order, [summed([t[1:] for t in terms])], [("dp", 4)])
    yield
    piece = summed([t[:1] for t in terms] + list(order.after(*got)))
    piece = yield from sum_dp_rest(order, piece)
    return (yield from gather_dp(order, piece))


def token_kernel(dk_ref, dv_ref, wk_ref, wv_ref, small_ref, keep_ref, send_ref, *, n_seq):
    for part in range(n_seq):
        rows = slice(part * T_DEV, (part + 1) * T_DEV)
        term = dot(dk_ref[rows, :], wk_ref[...], NT) + dot(dv_ref[rows, :], wv_ref[...], NT)
        out = send_ref if part % 2 else keep_ref
        out[part // 2 * T_DEV : (part // 2 + 1) * T_DEV, :] = term.astype(BF16)
    small = small_ref[...]
    high = small.astype(BF16)
    at = n_seq // 2 * T_DEV
    send_ref[at : at + SMALL_ROWS, :] = high
    send_ref[at + SMALL_ROWS : at + 2 * SMALL_ROWS, :] = (small - high.astype(F32)).astype(BF16)


def token_terms(d_key, d_value, w_key, w_value, small, n_seq):
    rows = n_seq // 2 * T_DEV
    return pl.pallas_call(
        lambda *refs: token_kernel(*refs, n_seq=n_seq),
        in_specs=[VMEM_SPEC] * 5,
        out_specs=[VMEM_SPEC] * 2,
        out_shape=[
            jax.ShapeDtypeStruct((rows, D), BF16),
            jax.ShapeDtypeStruct((rows + 2 * SMALL_ROWS, D), BF16),
        ],
        compiler_params=pltpu.CompilerParams(vmem_limit_bytes=20 * MIB),
        cost_estimate=cost(12),
        name="token_terms",
    )(d_key, d_value, w_key, w_value, small)


def token_chain(order, keep, send, small, masks):
    n_dp = lax.axis_size("dp")
    terms = [keep]
    for step, mask in enumerate(masks):
        half = terms[0].shape[0] // 2
        high = small.astype(BF16)
        rest = (small - high.astype(F32)).astype(BF16)
        if step:
            send = jnp.concatenate([summed([t[half:] for t in terms]), high, rest])
            terms = [t[:half] for t in terms]
        got = exchange(order, [send], [("seq", mask)])
        yield
        (got,) = order.after(*got)
        at = terms[0].shape[0]
        small = high.astype(F32) + rest.astype(F32)
        small = small + got[at : at + SMALL_ROWS].astype(F32) + got[at + SMALL_ROWS :].astype(F32)
        terms = terms + [got[:at]]
    total = sum(t.astype(F32) for t in terms)
    step = 1
    while step < n_dp:
        got = exchange(order, [small], [("dp", step)])
        yield
        small = small + order.after(*got)[0]
        step *= 2
    return total, small


def finish(chain):
    try:
        next(chain)
    except StopIteration as stop:
        return stop.value
    raise ValueError("steps left")


VECTORS = ("proj_bias", "ln1_gain", "ln1_bias", "down_bias", "ln2_gain", "ln2_bias")
FF_CHUNK = 768
PACK = 1024
SMALL_ROWS = 16
GELU_SCALE = 0.7978845608028654
GELU_CUBE = 0.044715


def rows_mean(array):
    return jnp.mean(array, axis=1, keepdims=True)


def rows_sum(array):
    return jnp.sum(array, axis=0, keepdims=True)


def norm_back(grad, xhat, inv, gain):
    scaled = grad * gain
    return inv * (scaled - rows_mean(scaled) - xhat * rows_mean(scaled * xhat))


def layer_kernel(
    x_ref, mixed_ref, grad_ref, proj_ref, up_ref, down_ref, packed_ref, *refs, own
):
    slope = refs[-1]
    normed_ref, hidden_ref, d_branch_ref, d_pre_ref, d_attn_ref = refs[:5]
    chunks = [slice(start, start + FF_CHUNK) for start in range(0, FF, FF_CHUNK)]
    packed = [packed_ref[i * PACK : (i + 1) * PACK].astype(F32)[None, :] for i in range(9)]
    vec = {name: row[:, :D] for name, row in zip(VECTORS, packed)}
    up_bias = jnp.concatenate(packed[len(VECTORS) :], axis=1)
    resid = x_ref[...].astype(F32) + dot(mixed_ref[...], proj_ref[...]) + vec["proj_bias"]
    center = resid - rows_mean(resid)
    inv1 = lax.rsqrt(rows_mean(center * center) + LN_EPS)
    xhat1 = center * inv1
    normed = xhat1 * vec["ln1_gain"] + vec["ln1_bias"]
    normed_low = normed.astype(BF16)
    normed_ref[...] = normed_low
    branch = jnp.zeros_like(normed)
    for cols in chunks:
        pre = dot(normed_low, up_ref[:, cols]) + up_bias[:, cols]
        square = pre * pre
        bent = jnp.tanh(pre * (GELU_SCALE + GELU_SCALE * GELU_CUBE * square))
        half = 0.5 + 0.5 * bent
        slope[:, cols] = half + (0.5 * pre) * (1.0 - bent * bent) * (
            GELU_SCALE + 3.0 * GELU_SCALE * GELU_CUBE * square
        )
        hidden = (pre * half).astype(BF16)
        hidden_ref[:, cols] = hidden
        branch = branch + dot(hidden, down_ref[cols, :])
    resid = normed + (branch + vec["down_bias"])
    center = resid - rows_mean(resid)
    inv2 = lax.rsqrt(rows_mean(center * center) + LN_EPS)
    xhat2 = center * inv2
    grad = grad_ref[...].astype(F32)
    d_resid2 = norm_back(grad, xhat2, inv2, vec["ln2_gain"])
    d_branch = d_resid2.astype(BF16)
    d_branch_ref[...] = d_branch
    d_normed = d_resid2
    for index, cols in enumerate(chunks):
        d_hidden = dot(d_branch, down_ref[cols, :], NT).astype(BF16).astype(F32)
        d_pre = (d_hidden * slope[:, cols]).astype(BF16)
        d_pre_ref[:, cols] = d_pre
        if own:
            refs[7][5 + index : 6 + index, :] = rows_sum(d_pre.astype(F32))
        d_normed = d_normed + dot(d_pre, up_ref[:, cols], NT)
    d_resid1 = norm_back(d_normed, xhat1, inv1, vec["ln1_gain"])
    d_attn = d_resid1.astype(BF16)
    d_attn_ref[...] = d_attn
    if own:
        out_ref, resid_ref, sums_ref, d_mixed_ref = refs[5:9]
        out_ref[...] = (xhat2 * vec["ln2_gain"] + vec["ln2_bias"]).astype(BF16)
        resid_ref[...] = d_resid1
        sums_ref[0:2, :] = jnp.zeros((2, D), F32)
        sums_ref[2:3, :] = rows_sum(d_attn.astype(F32))
        sums_ref[3:4, :] = rows_sum(d_normed * xhat1)
        sums_ref[4:5, :] = rows_sum(d_normed)
        sums_ref[9:10, :] = rows_sum(d_branch.astype(F32))
        sums_ref[10:11, :] = rows_sum(grad * xhat2)
        sums_ref[11:12, :] = rows_sum(grad)
        sums_ref[12:, :] = jnp.zeros((SMALL_ROWS - 12, D), F32)
        d_mixed_ref[...] = dot(d_attn, proj_ref[...], NT).astype(BF16)


def after_attention(tokens, mixed, out_grad, weights, own):
    wide, tall = jax.ShapeDtypeStruct((T_DEV, FF), BF16), jax.ShapeDtypeStruct((T_DEV, D), BF16)
    names = ["normed_low", "hidden", "d_branch", "d_pre", "d_attn"]
    shapes = [tall, wide, tall, wide, tall]
    if own:
        names += ["layer_out", "d_resid1", "sums", "d_mixed"]
        shapes += [
            tall,
            jax.ShapeDtypeStruct((T_DEV, D), F32),
            jax.ShapeDtypeStruct((SMALL_ROWS, D), F32),
            tall,
        ]
    outs = pl.pallas_call(
        lambda *refs: layer_kernel(*refs, own=own),
        in_specs=[VMEM_SPEC] * (3 + len(weights)),
        out_specs=[VMEM_SPEC] * len(shapes),
        out_shape=shapes,
        scratch_shapes=[pltpu.VMEM((T_DEV, FF), F32)],
        compiler_params=pltpu.CompilerParams(vmem_limit_bytes=20 * MIB),
        cost_estimate=cost(9),
        name="layer_own" if own else "layer_other",
    )(tokens, mixed, out_grad, *weights)
    return dict(zip(names, outs))


def on_device(
    inputs,
    w_query,
    query_bias,
    w_key,
    w_value,
    value_bias,
    w_proj,
    proj_bias,
    ln1_gain,
    ln1_bias,
    w_up,
    up_bias,
    w_down,
    down_bias,
    ln2_gain,
    ln2_bias,
    long_group,
    random_blocks,
    out_grad,
):
    n_seq, n_dp = lax.axis_size("seq"), lax.axis_size("dp")
    device, dp = lax.axis_index("seq"), lax.axis_index("dp")
    low = n_seq // 2
    place = jnp.stack([device // low, device % low, dp % 2, dp // 2 % QUARTERS]).astype(jnp.int32)
    tok_rows = inputs.reshape(T_DEV, D)
    cotangent = out_grad.reshape(T_DEV, D)
    parts = [tok_rows] + [None] * (n_seq - 1)
    step = low
    while step > 1:
        for j in range(0, n_seq, 2 * step):
            parts[j + step] = swap(parts[j], "seq", step)
        step //= 2
    for j in range(0, n_seq, 2):
        parts[j + 1] = swap(parts[j], "seq", 1)
    cotangent_partner = swap(cotangent, "seq", low)
    bias = block_bias(device, random_blocks[0], long_group[0] == 1, n_seq)
    bias = jnp.repeat(bias, BLOCK, axis=1)
    vectors = (proj_bias, ln1_gain, ln1_bias, down_bias, ln2_gain, ln2_bias)
    packed = jnp.concatenate([jnp.pad(vector, (0, PACK - D)) for vector in vectors] + [up_bias])
    bias, packed = lax.optimization_barrier((bias, packed))
    weights = (w_proj, w_up, w_down, packed)

    query = ((dot(tok_rows, w_query) + query_bias) * 0.125).astype(BF16)
    keys = [dot(part, w_key).astype(BF16) for part in parts]
    values = [(dot(part, w_value) + value_bias).astype(BF16) for part in parts]
    mixed, lse = attn_fwd(query, bias, keys, values)
    mixed_partner = swap(mixed, "seq", low)
    own = after_attention(tok_rows, mixed, cotangent, weights, True)
    mixed_partner, own["d_attn"] = lax.optimization_barrier((mixed_partner, own["d_attn"]))
    other = after_attention(parts[low], mixed_partner, cotangent_partner, weights, False)
    down_terms = half_share_grads(
        place,
        [(own["hidden"], own["d_branch"], other["hidden"], other["d_branch"])],
        n_seq,
        "grads_down",
    )
    up_terms = half_share_grads(
        place,
        [
            (own["normed_low"], own["d_pre"], other["normed_low"], other["d_pre"]),
            (mixed, own["d_attn"], mixed_partner, other["d_attn"]),
        ],
        n_seq,
        "grads_up_proj",
    )
    order = Order()
    low_masks = [1 << i for i in reversed(range(n_seq.bit_length() - 2))]
    seq_masks = [1] + [1 << i for i in reversed(range(1, n_seq.bit_length() - 1))]
    down = halves_first(order, *down_terms, low_masks)
    next(down)
    up = columns_first(order, *up_terms, low_masks)
    next(up)
    for _ in low_masks:
        next(up)
        ups = order.last
        next(down)
        order.mark(*order.last, *ups)
    (d_mixed,) = order.after(own["d_mixed"])
    d_query, d_key, d_value = attn_bwd(query, bias, keys, values, d_mixed, lse)
    *qkv_terms, small = full_share_grads(place, parts, d_query, d_key, d_value, own["sums"])
    qkv = columns_first(order, *qkv_terms, seq_masks)
    next(qkv)
    next(up)
    next(down)
    d_key, d_value = order.after(d_key, d_value)
    token_parts = token_terms(d_key, d_value, w_key, w_value, small, n_seq)
    input_grad = own["d_resid1"] + 0.125 * dot(d_query, w_query, NT)
    tail = token_chain(order, *token_parts, small, seq_masks)
    next(tail)
    rest = n_dp.bit_length() - 4

    def advance(chain, more=0):
        for _ in range(1 + more):
            next(chain)

    square = (D // n_seq, D)
    for _ in seq_masks[1:]:
        advance(qkv)
    advance(up)
    for _ in seq_masks[1:]:
        advance(tail)
    advance(down)
    advance(up, rest)
    advance(qkv)
    advance(down, rest)
    advance(tail)
    advance(up)
    advance(qkv)
    advance(down)
    advance(tail)
    advance(up)
    advance(qkv)
    advance(down)
    advance(tail, rest)
    advance(qkv, rest)
    total, small = finish(tail)
    input_grad = input_grad + total
    order.mark(input_grad)
    small = small.reshape(-1)
    advance(qkv)
    grad_up, grad_proj = assemble(place, finish(up), [(D // n_seq, FF), square], "assemble_up")
    order.mark(grad_up)
    advance(qkv)
    (grad_down,) = assemble(place, finish(down), [(FF // n_seq, D)], "assemble_down")
    grad_query, grad_key, grad_value = assemble(place, finish(qkv), [square] * 3, "assemble_qkv")
    up_end = 5 * D + FF
    return (
        own["layer_out"].reshape(1, T_DEV, D),
        input_grad.reshape(1, T_DEV, D),
        grad_query,
        grad_key,
        grad_value,
        grad_proj,
        grad_up,
        grad_down,
        small[0:D],
        small[D : 2 * D],
        small[2 * D : 3 * D],
        small[3 * D : 4 * D],
        small[4 * D : 5 * D],
        small[5 * D : up_end],
        small[up_end : up_end + D],
        small[up_end + D : up_end + 2 * D],
        small[up_end + 2 * D : up_end + 3 * D],
    )


def solution(mesh):
    tokens = P("dp", "seq", None)
    return jax.shard_map(
        on_device,
        mesh=mesh,
        in_specs=(tokens,) + (P(),) * 15 + (P("dp"), tokens, tokens),
        out_specs=(tokens, tokens) + (P("seq", None),) * 6 + (P(),) * 9,
        check_vma=False,
    )
```

profile of v0, /device:TPU:0, one launch (start us, length us, event | category | flops | bytes accessed | tf_op | source)
XLA Modules:
  0.0 178.6 jit_solution(9844855156521098014)
XLA Ops:
  0.7 0.5 collective-permute-start
  1.2 2.6 %collective-permute-start.1 = (bf16[256,768]{1,0:T(8,128)(2,1)}, bf16[256,768]{1,0:T(8,128)(2,1)}, u32[]{:S(2)}, u32[]{:S(2)}) collective-permute-start(bf16[256,768]{1,0:T(8,128)(2,1)} %bitcast.91), channel_id=1, source_target_pairs={{0,2},{1,3},{2,0},{3,1},{4,6},{5,7},{6,4},{7,5},{8,10},{9,11},{10,... | collective-permute-start | bytes 1179656 | tf_op jit(solution)/shard_map/ppermute | solution.py:326
  4.7 0.7 convert_element_type.448
  5.3 0.7 copy.41
  6.0 0.7 constant_dynamic-update-slice_fusion.6
  6.7 1.9 %convolution_convert_fusion.3.refs_2_.refs_4_ = bf16[256,768]{1,0:T(8,128)(2,1)S(1)} fusion(bf16[768,768]{1,0:T(8,128)(2,1)} %refs_2_.1, bf16[1,256,768]{2,1,0:T(8,128)(2,1)} %param.19), kind=kOutput, calls=%fused_computation.19 | convolution fusion | flops 302186496 | bytes 1966080 | tf_op jit(solution)/shard_map/dot_general | solution.py:32
  8.7 1.2 fusion.3.refs_0_
  10.2 0.6 copy-done.6
  10.8 0.7 broadcast_in_dim.35
  11.5 0.8 reshape.609.refs_1_
  12.3 1.3 convert_element_type.454
  13.7 1.8 fusion.4.refs_6_.refs_8_
  16.0 0.7 copy-done.9
  17.4 1.5 convolution_convert_fusion.1.refs_4_.refs_6_
  18.9 1.5 fusion.6.refs_8_.refs_10_
  21.9 9.5 %attn_fwd.1 = (bf16[256,768]{1,0:T(8,128)(2,1)S(1)}, f32[256,768]{1,0:T(8,128)S(1)}) custom-call(bf16[256,768]{1,0:T(8,128)(2,1)S(1)} %copy-done.3, f32[4,1024]{1,0:T(4,128)S(1)} %reshape.609.refs_1_, bf16[256,768]{1,0:T(8,128)(2,1)S(1)} %convolution_convert_fusion.3.refs_2_.refs_4_, bf16[256,768]{1,0:T(8,128)(2,1)S(1)} %convolution_convert_fusion.2.refs_3_.refs_5_, ...), custom_call_target="tpu_custom_call" | custom-call | flops 11000000512 | tf_op jit(solution)/shard_map/attn_fwd/pallas_call | solution.py:131
  31.4 1.9 %collective-permute-start.3 = (bf16[256,768]{1,0:T(8,128)(2,1)S(1)}, bf16[256,768]{1,0:T(8,128)(2,1)S(1)}, u32[]{:S(2)}, u32[]{:S(2)}) collective-permute-start(bf16[256,768]{1,0:T(8,128)(2,1)S(1)} %get-tuple-element.85.refs_1_.refs_5_), channel_id=1, source_target_pairs={{0,2},{1,3},{2,0},{3,1},{4,6},{5,7},{6,4},{7,5},{8,10},{9,11},{10,... | collective-permute-start | bytes 1179656 | tf_op jit(solution)/shard_map/ppermute | solution.py:326
  33.4 9.1 %layer_own.1 = (bf16[256,768]{1,0:T(8,128)(2,1)S(1)}, bf16[256,3072]{1,0:T(8,128)(2,1)S(1)}, bf16[256,768]{1,0:T(8,128)(2,1)S(1)}, bf16[256,3072]{1,0:T(8,128)(2...) custom-call(bf16[256,768]{1,0:T(8,128)(2,1)S(1)} %bitcast.92, ...), custom_call_target="tpu_custom_call" | custom-call | flops 9900000256 | tf_op jit(solution)/shard_map/layer_own/pallas_call | solution.py:574
  42.4 0.7 collective-permute-done.3.refs_1_.refs_7_
  43.1 8.8 %layer_other.1 = (bf16[256,768]{1,0:T(8,128)(2,1)S(1)}, bf16[256,3072]{1,0:T(8,128)(2,1)S(1)}, bf16[256,768]{1,0:T(8,128)(2,1)S(1)}, bf16[256,3072]{1,0:T(8,128)(2,1)S(1)}, bf16[256,768]{1,0:T(8,128)(2,1)S(1)}) custom-call(bf16[256,768]{1,0:T(8,128)(2,1)} %collective-permute-done.1.refs_0_.refs_7_, ...), custom_call_target="tpu_custom_call" | custom-call | flops 9900000256 | tf_op jit(solution)/shard_map/layer_other/pallas_call | solution.py:574
  51.9 2.7 %grads_up_proj.1 = (bf16[1,2,4,240,384]{4,3,2,1,0:T(8,128)(2,1)S(1)}, bf16[1,2,4,240,384]{4,3,2,1,0:T(8,128)(2,1)S(1)}) custom-call(s32[4]{0:T(128)S(1)} %pad_add_fusion.refs_0_, bf16[256,768]{1,0:T(8,128)(2,1)S(1)} %get-tuple-element.98.refs_1_, bf16[256,3072]{1,0:T(8,128)(2,1)S(1)} %get-tuple-element.99.refs_2_, ...), custom_call_target="tpu_custom_call" | custom-call | flops 11000000 | tf_op jit(solution)/shard_map/grads_up_proj/pallas_call | solution.py:227
  54.7 2.2 %grads_down.1 = (bf16[1,2,4,192,384]{4,3,2,1,0:T(8,128)(2,1)S(1)}, bf16[1,2,4,192,384]{4,3,2,1,0:T(8,128)(2,1)S(1)}) custom-call(s32[4]{0:T(128)S(1)} %pad_add_fusion.refs_0_, bf16[256,3072]{1,0:T(8,128)(2,1)S(1)} %get-tuple-element.90.refs_1_, bf16[256,768]{1,0:T(8,128)(2,1)S(1)} %get-tuple-element.91.refs_2_, ...), custom_call_target="tpu_custom_call" | custom-call | flops 11000000 | tf_op jit(solution)/shard_map/grads_down/pallas_call | solution.py:227
  57.0 0.6 collective-permute-start.5
  58.2 1.8 collective-permute-start.8
  60.2 1.9 %collective-permute-start.7 = (bf16[2,2,192,384]{3,2,1,0:T(8,128)(2,1)S(1)}, bf16[2,2,192,384]{3,2,1,0:T(8,128)(2,1)S(1)}, u32[]{:S(2)}, u32[]{:S(2)}) collective-permute-start(bf16[2,2,192,384]{3,2,1,0:T(8,128)(2,1)S(1)} %add_convert_fusion.2), channel_id=1, source_target_pairs={{0,8},{4,12},{8,0},{12,4},{16,24},{20,28},{24,16},{28,20},{1,9},{5... | collective-permute-start | bytes 1769480 | tf_op jit(solution)/shard_map/ppermute | solution.py:326
  62.0 13.8 %attn_bwd.1 = (bf16[256,768]{1,0:T(8,128)(2,1)S(1)}, bf16[1024,768]{1,0:T(8,128)(2,1)S(1)}, bf16[1024,768]{1,0:T(8,128)(2,1)S(1)}) custom-call(bf16[256,768]{1,0:T(8,128)(2,1)S(1)} %copy-done.3, f32[4,1024]{1,0:T(4,128)S(1)} %reshape.609.refs_1_, bf16[256,768]{1,0:T(8,128)(2,1)S(1)} %get-tuple-element.108.refs_2_, ...), custom_call_target="tpu_custom_call" | custom-call | flops 11000000 | tf_op jit(solution)/shard_map/attn_bwd/pallas_call | solution.py:149
  75.8 4.5 %grads_qkv.1 = (bf16[2,2,4,144,384]{4,3,2,1,0:T(8,128)(2,1)S(1)}, bf16[2,2,4,144,384]{4,3,2,1,0:T(8,128)(2,1)S(1)}, f32[16,768]{1,0:T(8,128)S(1)}) custom-call(s32[4]{0:T(128)S(1)} %pad_add_fusion.refs_0_, bf16[256,768]{1,0:T(8,128)(2,1)S(1)} %get-tuple-element.110.refs_1_, bf16[1024,768]{1,0:T(8,128)(2,1)S(1)} %get-tuple-element.117.refs_2_.refs_0_, ...), custom_call_target="tpu_custom_call" | custom-call | flops 11000000 | tf_op jit(solution)/shard_map/grads_qkv/pallas_call | solution.py:275
  80.8 2.7 %token_terms.1 = (bf16[512,768]{1,0:T(8,128)(2,1)S(1)}, bf16[544,768]{1,0:T(8,128)(2,1)S(1)}) custom-call(bf16[1024,768]{1,0:T(8,128)(2,1)S(1)} %get-tuple-element.117.refs_2_.refs_0_, bf16[1024,768]{1,0:T(8,128)(2,1)S(1)} %get-tuple-element.118.refs_3_.refs_1_, bf16[768,768]{1,0:T(8,128)(2,1)S(1)} %copy-done.1, bf16[768,768]{1,0:T(8,128)(2,1)S(1)} %copy-done.9, ...), custom_call_target="tpu_custom_call" | custom-call | flops 13200000000 | tf_op jit(solution)/shard_map/token_terms/pallas_call | solution.py:430
  84.2 1.7 collective-permute-start.13
  86.1 1.6 collective-permute-start.15
  87.7 6.8 %collective-permute-done.10 = bf16[2,240,384]{2,1,0:T(8,128)(2,1)S(1)} collective-permute-done((bf16[2,240,384]{2,1,0:T(8,128)(2,1)S(1)}, bf16[2,240,384]{2,1,0:T(8,128)(2,1)S(1)}, u32[]{:S(2)}, u32[]{:S(2)}) %collective-permute-start.10) | collective-permute-done | bytes 368672 | tf_op jit(solution)/shard_map/ppermute | solution.py:326
  94.6 2.6 %collective-permute-start.16 = (bf16[1,240,384]{2,1,0:T(8,128)(2,1)S(1)}, bf16[1,240,384]{2,1,0:T(8,128)(2,1)S(1)}, u32[]{:S(2)}, u32[]{:S(2)}) collective-permute-start(bf16[1,240,384]{2,1,0:T(8,128)(2,1)S(1)} %fusion.16), channel_id=1, source_target_pairs={{0,16},{4,20},{8,24},{12,28},{16,0},{20,4},{24,8},{28,12},{1,17},{... | collective-permute-start | bytes 552968 | tf_op jit(solution)/shard_map/ppermute | solution.py:326
  97.4 1.6 collective-permute-start.12
  99.5 8.9 %collective-permute-done.16 = bf16[1,240,384]{2,1,0:T(8,128)(2,1)S(1)} collective-permute-done((bf16[1,240,384]{2,1,0:T(8,128)(2,1)S(1)}, bf16[1,240,384]{2,1,0:T(8,128)(2,1)S(1)}, u32[]{:S(2)}, u32[]{:S(2)}) %collective-permute-start.16) | collective-permute-done | bytes 184352 | tf_op jit(solution)/shard_map/ppermute | solution.py:326
  108.9 1.5 collective-permute-start.17
  110.4 3.2 %collective-permute-done.14 = bf16[1,192,384]{2,1,0:T(8,128)(2,1)S(1)} collective-permute-done((bf16[1,192,384]{2,1,0:T(8,128)(2,1)S(1)}, bf16[1,192,384]{2,1,0:T(8,128)(2,1)S(1)}, u32[]{:S(2)}, u32[]{:S(2)}) %collective-permute-start.14) | collective-permute-done | bytes 147488 | tf_op jit(solution)/shard_map/ppermute | solution.py:326
  113.7 3.0 %collective-permute-done.12 = bf16[288,768]{1,0:T(8,128)(2,1)S(1)} collective-permute-done((bf16[288,768]{1,0:T(8,128)(2,1)S(1)}, bf16[288,768]{1,0:T(8,128)(2,1)S(1)}, u32[]{:S(2)}, u32[]{:S(2)}) %collective-permute-start.12) | collective-permute-done | bytes 442400 | tf_op jit(solution)/shard_map/ppermute | solution.py:326
  116.7 0.5 collective-permute-start.21
  117.3 3.8 %collective-permute-done.18 = bf16[1,240,384]{2,1,0:T(8,128)(2,1)S(1)} collective-permute-done((bf16[1,240,384]{2,1,0:T(8,128)(2,1)S(1)}, bf16[1,240,384]{2,1,0:T(8,128)(2,1)S(1)}, u32[]{:S(2)}, u32[]{:S(2)}) %collective-permute-start.18) | collective-permute-done | bytes 184352 | tf_op jit(solution)/shard_map/ppermute | solution.py:326
  121.1 3.2 %collective-permute-start.20 = (bf16[2,240,384]{2,1,0:T(8,128)(2,1)S(1)}, bf16[2,240,384]{2,1,0:T(8,128)(2,1)S(1)}, u32[]{:S(2)}, u32[]{:S(2)}) collective-permute-start(bf16[2,240,384]{2,1,0:T(8,128)(2,1)S(1)} %pad_maximum_fusion.4), channel_id=1, source_target_pairs={{0,8},{4,12},{8,0},{12,4},{16,24},{20,28},{24,16},{28,20},{1,9},{5... | collective-permute-start | bytes 1105928 | tf_op jit(solution)/shard_map/ppermute | solution.py:326
  124.5 1.3 collective-permute-done.22
  125.9 0.8 collective-permute-start.25
  126.7 1.4 collective-permute-start.24
  128.0 5.8 %collective-permute-done.20 = bf16[2,240,384]{2,1,0:T(8,128)(2,1)S(1)} collective-permute-done((bf16[2,240,384]{2,1,0:T(8,128)(2,1)S(1)}, bf16[2,240,384]{2,1,0:T(8,128)(2,1)S(1)}, u32[]{:S(2)}, u32[]{:S(2)}) %collective-permute-start.20) | collective-permute-done | bytes 368672 | tf_op jit(solution)/shard_map/ppermute | solution.py:326
  133.9 1.0 collective-permute-start.28
  134.9 3.6 %collective-permute-done.19 = bf16[2,144,384]{2,1,0:T(8,128)(2,1)S(1)} collective-permute-done((bf16[2,144,384]{2,1,0:T(8,128)(2,1)S(1)}, bf16[2,144,384]{2,1,0:T(8,128)(2,1)S(1)}, u32[]{:S(2)}, u32[]{:S(2)}) %collective-permute-start.19) | collective-permute-done | bytes 221216 | tf_op jit(solution)/shard_map/ppermute | solution.py:326
  138.6 2.3 %collective-permute-start.23 = (bf16[1,144,384]{2,1,0:T(8,128)(2,1)S(1)}, bf16[1,144,384]{2,1,0:T(8,128)(2,1)S(1)}, u32[]{:S(2)}, u32[]{:S(2)}) collective-permute-start(bf16[1,144,384]{2,1,0:T(8,128)(2,1)S(1)} %fusion.22), channel_id=1, source_target_pairs={{0,16},{4,20},{8,24},{12,28},{16,0},{20,4},{24,8},{28,12},{1,17},{... | collective-permute-start | bytes 331784 | tf_op jit(solution)/shard_map/ppermute | solution.py:326
  140.9 5.1 %collective-permute-done.25 = bf16[2,192,384]{2,1,0:T(8,128)(2,1)S(1)} collective-permute-done((bf16[2,192,384]{2,1,0:T(8,128)(2,1)S(1)}, bf16[2,192,384]{2,1,0:T(8,128)(2,1)S(1)}, u32[]{:S(2)}, u32[]{:S(2)}) %collective-permute-start.25) | collective-permute-done | bytes 294944 | tf_op jit(solution)/shard_map/ppermute | solution.py:326
  146.6 2.3 %collective-permute-start.26 = (bf16[1,144,384]{2,1,0:T(8,128)(2,1)S(1)}, bf16[1,144,384]{2,1,0:T(8,128)(2,1)S(1)}, u32[]{:S(2)}, u32[]{:S(2)}) collective-permute-start(bf16[1,144,384]{2,1,0:T(8,128)(2,1)S(1)} %fusion.25), channel_id=1, source_target_pairs={{0,16},{4,20},{8,24},{12,28},{16,0},{20,4},{24,8},{28,12},{1,17},{... | collective-permute-start | bytes 331784 | tf_op jit(solution)/shard_map/ppermute | solution.py:326
  149.0 1.4 fusion.1
  150.4 3.8 %collective-permute-done.26 = bf16[1,144,384]{2,1,0:T(8,128)(2,1)S(1)} collective-permute-done((bf16[1,144,384]{2,1,0:T(8,128)(2,1)S(1)}, bf16[1,144,384]{2,1,0:T(8,128)(2,1)S(1)}, u32[]{:S(2)}, u32[]{:S(2)}) %collective-permute-start.26) | collective-permute-done | bytes 110624 | tf_op jit(solution)/shard_map/ppermute | solution.py:326
  154.5 1.5 collective-permute-start.30
  156.0 2.4 %assemble_up.1 = (f32[192,3072]{1,0:T(8,128)}, f32[192,768]{1,0:T(8,128)}) custom-call(s32[4]{0:T(128)S(1)} %pad_add_fusion.refs_0_, bf16[4,240,384]{2,1,0:T(8,128)(2,1)S(1)} %pad_maximum_fusion.refs_1_, bf16[4,240,384]{2,1,0:T(8,128)(2,1)S(1)} %collective-permute-done.28.refs_2_), custom_call_target="tpu_custom_call" | custom-call | flops 11000000 | tf_op jit(solution)/shard_map/assemble_up/pallas_call | solution.py:313
  158.3 1.9 %collective-permute-done.27 = bf16[2,144,384]{2,1,0:T(8,128)(2,1)S(1)} collective-permute-done((bf16[2,144,384]{2,1,0:T(8,128)(2,1)S(1)}, bf16[2,144,384]{2,1,0:T(8,128)(2,1)S(1)}, u32[]{:S(2)}, u32[]{:S(2)}) %collective-permute-start.27) | collective-permute-done | bytes 221216 | tf_op jit(solution)/shard_map/ppermute | solution.py:326
  160.3 2.1 %collective-permute-start.29 = (bf16[4,144,384]{2,1,0:T(8,128)(2,1)S(1)}, bf16[4,144,384]{2,1,0:T(8,128)(2,1)S(1)}, u32[]{:S(2)}, u32[]{:S(2)}) collective-permute-start(bf16[4,144,384]{2,1,0:T(8,128)(2,1)S(1)} %pad_maximum_fusion.3.refs_1_), channel_id=1, source_target_pairs={{0,4},{4,0},{8,12},{12,8},{16,20},{20,16},{24,28},{28,24},{1,5},{5... | collective-permute-start | bytes 1327112 | tf_op jit(solution)/shard_map/ppermute | solution.py:326
  162.4 0.9 collective-permute-start.31
  163.3 4.1 %collective-permute-done.31 = f32[16,768]{1,0:T(8,128)S(1)} collective-permute-done((f32[16,768]{1,0:T(8,128)S(1)}, f32[16,768]{1,0:T(8,128)S(1)}, u32[]{:S(2)}, u32[]{:S(2)}) %collective-permute-start.31) | collective-permute-done | bytes 49184 | tf_op jit(solution)/shard_map/ppermute | solution.py:326
  167.4 0.6 slice.377
  168.0 0.7 slice_reduce_fusion
  168.7 2.1 %collective-permute-done.30.refs_2_ = bf16[4,192,384]{2,1,0:T(8,128)(2,1)S(1)} collective-permute-done((bf16[4,192,384]{2,1,0:T(8,128)(2,1)S(1)}, bf16[4,192,384]{2,1,0:T(8,128)(2,1)S(1)}, u32[]{:S(2)}, u32[]{:S(2)}) %collective-permute-start.30) | collective-permute-done | bytes 589856 | tf_op jit(solution)/shard_map/ppermute | solution.py:326
  170.8 0.7 copy-done.5
  171.4 2.1 %assemble_down.1 = f32[768,768]{1,0:T(8,128)} custom-call(s32[4]{0:T(128)S(1)} %copy-done.5, bf16[4,192,384]{2,1,0:T(8,128)(2,1)S(1)} %pad_maximum_fusion.1.refs_1_, bf16[4,192,384]{2,1,0:T(8,128)(2,1)S(1)} %collective-permute-done.30.refs_2_), custom_call_target="tpu_custom_call" | custom-call | flops 11000000 | tf_op jit(solution)/shard_map/assemble_down/pallas_call | solution.py:313
  173.5 3.2 %collective-permute-done.29.refs_2_ = bf16[4,144,384]{2,1,0:T(8,128)(2,1)S(1)} collective-permute-done((bf16[4,144,384]{2,1,0:T(8,128)(2,1)S(1)}, bf16[4,144,384]{2,1,0:T(8,128)(2,1)S(1)}, u32[]{:S(2)}, u32[]{:S(2)}) %collective-permute-start.29) | collective-permute-done | bytes 442400 | tf_op jit(solution)/shard_map/ppermute | solution.py:326
  176.7 1.9 %assemble_qkv.1 = (f32[192,768]{1,0:T(8,128)}, f32[192,768]{1,0:T(8,128)}, f32[192,768]{1,0:T(8,128)}) custom-call(s32[4]{0:T(128)S(1)} %copy-done.5, bf16[4,144,384]{2,1,0:T(8,128)(2,1)S(1)} %pad_maximum_fusion.3.refs_1_, bf16[4,144,384]{2,1,0:T(8,128)(2,1)S(1)} %collective-permute-done.29.refs_2_), custom_call_target="tpu_custom_call" | custom-call | flops 11000000 | tf_op jit(solution)/shard_map/assemble_qkv/pallas_call | solution.py:313
  (115 shorter events, 8.3 us)
Async XLA Ops:
  0.7 7.9 %copy-start = (bf16[768,768]{1,0:T(8,128)(2,1)S(1)}, bf16[768,768]{1,0:T(8,128)(2,1)}, u32[]{:S(2)}) copy-start(bf16[768,768]{1,0:T(8,128)(2,1)} %param.20) | copy-start | bytes 3538948
  0.7 7.9 %copy-start.2 = (bf16[1,256,768]{2,1,0:T(8,128)(2,1)S(1)}, bf16[1,256,768]{2,1,0:T(8,128)(2,1)}, u32[]{:S(2)}) copy-start(bf16[1,256,768]{2,1,0:T(8,128)(2,1)} %param.19) | copy-start | bytes 1179652
  0.7 14.8 %collective-permute-start = (bf16[256,768]{1,0:T(8,128)(2,1)}, bf16[256,768]{1,0:T(8,128)(2,1)S(1)}, u32[]{:S(2)}, u32[]{:S(2)}) collective-permute-start(bf16[256,768]{1,0:T(8,128)(2,1)} %bitcast.90), channel_id=1, source_target_pairs={{0,1},{1,0},{2,3},{3,2},{4,5},{5,4},{6,7},{7,6},{8,9},{9,8},{10,11... | collective-permute-start | bytes 1179656 | tf_op jit(solution)/shard_map/ppermute | solution.py:326
  1.2 16.0 %collective-permute-start.1 = (bf16[256,768]{1,0:T(8,128)(2,1)}, bf16[256,768]{1,0:T(8,128)(2,1)}, u32[]{:S(2)}, u32[]{:S(2)}) collective-permute-start(bf16[256,768]{1,0:T(8,128)(2,1)} %bitcast.91), channel_id=1, source_target_pairs={{0,2},{1,3},{2,0},{3,1},{4,6},{5,7},{6,4},{7,5},{8,10},{9,11},{10,... | collective-permute-start | bytes 1179656 | tf_op jit(solution)/shard_map/ppermute | solution.py:326
  3.8 39.3 %collective-permute-start.4 = (bf16[256,768]{1,0:T(8,128)(2,1)}, bf16[256,768]{1,0:T(8,128)(2,1)}, u32[]{:S(2)}, u32[]{:S(2)}) collective-permute-start(bf16[256,768]{1,0:T(8,128)(2,1)} %bitcast.102), channel_id=1, source_target_pairs={{0,2},{1,3},{2,0},{3,1},{4,6},{5,7},{6,4},{7,5},{8,10},{9,11},{10,... | collective-permute-start | bytes 1179656 | tf_op jit(solution)/shard_map/ppermute | solution.py:326
  8.6 1.4 copy-start.13
  8.6 1.4 copy-start.14
  8.6 1.4 copy-start.15
  8.6 1.4 copy-start.16
  8.7 1.4 copy-start.17
  8.7 1.5 copy-start.11
  10.2 0.6 copy-start.6
  10.8 4.7 %copy-start.1 = (bf16[768,768]{1,0:T(8,128)(2,1)S(1)}, bf16[768,768]{1,0:T(8,128)(2,1)}, u32[]{:S(2)}) copy-start(bf16[768,768]{1,0:T(8,128)(2,1)} %refs_2_.1) | copy-start | bytes 3538948
  13.7 142.3 %copy-start.4 = (s32[4]{0:T(128)}, s32[4]{0:T(128)S(1)}, u32[]{:S(2)}) copy-start(s32[4]{0:T(128)S(1)} %pad_add_fusion.refs_0_) | copy-start | bytes 52
  15.5 1.3 copy-start.9
  15.5 1.3 copy-start.12
  17.2 3.1 %collective-permute-start.2 = (bf16[256,768]{1,0:T(8,128)(2,1)}, bf16[256,768]{1,0:T(8,128)(2,1)S(1)}, u32[]{:S(2)}, u32[]{:S(2)}) collective-permute-start(bf16[256,768]{1,0:T(8,128)(2,1)} %collective-permute-done.1.refs_0_.refs_7_), channel_id=1, source_target_pairs={{0,1},{1,0},{2,3},{3,2},{4,5},{5,4},{6,7},{7,6},{8,9},{9,8},{10,11... | collective-permute-start | bytes 1179656 | tf_op jit(solution)/shard_map/ppermute | solution.py:326
  20.8 1.0 copy-start.3
  20.9 12.5 %slice-start = ((s8[4718592]{0:T(1024)(128)(4,1)}), s8[4194304]{0:T(1024)(128)(4,1)S(1)}, s32[]{:S(2)}) async-start(s8[4718592]{0:T(1024)(128)(4,1)} %bitcast.98), calls=%async_computation | async-start | bytes 8388608
  20.9 12.4 %slice-start.2 = ((s8[4718592]{0:T(1024)(128)(4,1)}), s8[4194304]{0:T(1024)(128)(4,1)S(1)}, s32[]{:S(2)}) async-start(s8[4718592]{0:T(1024)(128)(4,1)} %bitcast.100), calls=%async_computation.2 | async-start | bytes 8388608
  21.8 11.5 %copy-start.7 = (bf16[9216]{0:T(1024)(128)(2,1)S(1)}, bf16[9216]{0:T(1024)(128)(2,1)}, u32[]{:S(2)}) copy-start(bf16[9216]{0:T(1024)(128)(2,1)} %copy-done.6) | copy-start | bytes 55300
  21.8 11.5 %slice-start.1 = ((s8[4718592]{0:T(1024)(128)(4,1)}), s8[524288]{0:T(1024)(128)(4,1)S(1)}, s32[]{:S(2)}) async-start(s8[4718592]{0:T(1024)(128)(4,1)} %bitcast.98), calls=%async_computation.1 | async-start | bytes 1048576
  21.8 11.5 %slice-start.3 = ((s8[4718592]{0:T(1024)(128)(4,1)}), s8[524288]{0:T(1024)(128)(4,1)S(1)}, s32[]{:S(2)}) async-start(s8[4718592]{0:T(1024)(128)(4,1)} %bitcast.100), calls=%async_computation.3 | async-start | bytes 1048576
  21.8 11.5 %copy-start.8 = (bf16[768,768]{1,0:T(8,128)(2,1)S(1)}, bf16[768,768]{1,0:T(8,128)(2,1)}, u32[]{:S(2)}) copy-start(bf16[768,768]{1,0:T(8,128)(2,1)} %refs_3_.4) | copy-start | bytes 3538948
  21.9 11.5 %copy-start.10 = (bf16[1,256,768]{2,1,0:T(8,128)(2,1)S(1)}, bf16[1,256,768]{2,1,0:T(8,128)(2,1)}, u32[]{:S(2)}) copy-start(bf16[1,256,768]{2,1,0:T(8,128)(2,1)} %param.37) | copy-start | bytes 1179652
  31.4 11.7 %collective-permute-start.3 = (bf16[256,768]{1,0:T(8,128)(2,1)S(1)}, bf16[256,768]{1,0:T(8,128)(2,1)S(1)}, u32[]{:S(2)}, u32[]{:S(2)}) collective-permute-start(bf16[256,768]{1,0:T(8,128)(2,1)S(1)} %get-tuple-element.85.refs_1_.refs_5_), channel_id=1, source_target_pairs={{0,2},{1,3},{2,0},{3,1},{4,6},{5,7},{6,4},{7,5},{8,10},{9,11},{10,... | collective-permute-start | bytes 1179656 | tf_op jit(solution)/shard_map/ppermute | solution.py:326
  54.6 3.3 %collective-permute-start.6 = (bf16[1,2,4,240,384]{4,3,2,1,0:T(8,128)(2,1)S(1)}, bf16[1,2,4,240,384]{4,3,2,1,0:T(8,128)(2,1)S(1)}, u32[]{:S(2)}, u32[]{:S(2)}) collective-permute-start(bf16[1,2,4,240,384]{4,3,2,1,0:T(8,128)(2,1)S(1)} %get-tuple-element.105), channel_id=1, source_target_pairs={{0,1},{1,0},{2,3},{3,2},{4,5},{5,4},{6,7},{7,6},{8,9},{9,8},{10,11... | collective-permute-start | bytes 4423688 | tf_op jit(solution)/shard_map/ppermute | solution.py:326
  57.0 3.0 %collective-permute-start.5 = (bf16[1,2,4,192,384]{4,3,2,1,0:T(8,128)(2,1)S(1)}, bf16[1,2,4,192,384]{4,3,2,1,0:T(8,128)(2,1)S(1)}, u32[]{:S(2)}, u32[]{:S(2)}) collective-permute-start(bf16[1,2,4,192,384]{4,3,2,1,0:T(8,128)(2,1)S(1)} %get-tuple-element.97), channel_id=1, source_target_pairs={{0,1},{1,0},{2,3},{3,2},{4,5},{5,4},{6,7},{7,6},{8,9},{9,8},{10,11... | collective-permute-start | bytes 3538952 | tf_op jit(solution)/shard_map/ppermute | solution.py:326
  58.2 22.3 %collective-permute-start.8 = (bf16[4,240,384]{2,1,0:T(8,128)(2,1)S(1)}, bf16[4,240,384]{2,1,0:T(8,128)(2,1)S(1)}, u32[]{:S(2)}, u32[]{:S(2)}) collective-permute-start(bf16[4,240,384]{2,1,0:T(8,128)(2,1)S(1)} %fusion.8), channel_id=1, source_target_pairs={{0,4},{4,0},{8,12},{12,8},{16,20},{20,16},{24,28},{28,24},{1,5},{5... | collective-permute-start | bytes 2211848 | tf_op jit(solution)/shard_map/ppermute | solution.py:326
  60.2 20.5 %collective-permute-start.7 = (bf16[2,2,192,384]{3,2,1,0:T(8,128)(2,1)S(1)}, bf16[2,2,192,384]{3,2,1,0:T(8,128)(2,1)S(1)}, u32[]{:S(2)}, u32[]{:S(2)}) collective-permute-start(bf16[2,2,192,384]{3,2,1,0:T(8,128)(2,1)S(1)} %add_convert_fusion.2), channel_id=1, source_target_pairs={{0,8},{4,12},{8,0},{12,4},{16,24},{20,28},{24,16},{28,20},{1,9},{5... | collective-permute-start | bytes 1769480 | tf_op jit(solution)/shard_map/ppermute | solution.py:326
  80.3 5.5 %collective-permute-start.11 = (bf16[2,2,4,144,384]{4,3,2,1,0:T(8,128)(2,1)S(1)}, bf16[2,2,4,144,384]{4,3,2,1,0:T(8,128)(2,1)S(1)}, u32[]{:S(2)}, u32[]{:S(2)}) collective-permute-start(bf16[2,2,4,144,384]{4,3,2,1,0:T(8,128)(2,1)S(1)} %get-tuple-element.114), channel_id=1, source_target_pairs={{0,1},{1,0},{2,3},{3,2},{4,5},{5,4},{6,7},{7,6},{8,9},{9,8},{10,11... | collective-permute-start | bytes 5308424 | tf_op jit(solution)/shard_map/ppermute | solution.py:326
  83.4 13.8 %collective-permute-start.9 = (bf16[544,768]{1,0:T(8,128)(2,1)S(1)}, bf16[544,768]{1,0:T(8,128)(2,1)S(1)}, u32[]{:S(2)}, u32[]{:S(2)}) collective-permute-start(bf16[544,768]{1,0:T(8,128)(2,1)S(1)} %get-tuple-element.121), channel_id=1, source_target_pairs={{0,1},{1,0},{2,3},{3,2},{4,5},{5,4},{6,7},{7,6},{8,9},{9,8},{10,11... | collective-permute-start | bytes 2506760 | tf_op jit(solution)/shard_map/ppermute | solution.py:326
  83.9 10.6 %collective-permute-start.10 = (bf16[2,240,384]{2,1,0:T(8,128)(2,1)S(1)}, bf16[2,240,384]{2,1,0:T(8,128)(2,1)S(1)}, u32[]{:S(2)}, u32[]{:S(2)}) collective-permute-start(bf16[2,240,384]{2,1,0:T(8,128)(2,1)S(1)} %fusion.9), channel_id=1, source_target_pairs={{0,8},{4,12},{8,0},{12,4},{16,24},{20,28},{24,16},{28,20},{1,9},{5... | collective-permute-start | bytes 1105928 | tf_op jit(solution)/shard_map/ppermute | solution.py:326
  84.2 14.9 %collective-permute-start.13 = (bf16[2,192,384]{2,1,0:T(8,128)(2,1)S(1)}, bf16[2,192,384]{2,1,0:T(8,128)(2,1)S(1)}, u32[]{:S(2)}, u32[]{:S(2)}) collective-permute-start(bf16[2,192,384]{2,1,0:T(8,128)(2,1)S(1)} %fusion.17), channel_id=1, source_target_pairs={{0,4},{4,0},{8,12},{12,8},{16,20},{20,16},{24,28},{28,24},{1,5},{5... | collective-permute-start | bytes 884744 | tf_op jit(solution)/shard_map/ppermute | solution.py:326
  86.1 22.6 %collective-permute-start.15 = (bf16[1,2,4,144,384]{4,3,2,1,0:T(8,128)(2,1)S(1)}, bf16[1,2,4,144,384]{4,3,2,1,0:T(8,128)(2,1)S(1)}, u32[]{:S(2)}, u32[]{:S(2)}) collective-permute-start(bf16[1,2,4,144,384]{4,3,2,1,0:T(8,128)(2,1)S(1)} %add_convert_fusion), channel_id=1, source_target_pairs={{0,2},{1,3},{2,0},{3,1},{4,6},{5,7},{6,4},{7,5},{8,10},{9,11},{10,... | collective-permute-start | bytes 2654216 | tf_op jit(solution)/shard_map/ppermute | solution.py:326
  94.6 13.8 %collective-permute-start.16 = (bf16[1,240,384]{2,1,0:T(8,128)(2,1)S(1)}, bf16[1,240,384]{2,1,0:T(8,128)(2,1)S(1)}, u32[]{:S(2)}, u32[]{:S(2)}) collective-permute-start(bf16[1,240,384]{2,1,0:T(8,128)(2,1)S(1)} %fusion.16), channel_id=1, source_target_pairs={{0,16},{4,20},{8,24},{12,28},{16,0},{20,4},{24,8},{28,12},{1,17},{... | collective-permute-start | bytes 552968 | tf_op jit(solution)/shard_map/ppermute | solution.py:326
  97.4 19.3 %collective-permute-start.12 = (bf16[288,768]{1,0:T(8,128)(2,1)S(1)}, bf16[288,768]{1,0:T(8,128)(2,1)S(1)}, u32[]{:S(2)}, u32[]{:S(2)}) collective-permute-start(bf16[288,768]{1,0:T(8,128)(2,1)S(1)} %pad_maximum_fusion.2), channel_id=1, source_target_pairs={{0,2},{1,3},{2,0},{3,1},{4,6},{5,7},{6,4},{7,5},{8,10},{9,11},{10,... | collective-permute-start | bytes 1327112 | tf_op jit(solution)/shard_map/ppermute | solution.py:326
  99.1 14.4 %collective-permute-start.14 = (bf16[1,192,384]{2,1,0:T(8,128)(2,1)S(1)}, bf16[1,192,384]{2,1,0:T(8,128)(2,1)S(1)}, u32[]{:S(2)}, u32[]{:S(2)}) collective-permute-start(bf16[1,192,384]{2,1,0:T(8,128)(2,1)S(1)} %fusion.18), channel_id=1, source_target_pairs={{0,16},{4,20},{8,24},{12,28},{16,0},{20,4},{24,8},{28,12},{1,17},{... | collective-permute-start | bytes 442376 | tf_op jit(solution)/shard_map/ppermute | solution.py:326
  108.6 12.5 %collective-permute-start.18 = (bf16[1,240,384]{2,1,0:T(8,128)(2,1)S(1)}, bf16[1,240,384]{2,1,0:T(8,128)(2,1)S(1)}, u32[]{:S(2)}, u32[]{:S(2)}) collective-permute-start(bf16[1,240,384]{2,1,0:T(8,128)(2,1)S(1)} %fusion.14), channel_id=1, source_target_pairs={{0,16},{4,20},{8,24},{12,28},{16,0},{20,4},{24,8},{28,12},{1,17},{... | collective-permute-start | bytes 552968 | tf_op jit(solution)/shard_map/ppermute | solution.py:326
  108.9 15.4 %collective-permute-start.17 = (bf16[4,144,384]{2,1,0:T(8,128)(2,1)S(1)}, bf16[4,144,384]{2,1,0:T(8,128)(2,1)S(1)}, u32[]{:S(2)}, u32[]{:S(2)}) collective-permute-start(bf16[4,144,384]{2,1,0:T(8,128)(2,1)S(1)} %fusion.10), channel_id=1, source_target_pairs={{0,4},{4,0},{8,12},{12,8},{16,20},{20,16},{24,28},{28,24},{1,5},{5... | collective-permute-start | bytes 1327112 | tf_op jit(solution)/shard_map/ppermute | solution.py:326
  113.7 12.1 %collective-permute-start.22 = (bf16[1,192,384]{2,1,0:T(8,128)(2,1)S(1)}, bf16[1,192,384]{2,1,0:T(8,128)(2,1)S(1)}, u32[]{:S(2)}, u32[]{:S(2)}) collective-permute-start(bf16[1,192,384]{2,1,0:T(8,128)(2,1)S(1)} %fusion.20), channel_id=1, source_target_pairs={{0,16},{4,20},{8,24},{12,28},{16,0},{20,4},{24,8},{28,12},{1,17},{... | collective-permute-start | bytes 442376 | tf_op jit(solution)/shard_map/ppermute | solution.py:326
  116.7 9.9 %collective-permute-start.21 = (f32[16,768]{1,0:T(8,128)S(1)}, f32[16,768]{1,0:T(8,128)S(1)}, u32[]{:S(2)}, u32[]{:S(2)}) collective-permute-start(f32[16,768]{1,0:T(8,128)S(1)} %fusion.31), channel_id=1, source_target_pairs={{0,4},{4,0},{8,12},{12,8},{16,20},{20,16},{24,28},{28,24},{1,5},{5... | collective-permute-start | bytes 147464 | tf_op jit(solution)/shard_map/ppermute | solution.py:326
  121.1 12.7 %collective-permute-start.20 = (bf16[2,240,384]{2,1,0:T(8,128)(2,1)S(1)}, bf16[2,240,384]{2,1,0:T(8,128)(2,1)S(1)}, u32[]{:S(2)}, u32[]{:S(2)}) collective-permute-start(bf16[2,240,384]{2,1,0:T(8,128)(2,1)S(1)} %pad_maximum_fusion.4), channel_id=1, source_target_pairs={{0,8},{4,12},{8,0},{12,4},{16,24},{20,28},{24,16},{28,20},{1,9},{5... | collective-permute-start | bytes 1105928 | tf_op jit(solution)/shard_map/ppermute | solution.py:326
  124.4 14.1 %collective-permute-start.19 = (bf16[2,144,384]{2,1,0:T(8,128)(2,1)S(1)}, bf16[2,144,384]{2,1,0:T(8,128)(2,1)S(1)}, u32[]{:S(2)}, u32[]{:S(2)}) collective-permute-start(bf16[2,144,384]{2,1,0:T(8,128)(2,1)S(1)} %fusion.11), channel_id=1, source_target_pairs={{0,8},{4,12},{8,0},{12,4},{16,24},{20,28},{24,16},{28,20},{1,9},{5... | collective-permute-start | bytes 663560 | tf_op jit(solution)/shard_map/ppermute | solution.py:326
  125.9 20.1 %collective-permute-start.25 = (bf16[2,192,384]{2,1,0:T(8,128)(2,1)S(1)}, bf16[2,192,384]{2,1,0:T(8,128)(2,1)S(1)}, u32[]{:S(2)}, u32[]{:S(2)}) collective-permute-start(bf16[2,192,384]{2,1,0:T(8,128)(2,1)S(1)} %pad_maximum_fusion.5), channel_id=1, source_target_pairs={{0,8},{4,12},{8,0},{12,4},{16,24},{20,28},{24,16},{28,20},{1,9},{5... | collective-permute-start | bytes 884744 | tf_op jit(solution)/shard_map/ppermute | solution.py:326
  126.7 19.9 %collective-permute-start.24 = (f32[16,768]{1,0:T(8,128)S(1)}, f32[16,768]{1,0:T(8,128)S(1)}, u32[]{:S(2)}, u32[]{:S(2)}) collective-permute-start(f32[16,768]{1,0:T(8,128)S(1)} %add.569), channel_id=1, source_target_pairs={{0,8},{4,12},{8,0},{12,4},{16,24},{20,28},{24,16},{28,20},{1,9},{5... | collective-permute-start | bytes 147464 | tf_op jit(solution)/shard_map/ppermute | solution.py:326
  133.9 22.1 %collective-permute-start.28 = (bf16[4,240,384]{2,1,0:T(8,128)(2,1)S(1)}, bf16[4,240,384]{2,1,0:T(8,128)(2,1)S(1)}, u32[]{:S(2)}, u32[]{:S(2)}) collective-permute-start(bf16[4,240,384]{2,1,0:T(8,128)(2,1)S(1)} %pad_maximum_fusion.refs_1_), channel_id=1, source_target_pairs={{0,4},{4,0},{8,12},{12,8},{16,20},{20,16},{24,28},{28,24},{1,5},{5... | collective-permute-start | bytes 2211848 | tf_op jit(solution)/shard_map/ppermute | solution.py:326
  138.6 7.9 %collective-permute-start.23 = (bf16[1,144,384]{2,1,0:T(8,128)(2,1)S(1)}, bf16[1,144,384]{2,1,0:T(8,128)(2,1)S(1)}, u32[]{:S(2)}, u32[]{:S(2)}) collective-permute-start(bf16[1,144,384]{2,1,0:T(8,128)(2,1)S(1)} %fusion.22), channel_id=1, source_target_pairs={{0,16},{4,20},{8,24},{12,28},{16,0},{20,4},{24,8},{28,12},{1,17},{... | collective-permute-start | bytes 331784 | tf_op jit(solution)/shard_map/ppermute | solution.py:326
  146.6 7.6 %collective-permute-start.26 = (bf16[1,144,384]{2,1,0:T(8,128)(2,1)S(1)}, bf16[1,144,384]{2,1,0:T(8,128)(2,1)S(1)}, u32[]{:S(2)}, u32[]{:S(2)}) collective-permute-start(bf16[1,144,384]{2,1,0:T(8,128)(2,1)S(1)} %fusion.25), channel_id=1, source_target_pairs={{0,16},{4,20},{8,24},{12,28},{16,0},{20,4},{24,8},{28,12},{1,17},{... | collective-permute-start | bytes 331784 | tf_op jit(solution)/shard_map/ppermute | solution.py:326
  154.2 6.0 %collective-permute-start.27 = (bf16[2,144,384]{2,1,0:T(8,128)(2,1)S(1)}, bf16[2,144,384]{2,1,0:T(8,128)(2,1)S(1)}, u32[]{:S(2)}, u32[]{:S(2)}) collective-permute-start(bf16[2,144,384]{2,1,0:T(8,128)(2,1)S(1)} %pad_maximum_fusion.6), channel_id=1, source_target_pairs={{0,8},{4,12},{8,0},{12,4},{16,24},{20,28},{24,16},{28,20},{1,9},{5... | collective-permute-start | bytes 663560 | tf_op jit(solution)/shard_map/ppermute | solution.py:326
  154.5 16.3 %collective-permute-start.30 = (bf16[4,192,384]{2,1,0:T(8,128)(2,1)S(1)}, bf16[4,192,384]{2,1,0:T(8,128)(2,1)S(1)}, u32[]{:S(2)}, u32[]{:S(2)}) collective-permute-start(bf16[4,192,384]{2,1,0:T(8,128)(2,1)S(1)} %pad_maximum_fusion.1.refs_1_), channel_id=1, source_target_pairs={{0,4},{4,0},{8,12},{12,8},{16,20},{20,16},{24,28},{28,24},{1,5},{5... | collective-permute-start | bytes 1769480 | tf_op jit(solution)/shard_map/ppermute | solution.py:326
  160.3 16.4 %collective-permute-start.29 = (bf16[4,144,384]{2,1,0:T(8,128)(2,1)S(1)}, bf16[4,144,384]{2,1,0:T(8,128)(2,1)S(1)}, u32[]{:S(2)}, u32[]{:S(2)}) collective-permute-start(bf16[4,144,384]{2,1,0:T(8,128)(2,1)S(1)} %pad_maximum_fusion.3.refs_1_), channel_id=1, source_target_pairs={{0,4},{4,0},{8,12},{12,8},{16,20},{20,16},{24,28},{28,24},{1,5},{5... | collective-permute-start | bytes 1327112 | tf_op jit(solution)/shard_map/ppermute | solution.py:326
  162.4 5.0 %collective-permute-start.31 = (f32[16,768]{1,0:T(8,128)S(1)}, f32[16,768]{1,0:T(8,128)S(1)}, u32[]{:S(2)}, u32[]{:S(2)}) collective-permute-start(f32[16,768]{1,0:T(8,128)S(1)} %add.576), channel_id=1, source_target_pairs={{0,16},{4,20},{8,24},{12,28},{16,0},{20,4},{24,8},{28,12},{1,17},{... | collective-permute-start | bytes 147464 | tf_op jit(solution)/shard_map/ppermute | solution.py:326
  170.8 0.7 copy-start.5
where the time goes:
time: 179 us
  Pallas kernels  59.6 us (33%)
  waiting for transfers between devices  58.3 us (33%)
  starting transfers between devices  36.3 us (20%)
  matrix products  11.1 us (6%)
  local copies, waits for them, and re-layouts  6.78 us (4%)
  other arithmetic  4.51 us (3%)
  between operations  1.9 us (1%)
    ppermute x32, waiting for transfers between devices, swap(): return lax.ppermute(value, axis, [(i, i ^ mask) for i in range(size)])  58.3 us
    ppermute x32, starting transfers between devices, swap(): return lax.ppermute(value, axis, [(i, i ^ mask) for i in range(size)])  36.3 us
    pallas_call x2, Pallas kernels, after_attention(): pl.pallas_call(lambda *refs: layer_kernel(*refs, own=own), in_specs=[VMEM...  17.9 us
    pallas_call x1, Pallas kernels, attn_bwd(): pl.pallas_call(lambda *refs: attn_bwd_kernel(*refs, parts=len(keys)), gri...  13.8 us
    dot_general x10, matrix products, dot(): return lax.dot_general(left, right, dims, preferred_element_type=F32)  11.1 us
    pallas_call x1, Pallas kernels, attn_fwd(): pl.pallas_call(lambda *refs: attn_fwd_kernel(*refs, parts=len(keys)), gri...  9.49 us
    pallas_call x3, Pallas kernels, assemble(): pl.pallas_call(lambda *refs: assemble_kernel(*refs, plan=plan), in_specs=...  6.31 us
    pallas_call x2, Pallas kernels, half_share_grads(): pl.pallas_call(lambda *refs: half_share_kernel(*refs, plan=plan, low=low)...  4.97 us
  transfers between devices with their start and end apart: 32, of which 19 were waited for; matrix products, arithmetic and copies ran while one was open for 11% of the time, Pallas kernels for 26%

commit v1 on v0

--- a/solution.py
+++ b/solution.py
@@ -28,32 +28,76 @@
 TN = (((0,), (0,)), ((), ()))
 
 
+VMEM_SPEC = pl.BlockSpec(memory_space=pltpu.VMEM)
+SMEM_SPEC = pl.BlockSpec(memory_space=pltpu.SMEM)
+
+
 def dot(left, right, dims=NN):
     return lax.dot_general(left, right, dims, preferred_element_type=F32)
 
 
-def seq_coords(blocks, is_long):
-    device = blocks // PER_DEV
-    within = blocks % PER_DEV
-    slot_id = jnp.where(is_long, 0, within // PER_SLOT)
-    position = jnp.where(is_long, blocks, device * PER_SLOT + within % PER_SLOT)
-    return (slot_id, position)
-
-
-def block_bias(device, chosen, is_long, n_seq):
-    total_blocks = PER_DEV * n_seq
-    last_pos = jnp.where(is_long, total_blocks, total_blocks // SLOTS) - 1
-    own_slot, own_pos = seq_coords(device * PER_DEV + jnp.arange(PER_DEV), is_long)
-    columns = jnp.arange(total_blocks)
-    key_ids = (device ^ (columns // PER_DEV)) * PER_DEV + columns % PER_DEV
-    key_slot, key_pos = seq_coords(key_ids, is_long)
-    same = own_slot[:, None] == key_slot[None, :]
-    ends = (key_pos == 0) | (key_pos == last_pos)
-    near = jnp.abs(own_pos[:, None] - key_pos[None, :]) <= 1
-    drawn = jnp.any(chosen[:, :, None] == key_pos[None, None, :], axis=1)
-    is_global = (own_pos == 0) | (own_pos == last_pos)
-    keep = same & (is_global[:, None] | ends[None, :] | near | drawn)
-    return jnp.where(keep, 0.0, MASKED).astype(F32)
+def coords(device, within, is_long):
+    slot = jnp.where(is_long, 0, within // PER_SLOT)
+    position = jnp.where(
+        is_long, device * PER_DEV + within, device * PER_SLOT + within % PER_SLOT
+    )
+    return slot, position
+
+
+def bias_kernel(place_ref, long_ref, chosen_ref, bias_ref, *, n_seq):
+    device = place_ref[0] * (n_seq // 2) + place_ref[1]
+    is_long = long_ref[0] == 1
+    last = jnp.where(is_long, n_seq * PER_DEV, n_seq * PER_DEV // SLOTS) - 1
+    column = lax.broadcasted_iota(jnp.int32, (1, n_seq * T_DEV), 1)
+    key_slot, key_pos = coords(
+        (column // T_DEV) ^ device, column % T_DEV // BLOCK, is_long
+    )
+    ends = (key_pos == 0) | (key_pos == last)
+    for block in range(PER_DEV):
+        slot, position = coords(device, block, is_long)
+        keep = ends | (jnp.abs(key_pos - position) <= 1)
+        for draw in range(RAND):
+            keep = keep | (key_pos == chosen_ref[0, block, draw])
+        keep = keep | (position == 0) | (position == last)
+        keep = keep & (key_slot == slot)
+        bias_ref[block : block + 1, :] = jnp.where(keep, 0.0, MASKED)
+
+
+def block_bias(place, long_group, random_blocks, n_seq):
+    return pl.pallas_call(
+        lambda *refs: bias_kernel(*refs, n_seq=n_seq),
+        in_specs=[SMEM_SPEC] * 3,
+        out_specs=VMEM_SPEC,
+        out_shape=jax.ShapeDtypeStruct((PER_DEV, n_seq * T_DEV), F32),
+        compiler_params=pltpu.CompilerParams(vmem_limit_bytes=4 * MIB),
+        cost_estimate=cost(1),
+        name="block_bias",
+    )(place, long_group, random_blocks)
+
+
+def project_kernel(wk_ref, wv_ref, v_bias_ref, *refs, count, with_query):
+    parts, refs = refs[:count], refs[count:]
+    if with_query:
+        wq_ref, q_bias_ref, q_ref, *refs = refs
+        query = dot(parts[0][...], wq_ref[...]) + q_bias_ref[...].astype(F32)[None, :]
+        q_ref[...] = (query * 0.125).astype(BF16)
+    v_bias = v_bias_ref[...].astype(F32)[None, :]
+    for index, part in enumerate(parts):
+        refs[2 * index][...] = dot(part[...], wk_ref[...]).astype(BF16)
+        refs[2 * index + 1][...] = (dot(part[...], wv_ref[...]) + v_bias).astype(BF16)
+
+
+def project(parts, w_key, w_value, value_bias, *query):
+    count = 2 * len(parts) + (1 if query else 0)
+    return pl.pallas_call(
+        lambda *refs: project_kernel(*refs, count=len(parts), with_query=bool(query)),
+        in_specs=[VMEM_SPEC] * (3 + len(parts) + len(query)),
+        out_specs=[VMEM_SPEC] * count,
+        out_shape=[jax.ShapeDtypeStruct((T_DEV, D), BF16)] * count,
+        compiler_params=pltpu.CompilerParams(vmem_limit_bytes=16 * MIB),
+        cost_estimate=cost(1),
+        name="project_near" if query else "project_far",
+    )(w_key, w_value, value_bias, *parts, *query)
 
 
 def joined(refs):
@@ -73,7 +117,7 @@
         peak = jnp.max(scores, axis=1, keepdims=True)
         weight = jnp.exp(scores - peak)
         total = jnp.sum(weight, axis=1, keepdims=True)
-        outs.append(dot((weight * (1.0 / total)).astype(BF16), value))
+        outs.append(dot(weight.astype(BF16), value) * (1.0 / total))
         lses.append(peak + jnp.log(total))
     mixed_ref[...] = jnp.where(first, outs[0], outs[1]).astype(BF16)
     lse_ref[...] = jnp.where(first, lses[0], lses[1])
@@ -215,10 +259,6 @@
     send_ref[...] = stage[low // 2 : low]
 
 
-VMEM_SPEC = pl.BlockSpec(memory_space=pltpu.VMEM)
-SMEM_SPEC = pl.BlockSpec(memory_space=pltpu.SMEM)
-
-
 def half_share_grads(place, weights, n_seq, name):
     low = n_seq // 2
     plan = [(w[0].shape[1], w[1].shape[1]) for w in weights]
@@ -333,6 +373,9 @@
     return total.astype(BF16)
 
 
+STEPS = "TUCDUCDCUCDTUCDCTUTDTC"
+
+
 class Order:
     def __init__(self):
         self.last = ()
@@ -353,10 +396,11 @@
     got = exchange(order, [send], [("seq", seq_masks[0])])
     yield
     terms = [keep, *order.after(*got)]
-    for mask in seq_masks[1:]:
+    for step, mask in enumerate(seq_masks[1:]):
         half = terms[0].shape[0] // 2
         got = exchange(order, [summed([t[half:] for t in terms])], [("seq", mask)])
-        yield
+        if step == 0:
+            yield
         terms = [t[:half] for t in terms] + list(order.after(*got))
     return [t[0] for t in terms]
 
@@ -365,21 +409,21 @@
     step = 2 * QUARTERS
     while step < lax.axis_size("dp"):
         got = exchange(order, [piece], [("dp", step)])
-        yield
         piece = summed([piece, *order.after(*got)])
         step *= 2
     return piece
 
 
-def gather_dp(order, own):
-    for mask in (4, 2):
-        got = exchange(order, [own], [("dp", mask)])
-        yield
-        own = jnp.concatenate([own, *order.after(*got)])
-    got = exchange(order, [own], [("dp", 1)])
-    yield
-    (other,) = order.after(*got)
-    return [own, other]
+def gather_dp(order, piece):
+    got = exchange(order, [piece], [("dp", 4)])
+    yield
+    first = jnp.concatenate([piece, *order.after(*got)])
+    got = exchange(order, [first, first], [("dp", 2), ("dp", 1)])
+    yield
+    second, far_first = order.after(*got)
+    got = exchange(order, [second], [("dp", 1)])
+    yield
+    return [first, second, far_first, *order.after(*got)]
 
 
 def columns_first(order, keep, send, seq_masks):
@@ -392,7 +436,46 @@
         got = exchange(order, [summed([t[half:] for t in terms])], [("dp", mask)])
         yield
         terms = [t[:half] for t in terms] + list(order.after(*got))
-    piece = yield from sum_dp_rest(order, summed(terms))
+    piece = sum_dp_rest(order, summed(terms))
+    return (yield from gather_dp(order, piece))
+
+
+def both_first(order, keep, send, seq_masks):
+    got = exchange(order, [send], [("seq", seq_masks[0])])
+    yield
+    terms = [keep, *order.after(*got)]
+    for mask in seq_masks[1:-1]:
+        count = terms[0].shape[0] // 2
+        got = exchange(order, [summed([t[count:] for t in terms])], [("seq", mask)])
+        terms = [t[:count] for t in terms] + list(order.after(*got))
+    along_seq, along_dp = ("seq", seq_masks[-1]), ("dp", 1)
+    half = QUARTERS // 2
+    low, high = [t[:, :, :half] for t in terms], [t[:, :, half:] for t in terms]
+    got = exchange(
+        order,
+        [summed([t[1] for t in low]), summed([t[:, 1] for t in high])],
+        [along_seq, along_dp],
+    )
+    yield
+    low_got, high_got = order.after(*got)
+    low = [t[0] for t in low] + [low_got]
+    high = [t[:, 0] for t in high] + [high_got]
+    got = exchange(
+        order,
+        [summed([t[1] for t in low]), summed([t[1] for t in high])],
+        [along_dp, along_seq],
+    )
+    yield
+    low_got, high_got = order.after(*got)
+    low = [t[0] for t in low] + [low_got]
+    high = [t[0] for t in high] + [high_got]
+    got = exchange(order, [summed(high)], [("dp", 2)])
+    yield
+    terms = low + list(order.after(*got))
+    got = exchange(order, [summed([t[1:] for t in terms])], [("dp", 4)])
+    yield
+    terms = [t[:1] for t in terms] + list(order.after(*got))
+    piece = sum_dp_rest(order, summed(terms))
     return (yield from gather_dp(order, piece))
 
 
@@ -408,7 +491,7 @@
     got = exchange(order, [summed([t[1:] for t in terms])], [("dp", 4)])
     yield
     piece = summed([t[:1] for t in terms] + list(order.after(*got)))
-    piece = yield from sum_dp_rest(order, piece)
+    piece = sum_dp_rest(order, piece)
     return (yield from gather_dp(order, piece))
 
 
@@ -452,7 +535,8 @@
             send = jnp.concatenate([summed([t[half:] for t in terms]), high, rest])
             terms = [t[:half] for t in terms]
         got = exchange(order, [send], [("seq", mask)])
-        yield
+        if step < 2:
+            yield
         (got,) = order.after(*got)
         at = terms[0].shape[0]
         small = high.astype(F32) + rest.astype(F32)
@@ -462,7 +546,8 @@
     step = 1
     while step < n_dp:
         got = exchange(order, [small], [("dp", step)])
-        yield
+        if step < 2 * QUARTERS:
+            yield
         small = small + order.after(*got)[0]
         step *= 2
     return total, small
@@ -608,28 +693,32 @@
     n_seq, n_dp = lax.axis_size("seq"), lax.axis_size("dp")
     device, dp = lax.axis_index("seq"), lax.axis_index("dp")
     low = n_seq // 2
-    place = jnp.stack([device // low, device % low, dp % 2, dp // 2 % QUARTERS]).astype(jnp.int32)
+    low_bits = low.bit_length() - 1
+    place = jnp.stack(
+        [device >> low_bits, device & (low - 1), dp & 1, (dp >> 1) & (QUARTERS - 1)]
+    ).astype(jnp.int32)
     tok_rows = inputs.reshape(T_DEV, D)
     cotangent = out_grad.reshape(T_DEV, D)
-    parts = [tok_rows] + [None] * (n_seq - 1)
+    bias = block_bias(place, long_group, random_blocks, n_seq)
+    parts = [tok_rows, swap(tok_rows, "seq", 1)] + [None] * (n_seq - 2)
     step = low
     while step > 1:
         for j in range(0, n_seq, 2 * step):
             parts[j + step] = swap(parts[j], "seq", step)
         step //= 2
-    for j in range(0, n_seq, 2):
+    query, *near = project(parts[:2], w_key, w_value, value_bias, w_query, query_bias)
+    *parts[2::2], bias, query = lax.optimization_barrier((*parts[2::2], bias, query))
+    for j in range(2, n_seq, 2):
         parts[j + 1] = swap(parts[j], "seq", 1)
     cotangent_partner = swap(cotangent, "seq", low)
-    bias = block_bias(device, random_blocks[0], long_group[0] == 1, n_seq)
-    bias = jnp.repeat(bias, BLOCK, axis=1)
     vectors = (proj_bias, ln1_gain, ln1_bias, down_bias, ln2_gain, ln2_bias)
     packed = jnp.concatenate([jnp.pad(vector, (0, PACK - D)) for vector in vectors] + [up_bias])
     bias, packed = lax.optimization_barrier((bias, packed))
     weights = (w_proj, w_up, w_down, packed)
 
-    query = ((dot(tok_rows, w_query) + query_bias) * 0.125).astype(BF16)
-    keys = [dot(part, w_key).astype(BF16) for part in parts]
-    values = [(dot(part, w_value) + value_bias).astype(BF16) for part in parts]
+    far = [project([part], w_key, w_value, value_bias) for part in parts[2:]]
+    keys = [near[0], near[2]] + [pair[0] for pair in far]
+    values = [near[1], near[3]] + [pair[1] for pair in far]
     mixed, lse = attn_fwd(query, bias, keys, values)
     mixed_partner = swap(mixed, "seq", low)
     own = after_attention(tok_rows, mixed, cotangent, weights, True)
@@ -657,7 +746,7 @@
     next(down)
     up = columns_first(order, *up_terms, low_masks)
     next(up)
-    for _ in low_masks:
+    for _ in low_masks[:2]:
         next(up)
         ups = order.last
         next(down)
@@ -665,51 +754,34 @@
     (d_mixed,) = order.after(own["d_mixed"])
     d_query, d_key, d_value = attn_bwd(query, bias, keys, values, d_mixed, lse)
     *qkv_terms, small = full_share_grads(place, parts, d_query, d_key, d_value, own["sums"])
-    qkv = columns_first(order, *qkv_terms, seq_masks)
+    qkv = both_first(order, *qkv_terms, seq_masks)
     next(qkv)
     next(up)
     next(down)
     d_key, d_value = order.after(d_key, d_value)
     token_parts = token_terms(d_key, d_value, w_key, w_value, small, n_seq)
-    input_grad = own["d_resid1"] + 0.125 * dot(d_query, w_query, NT)
     tail = token_chain(order, *token_parts, small, seq_masks)
     next(tail)
-    rest = n_dp.bit_length() - 4
-
-    def advance(chain, more=0):
-        for _ in range(1 + more):
-            next(chain)
+    next(qkv)
 
     square = (D // n_seq, D)
-    for _ in seq_masks[1:]:
-        advance(qkv)
-    advance(up)
-    for _ in seq_masks[1:]:
-        advance(tail)
-    advance(down)
-    advance(up, rest)
-    advance(qkv)
-    advance(down, rest)
-    advance(tail)
-    advance(up)
-    advance(qkv)
-    advance(down)
-    advance(tail)
-    advance(up)
-    advance(qkv)
-    advance(down)
-    advance(tail, rest)
-    advance(qkv, rest)
-    total, small = finish(tail)
-    input_grad = input_grad + total
-    order.mark(input_grad)
+    chains = dict(D=down, U=up, C=qkv, T=tail)
+    plans = dict(D=[(FF // n_seq, D)], U=[(D // n_seq, FF), square], C=[square] * 3)
+    results = {}
+    for name in STEPS:
+        try:
+            next(chains[name])
+        except StopIteration as stop:
+            if name == "T":
+                total, small = stop.value
+                results[name] = [own["d_resid1"] + 0.125 * dot(d_query, w_query, NT) + total]
+            else:
+                results[name] = assemble(place, stop.value, plans[name], "assemble_" + name)
+            order.mark(*order.last, results[name][0])
+    (grad_down,), (grad_up, grad_proj) = results["D"], results["U"]
+    grad_query, grad_key, grad_value = results["C"]
+    (input_grad,) = results["T"]
     small = small.reshape(-1)
-    advance(qkv)
-    grad_up, grad_proj = assemble(place, finish(up), [(D // n_seq, FF), square], "assemble_up")
-    order.mark(grad_up)
-    advance(qkv)
-    (grad_down,) = assemble(place, finish(down), [(FF // n_seq, D)], "assemble_down")
-    grad_query, grad_key, grad_value = assemble(place, finish(qkv), [square] * 3, "assemble_qkv")
     up_end = 5 * D + FF
     return (
         own["layer_out"].reshape(1, T_DEV, D),

time: 179 us -> 163 us (0.911)
  matrix products: 11.1 us -> 1.43 us
  waiting for transfers between devices: 58.3 us -> 54 us
  other arithmetic: 4.51 us -> 2.08 us
  starting transfers between devices: 36.3 us -> 38.7 us
  local copies, waits for them, and re-layouts: 6.78 us -> 4.81 us
    dot_general x10 -> x1, matrix products: 11.1 us -> 1.43 us  [dot(): return lax.dot_general(left, right, dims, preferred_element_type=F32)]
    ppermute x32 -> x37, waiting for transfers between devices: 58.3 us -> 54 us  [swap(): return lax.ppermute(value, axis, [(i, i ^ mask) for i in range(size)])]
    pallas_call x0 -> x4, Pallas kernels: none -> 3.98 us  [the longest x3 3.26 us: project(): pl.pallas_call(lambda *refs: project_kernel(*refs, count=len(parts), with...]
    ppermute x32 -> x37, starting transfers between devices: 36.3 us -> 38.7 us  [swap(): return lax.ppermute(value, axis, [(i, i ^ mask) for i in range(size)])]
    convert_element_type x2 -> x0, other arithmetic: 1.96 us -> none  [the longest x1 1.27 us: on_device(): values = [(dot(part, w_value) + value_bias).astype(BF16) for part in parts]]
  transfers between devices with their start and end apart: 32 -> 37, of which waited for: 19 -> 19; matrix products, arithmetic and copies ran while one was open for 11% -> 4% of each run, Pallas kernels for 26% -> 30%
where the time goes in v1:
time: 163 us
  Pallas kernels  60.5 us (37%)
  waiting for transfers between devices  54 us (33%)
  starting transfers between devices  38.7 us (24%)
  local copies, waits for them, and re-layouts  4.81 us (3%)
  other arithmetic  2.08 us (1%)
  between operations  1.76 us (1%)
    ppermute x37, waiting for transfers between devices, swap(): return lax.ppermute(value, axis, [(i, i ^ mask) for i in range(size)])  54 us
    ppermute x37, starting transfers between devices, swap(): return lax.ppermute(value, axis, [(i, i ^ mask) for i in range(size)])  38.7 us
    pallas_call x2, Pallas kernels, after_attention(): pl.pallas_call(lambda *refs: layer_kernel(*refs, own=own), in_specs=[VMEM...  16.8 us
    pallas_call x1, Pallas kernels, attn_bwd(): pl.pallas_call(lambda *refs: attn_bwd_kernel(*refs, parts=len(keys)), gri...  13.8 us
    pallas_call x1, Pallas kernels, attn_fwd(): pl.pallas_call(lambda *refs: attn_fwd_kernel(*refs, parts=len(keys)), gri...  7.95 us
    pallas_call x3, Pallas kernels, assemble(): pl.pallas_call(lambda *refs: assemble_kernel(*refs, plan=plan), in_specs=...  6.31 us
    pallas_call x2, Pallas kernels, half_share_grads(): pl.pallas_call(lambda *refs: half_share_kernel(*refs, plan=plan, low=low)...  4.97 us
    pallas_call x1, Pallas kernels, full_share_grads(): pl.pallas_call(lambda *refs: full_share_kernel(*refs, n_seq=n_seq), in_sp...  4.04 us
  transfers between devices with their start and end apart: 37, of which 19 were waited for; matrix products, arithmetic and copies ran while one was open for 4% of the time, Pallas kernels for 30%

profile of v1, /device:TPU:0, one launch (start us, length us, event | category | flops | bytes accessed | tf_op | source)
XLA Modules:
  0.0 163.2 jit_solution(15605493557875166551)
XLA Ops:
  0.7 3.0 %collective-permute-start = (bf16[256,768]{1,0:T(8,128)(2,1)}, bf16[256,768]{1,0:T(8,128)(2,1)S(1)}, u32[]{:S(2)}, u32[]{:S(2)}) collective-permute-start(bf16[256,768]{1,0:T(8,128)(2,1)} %bitcast.73), channel_id=1, source_target_pairs={{0,2},{1,3},{2,0},{3,1},{4,6},{5,7},{6,4},{7,5},{8,10},{9,11},{10,... | collective-permute-start | bytes 1179656 | tf_op jit(solution)/shard_map/ppermute | solution.py:366
  4.5 0.8 copy.36.refs_2_
  5.3 0.7 constant_dynamic-update-slice_fusion.6
  6.0 0.7 constant_dynamic-update-slice_fusion.5
  6.8 0.7 block_bias.1.refs_1_
  7.6 0.4 copy-done
  8.9 1.7 %project_near.1 = (bf16[256,768]{1,0:T(8,128)(2,1)S(1)}, bf16[256,768]{1,0:T(8,128)(2,1)S(1)}, bf16[256,768]{1,0:T(8,128)(2,1)S(1)}, bf16[256,768]{1,0:T(8,128)(2,1)S(1)}, bf16[256,768]{1,0:T(8,128)(2,1)S(1)}) custom-call(bf16[768,768]{1,0:T(8,128)(2,1)S(1)} %copy-done.2, bf16[768,768]{1,0:T(8,128)(2,1)S(1)} %copy-done.3, bf16[768]{0:T(1024)(128)(2,1)S(1)} %copy-done.5, ...), custom_call_target="tpu_custom_call" | custom-call | flops 1100000000 | tf_op jit(solution)/shard_map/project_near/pallas_call | solution.py:92
  10.6 3.3 %collective-permute-done.refs_3_.refs_0_.refs_7_ = bf16[256,768]{1,0:T(8,128)(2,1)S(1)} collective-permute-done((bf16[256,768]{1,0:T(8,128)(2,1)}, bf16[256,768]{1,0:T(8,128)(2,1)S(1)}, u32[]{:S(2)}, u32[]{:S(2)}) %collective-permute-start) | collective-permute-done | bytes 393248 | tf_op jit(solution)/shard_map/ppermute | solution.py:366
  13.9 0.8 project_far.2
  14.7 0.9 collective-permute-done.2.refs_3_.refs_8_
  15.6 0.8 project_far.3
  16.4 8.0 %attn_fwd.1 = (bf16[256,768]{1,0:T(8,128)(2,1)S(1)}, f32[256,768]{1,0:T(8,128)S(1)}) custom-call(bf16[256,768]{1,0:T(8,128)(2,1)S(1)} %get-tuple-element.102.refs_0_, f32[4,1024]{1,0:T(4,128)S(1)} %block_bias.1.refs_1_, bf16[256,768]{1,0:T(8,128)(2,1)S(1)} %get-tuple-element.105.refs_2_.refs_4_, bf16[256,768]{1,0:T(8,128)(2,1)S(1)} %get-tuple-element.106.refs_3_.refs_5_, ...), custom_call_target="tpu_custom_call" | custom-call | flops 11000000512 | tf_op jit(solution)/shard_map/attn_fwd/pallas_call | solution.py:175
  24.4 2.1 %collective-permute-start.3 = (bf16[256,768]{1,0:T(8,128)(2,1)S(1)}, bf16[256,768]{1,0:T(8,128)(2,1)S(1)}, u32[]{:S(2)}, u32[]{:S(2)}) collective-permute-start(bf16[256,768]{1,0:T(8,128)(2,1)S(1)} %get-tuple-element.114.refs_1_.refs_5_), channel_id=1, source_target_pairs={{0,2},{1,3},{2,0},{3,1},{4,6},{5,7},{6,4},{7,5},{8,10},{9,11},{10,... | collective-permute-start | bytes 1179656 | tf_op jit(solution)/shard_map/ppermute | solution.py:366
  26.5 9.1 %layer_own.1 = (bf16[256,768]{1,0:T(8,128)(2,1)S(1)}, bf16[256,3072]{1,0:T(8,128)(2,1)S(1)}, bf16[256,768]{1,0:T(8,128)(2,1)S(1)}, bf16[256,3072]{1,0:T(8,128)(2...) custom-call(bf16[256,768]{1,0:T(8,128)(2,1)S(1)} %bitcast.76, ...), custom_call_target="tpu_custom_call" | custom-call | flops 9900000256 | tf_op jit(solution)/shard_map/layer_own/pallas_call | solution.py:659
  35.9 7.7 %layer_other.1 = (bf16[256,768]{1,0:T(8,128)(2,1)S(1)}, bf16[256,3072]{1,0:T(8,128)(2,1)S(1)}, bf16[256,768]{1,0:T(8,128)(2,1)S(1)}, bf16[256,3072]{1,0:T(8,128)(2,1)S(1)}, bf16[256,768]{1,0:T(8,128)(2,1)S(1)}) custom-call(bf16[256,768]{1,0:T(8,128)(2,1)S(1)} %collective-permute-done.refs_3_.refs_0_.refs_7_, ...), custom_call_target="tpu_custom_call" | custom-call | flops 9900000256 | tf_op jit(solution)/shard_map/layer_other/pallas_call | solution.py:659
  43.6 2.7 %grads_up_proj.1 = (bf16[1,2,4,240,384]{4,3,2,1,0:T(8,128)(2,1)S(1)}, bf16[1,2,4,240,384]{4,3,2,1,0:T(8,128)(2,1)S(1)}) custom-call(s32[4]{0:T(128)S(1)} %pad_add_fusion.refs_0_, bf16[256,768]{1,0:T(8,128)(2,1)S(1)} %get-tuple-element.127.refs_1_, bf16[256,3072]{1,0:T(8,128)(2,1)S(1)} %get-tuple-element.128.refs_2_, ...), custom_call_target="tpu_custom_call" | custom-call | flops 11000000 | tf_op jit(solution)/shard_map/grads_up_proj/pallas_call | solution.py:267
  46.4 2.2 %grads_down.1 = (bf16[1,2,4,192,384]{4,3,2,1,0:T(8,128)(2,1)S(1)}, bf16[1,2,4,192,384]{4,3,2,1,0:T(8,128)(2,1)S(1)}) custom-call(s32[4]{0:T(128)S(1)} %pad_add_fusion.refs_0_, bf16[256,3072]{1,0:T(8,128)(2,1)S(1)} %get-tuple-element.119.refs_1_, bf16[256,768]{1,0:T(8,128)(2,1)S(1)} %get-tuple-element.120.refs_2_, ...), custom_call_target="tpu_custom_call" | custom-call | flops 11000000 | tf_op jit(solution)/shard_map/grads_down/pallas_call | solution.py:267
  48.7 0.6 collective-permute-start.5
  49.2 0.4 collective-permute-done.6
  49.9 1.8 %collective-permute-start.8 = (bf16[4,240,384]{2,1,0:T(8,128)(2,1)S(1)}, bf16[4,240,384]{2,1,0:T(8,128)(2,1)S(1)}, u32[]{:S(2)}, u32[]{:S(2)}) collective-permute-start(bf16[4,240,384]{2,1,0:T(8,128)(2,1)S(1)} %fusion.2), channel_id=1, source_target_pairs={{0,4},{4,0},{8,12},{12,8},{16,20},{20,16},{24,28},{28,24},{1,5},{5... | collective-permute-start | bytes 2211848 | tf_op jit(solution)/shard_map/ppermute | solution.py:366
  51.9 1.9 %collective-permute-start.7 = (bf16[2,2,192,384]{3,2,1,0:T(8,128)(2,1)S(1)}, bf16[2,2,192,384]{3,2,1,0:T(8,128)(2,1)S(1)}, u32[]{:S(2)}, u32[]{:S(2)}) collective-permute-start(bf16[2,2,192,384]{3,2,1,0:T(8,128)(2,1)S(1)} %add_convert_fusion.1), channel_id=1, source_target_pairs={{0,8},{4,12},{8,0},{12,4},{16,24},{20,28},{24,16},{28,20},{1,9},{5... | collective-permute-start | bytes 1769480 | tf_op jit(solution)/shard_map/ppermute | solution.py:366
  53.8 13.8 %attn_bwd.1 = (bf16[256,768]{1,0:T(8,128)(2,1)S(1)}, bf16[1024,768]{1,0:T(8,128)(2,1)S(1)}, bf16[1024,768]{1,0:T(8,128)(2,1)S(1)}) custom-call(bf16[256,768]{1,0:T(8,128)(2,1)S(1)} %get-tuple-element.102.refs_0_, f32[4,1024]{1,0:T(4,128)S(1)} %block_bias.1.refs_1_, bf16[256,768]{1,0:T(8,128)(2,1)S(1)} %get-tuple-element.137.refs_2_, ...), custom_call_target="tpu_custom_call" | custom-call | flops 11000000 | tf_op jit(solution)/shard_map/attn_bwd/pallas_call | solution.py:193
  67.5 4.0 %grads_qkv.1 = (bf16[2,2,4,144,384]{4,3,2,1,0:T(8,128)(2,1)S(1)}, bf16[2,2,4,144,384]{4,3,2,1,0:T(8,128)(2,1)S(1)}, f32[16,768]{1,0:T(8,128)S(1)}) custom-call(s32[4]{0:T(128)S(1)} %pad_add_fusion.refs_0_, bf16[256,768]{1,0:T(8,128)(2,1)S(1)} %get-tuple-element.139.refs_1_, bf16[1024,768]{1,0:T(8,128)(2,1)S(1)} %get-tuple-element.146.refs_2_.refs_0_, ...), custom_call_target="tpu_custom_call" | custom-call | flops 11000000 | tf_op jit(solution)/shard_map/grads_qkv/pallas_call | solution.py:315
  72.0 2.7 %token_terms.1 = (bf16[512,768]{1,0:T(8,128)(2,1)S(1)}, bf16[544,768]{1,0:T(8,128)(2,1)S(1)}) custom-call(bf16[1024,768]{1,0:T(8,128)(2,1)S(1)} %get-tuple-element.146.refs_2_.refs_0_, bf16[1024,768]{1,0:T(8,128)(2,1)S(1)} %get-tuple-element.147.refs_3_.refs_1_, bf16[768,768]{1,0:T(8,128)(2,1)S(1)} %copy-done.2, bf16[768,768]{1,0:T(8,128)(2,1)S(1)} %copy-done.3, ...), custom_call_target="tpu_custom_call" | custom-call | flops 13200000000 | tf_op jit(solution)/shard_map/token_terms/pallas_call | solution.py:513
  74.7 0.5 collective-permute-start.9
  75.2 1.5 collective-permute-start.12
  76.6 0.5 collective-permute-start.15
  77.2 1.6 collective-permute-start.13
  78.9 0.6 collective-permute-start.14
  80.0 6.9 %collective-permute-done.15 = bf16[2,240,384]{2,1,0:T(8,128)(2,1)S(1)} collective-permute-done((bf16[2,240,384]{2,1,0:T(8,128)(2,1)S(1)}, bf16[2,240,384]{2,1,0:T(8,128)(2,1)S(1)}, u32[]{:S(2)}, u32[]{:S(2)}) %collective-permute-start.15) | collective-permute-done | bytes 368672 | tf_op jit(solution)/shard_map/ppermute | solution.py:366
  87.0 2.7 %collective-permute-start.19 = (bf16[1,240,384]{2,1,0:T(8,128)(2,1)S(1)}, bf16[1,240,384]{2,1,0:T(8,128)(2,1)S(1)}, u32[]{:S(2)}, u32[]{:S(2)}) collective-permute-start(bf16[1,240,384]{2,1,0:T(8,128)(2,1)S(1)} %fusion.14), channel_id=1, source_target_pairs={{0,16},{4,20},{8,24},{12,28},{16,0},{20,4},{24,8},{28,12},{1,17},{... | collective-permute-start | bytes 552968 | tf_op jit(solution)/shard_map/ppermute | solution.py:366
  89.7 0.7 collective-permute-done.13
  90.4 3.2 %collective-permute-done.14 = bf16[2,2,144,384]{3,2,1,0:T(8,128)(2,1)S(1)} collective-permute-done((bf16[2,2,144,384]{3,2,1,0:T(8,128)(2,1)S(1)}, bf16[2,2,144,384]{3,2,1,0:T(8,128)(2,1)S(1)}, u32[]{:S(2)}, u32[]{:S(2)}) %collective-permute-start.14) | collective-permute-done | bytes 442400 | tf_op jit(solution)/shard_map/ppermute | solution.py:366
  93.8 1.5 collective-permute-start.17
  95.4 1.6 collective-permute-start.18
  97.0 2.6 %collective-permute-start.16 = (bf16[1,192,384]{2,1,0:T(8,128)(2,1)S(1)}, bf16[1,192,384]{2,1,0:T(8,128)(2,1)S(1)}, u32[]{:S(2)}, u32[]{:S(2)}) collective-permute-start(bf16[1,192,384]{2,1,0:T(8,128)(2,1)S(1)} %fusion.16), channel_id=1, source_target_pairs={{0,16},{4,20},{8,24},{12,28},{16,0},{20,4},{24,8},{28,12},{1,17},{... | collective-permute-start | bytes 442376 | tf_op jit(solution)/shard_map/ppermute | solution.py:366
  100.4 2.7 %collective-permute-done.18 = bf16[2,144,384]{2,1,0:T(8,128)(2,1)S(1)} collective-permute-done((bf16[2,144,384]{2,1,0:T(8,128)(2,1)S(1)}, bf16[2,144,384]{2,1,0:T(8,128)(2,1)S(1)}, u32[]{:S(2)}, u32[]{:S(2)}) %collective-permute-start.18) | collective-permute-done | bytes 221216 | tf_op jit(solution)/shard_map/ppermute | solution.py:366
  103.2 1.6 collective-permute-start.21
  104.9 5.5 %collective-permute-done.16 = bf16[1,192,384]{2,1,0:T(8,128)(2,1)S(1)} collective-permute-done((bf16[1,192,384]{2,1,0:T(8,128)(2,1)S(1)}, bf16[1,192,384]{2,1,0:T(8,128)(2,1)S(1)}, u32[]{:S(2)}, u32[]{:S(2)}) %collective-permute-start.16) | collective-permute-done | bytes 147488 | tf_op jit(solution)/shard_map/ppermute | solution.py:366
  110.5 5.2 %collective-permute-done.21 = bf16[2,144,384]{2,1,0:T(8,128)(2,1)S(1)} collective-permute-done((bf16[2,144,384]{2,1,0:T(8,128)(2,1)S(1)}, bf16[2,144,384]{2,1,0:T(8,128)(2,1)S(1)}, u32[]{:S(2)}, u32[]{:S(2)}) %collective-permute-start.21) | collective-permute-done | bytes 221216 | tf_op jit(solution)/shard_map/ppermute | solution.py:366
  115.9 1.6 collective-permute-done.23
  117.5 1.2 collective-permute-start.25
  118.7 0.6 collective-permute-start.26
  119.3 5.2 %collective-permute-done.22 = bf16[1,144,384]{2,1,0:T(8,128)(2,1)S(1)} collective-permute-done((bf16[1,144,384]{2,1,0:T(8,128)(2,1)S(1)}, bf16[1,144,384]{2,1,0:T(8,128)(2,1)S(1)}, u32[]{:S(2)}, u32[]{:S(2)}) %collective-permute-start.22) | collective-permute-done | bytes 110624 | tf_op jit(solution)/shard_map/ppermute | solution.py:366
  124.8 3.1 %collective-permute-start.29 = (bf16[2,192,384]{2,1,0:T(8,128)(2,1)S(1)}, bf16[2,192,384]{2,1,0:T(8,128)(2,1)S(1)}, u32[]{:S(2)}, u32[]{:S(2)}) collective-permute-start(bf16[2,192,384]{2,1,0:T(8,128)(2,1)S(1)} %pad_maximum_fusion.2.refs_1_), channel_id=1, source_target_pairs={{0,8},{4,12},{8,0},{12,4},{16,24},{20,28},{24,16},{28,20},{1,9},{5... | collective-permute-start | bytes 884744 | tf_op jit(solution)/shard_map/ppermute | solution.py:366
  127.9 0.5 collective-permute-start.30
  128.5 6.0 %collective-permute-done.25.refs_2_ = bf16[2,240,384]{2,1,0:T(8,128)(2,1)S(1)} collective-permute-done((bf16[2,240,384]{2,1,0:T(8,128)(2,1)S(1)}, bf16[2,240,384]{2,1,0:T(8,128)(2,1)S(1)}, u32[]{:S(2)}, u32[]{:S(2)}) %collective-permute-start.25) | collective-permute-done | bytes 368672 | tf_op jit(solution)/shard_map/ppermute | solution.py:366
  134.5 0.6 collective-permute-start.34
  135.2 1.5 collective-permute-start.28
  136.7 4.1 %collective-permute-done.29.refs_2_ = bf16[2,192,384]{2,1,0:T(8,128)(2,1)S(1)} collective-permute-done((bf16[2,192,384]{2,1,0:T(8,128)(2,1)S(1)}, bf16[2,192,384]{2,1,0:T(8,128)(2,1)S(1)}, u32[]{:S(2)}, u32[]{:S(2)}) %collective-permute-start.29) | collective-permute-done | bytes 294944 | tf_op jit(solution)/shard_map/ppermute | solution.py:366
  140.8 0.6 collective-permute-start.32
  141.4 2.3 %collective-permute-done.27.refs_2_ = bf16[2,144,384]{2,1,0:T(8,128)(2,1)S(1)} collective-permute-done((bf16[2,144,384]{2,1,0:T(8,128)(2,1)S(1)}, bf16[2,144,384]{2,1,0:T(8,128)(2,1)S(1)}, u32[]{:S(2)}, u32[]{:S(2)}) %collective-permute-start.27) | collective-permute-done | bytes 221216 | tf_op jit(solution)/shard_map/ppermute | solution.py:366
  143.7 4.6 %collective-permute-done.28.refs_3_ = bf16[2,144,384]{2,1,0:T(8,128)(2,1)S(1)} collective-permute-done((bf16[2,144,384]{2,1,0:T(8,128)(2,1)S(1)}, bf16[2,144,384]{2,1,0:T(8,128)(2,1)S(1)}, u32[]{:S(2)}, u32[]{:S(2)}) %collective-permute-start.28) | collective-permute-done | bytes 221216 | tf_op jit(solution)/shard_map/ppermute | solution.py:366
  148.3 0.5 collective-permute-done.32
  148.8 0.4 collective-permute-start.33
  149.3 0.5 collective-permute-start.35
  149.8 1.5 collective-permute-start.31
  151.3 2.3 %assemble_U.1 = (f32[192,3072]{1,0:T(8,128)}, f32[192,768]{1,0:T(8,128)}) custom-call(s32[4]{0:T(128)S(1)} %pad_add_fusion.refs_0_, bf16[2,240,384]{2,1,0:T(8,128)(2,1)S(1)} %pad_maximum_fusion.1.refs_1_, bf16[2,240,384]{2,1,0:T(8,128)(2,1)S(1)} %collective-permute-done.25.refs_2_, bf16[2,240,384]{2,1,0:T(8,128)(2,1)S(1)} %collective-permute-done.26.refs_3_, ...), custom_call_target="tpu_custom_call" | custom-call | flops 11000000 | tf_op jit(solution)/shard_map/assemble_U/pallas_call | solution.py:353
  153.6 2.6 %collective-permute-start.36 = (f32[16,768]{1,0:T(8,128)S(1)}, f32[16,768]{1,0:T(8,128)S(1)}, u32[]{:S(2)}, u32[]{:S(2)}) collective-permute-start(f32[16,768]{1,0:T(8,128)S(1)} %add.345), channel_id=1, source_target_pairs={{0,16},{4,20},{8,24},{12,28},{16,0},{20,4},{24,8},{28,12},{1,17},{... | collective-permute-start | bytes 147464 | tf_op jit(solution)/shard_map/ppermute | solution.py:366
  156.3 1.4 fusion.1
  157.9 2.1 %assemble_D.1 = f32[768,768]{1,0:T(8,128)} custom-call(s32[4]{0:T(128)S(1)} %pad_add_fusion.refs_0_, bf16[2,192,384]{2,1,0:T(8,128)(2,1)S(1)} %pad_maximum_fusion.2.refs_1_, bf16[2,192,384]{2,1,0:T(8,128)(2,1)S(1)} %collective-permute-done.29.refs_2_, bf16[2,192,384]{2,1,0:T(8,128)(2,1)S(1)} %collective-permute-done.30.refs_3_, ...), custom_call_target="tpu_custom_call" | custom-call | flops 11000000 | tf_op jit(solution)/shard_map/assemble_D/pallas_call | solution.py:353
  160.1 0.6 slice.395
  160.7 0.7 slice_reduce_fusion
  161.3 1.9 %assemble_C.1 = (f32[192,768]{1,0:T(8,128)}, f32[192,768]{1,0:T(8,128)}, f32[192,768]{1,0:T(8,128)}) custom-call(s32[4]{0:T(128)S(1)} %pad_add_fusion.refs_0_, bf16[2,144,384]{2,1,0:T(8,128)(2,1)S(1)} %pad_maximum_fusion.3.refs_1_, bf16[2,144,384]{2,1,0:T(8,128)(2,1)S(1)} %collective-permute-done.27.refs_2_, ...), custom_call_target="tpu_custom_call" | custom-call | flops 11000000 | tf_op jit(solution)/shard_map/assemble_C/pallas_call | solution.py:353
  (98 shorter events, 5.3 us)
Async XLA Ops:
  0.7 13.2 %collective-permute-start = (bf16[256,768]{1,0:T(8,128)(2,1)}, bf16[256,768]{1,0:T(8,128)(2,1)S(1)}, u32[]{:S(2)}, u32[]{:S(2)}) collective-permute-start(bf16[256,768]{1,0:T(8,128)(2,1)} %bitcast.73), channel_id=1, source_target_pairs={{0,2},{1,3},{2,0},{3,1},{4,6},{5,7},{6,4},{7,5},{8,10},{9,11},{10,... | collective-permute-start | bytes 1179656 | tf_op jit(solution)/shard_map/ppermute | solution.py:366
  3.7 3.9 %collective-permute-start.1 = (bf16[256,768]{1,0:T(8,128)(2,1)}, bf16[256,768]{1,0:T(8,128)(2,1)S(1)}, u32[]{:S(2)}, u32[]{:S(2)}) collective-permute-start(bf16[256,768]{1,0:T(8,128)(2,1)} %bitcast.74), channel_id=1, source_target_pairs={{0,1},{1,0},{2,3},{3,2},{4,5},{5,4},{6,7},{7,6},{8,9},{9,8},{10,11... | collective-permute-start | bytes 1179656 | tf_op jit(solution)/shard_map/ppermute | solution.py:366
  3.7 32.2 %collective-permute-start.4 = (bf16[256,768]{1,0:T(8,128)(2,1)}, bf16[256,768]{1,0:T(8,128)(2,1)S(1)}, u32[]{:S(2)}, u32[]{:S(2)}) collective-permute-start(bf16[256,768]{1,0:T(8,128)(2,1)} %bitcast.86), channel_id=1, source_target_pairs={{0,2},{1,3},{2,0},{3,1},{4,6},{5,7},{6,4},{7,5},{8,10},{9,11},{10,... | collective-permute-start | bytes 1179656 | tf_op jit(solution)/shard_map/ppermute | solution.py:366
  6.7 0.8 copy-start.9
  6.7 0.8 copy-start.10
  6.7 1.3 copy-start
  6.7 1.4 copy-start.1
  6.7 1.8 %copy-start.2 = (bf16[768,768]{1,0:T(8,128)(2,1)S(1)}, bf16[768,768]{1,0:T(8,128)(2,1)}, u32[]{:S(2)}) copy-start(bf16[768,768]{1,0:T(8,128)(2,1)} %refs_2_.8) | copy-start | bytes 3538948
  6.7 2.1 %copy-start.3 = (bf16[768,768]{1,0:T(8,128)(2,1)S(1)}, bf16[768,768]{1,0:T(8,128)(2,1)}, u32[]{:S(2)}) copy-start(bf16[768,768]{1,0:T(8,128)(2,1)} %refs_3_.5) | copy-start | bytes 3538948
  6.8 2.1 %copy-start.4 = (bf16[768]{0:T(1024)(128)(2,1)S(1)}, bf16[768]{0:T(1024)(128)(2,1)}, u32[]{:S(2)}) copy-start(bf16[768]{0:T(1024)(128)(2,1)} %refs_6_.1) | copy-start | bytes 4612
  6.8 2.1 %copy-start.5 = (bf16[768]{0:T(1024)(128)(2,1)S(1)}, bf16[768]{0:T(1024)(128)(2,1)}, u32[]{:S(2)}) copy-start(bf16[768]{0:T(1024)(128)(2,1)} %refs_2_.7) | copy-start | bytes 4612
  7.5 6.3 %copy-start.11 = (bf16[768]{0:T(1024)(128)(2,1)S(1)}, bf16[768]{0:T(1024)(128)(2,1)}, u32[]{:S(2)}) copy-start(bf16[768]{0:T(1024)(128)(2,1)} %param.33) | copy-start | bytes 4612
  7.6 6.3 %copy-start.12 = (bf16[768]{0:T(1024)(128)(2,1)S(1)}, bf16[768]{0:T(1024)(128)(2,1)}, u32[]{:S(2)}) copy-start(bf16[768]{0:T(1024)(128)(2,1)} %param.34) | copy-start | bytes 4612
  7.6 6.3 %copy-start.8 = (bf16[3072]{0:T(1024)(128)(2,1)S(1)}, bf16[3072]{0:T(1024)(128)(2,1)}, u32[]{:S(2)}) copy-start(bf16[3072]{0:T(1024)(128)(2,1)} %param.30) | copy-start | bytes 18436
  13.8 1.7 %collective-permute-start.2 = (bf16[256,768]{1,0:T(8,128)(2,1)S(1)}, bf16[256,768]{1,0:T(8,128)(2,1)S(1)}, u32[]{:S(2)}, u32[]{:S(2)}) collective-permute-start(bf16[256,768]{1,0:T(8,128)(2,1)S(1)} %collective-permute-done.refs_3_.refs_0_.refs_7_), channel_id=1, source_target_pairs={{0,1},{1,0},{2,3},{3,2},{4,5},{5,4},{6,7},{7,6},{8,9},{9,8},{10,11... | collective-permute-start | bytes 1179656 | tf_op jit(solution)/shard_map/ppermute | solution.py:366
  15.6 10.9 %slice-start = ((s8[4718592]{0:T(1024)(128)(4,1)}), s8[4194304]{0:T(1024)(128)(4,1)S(1)}, s32[]{:S(2)}) async-start(s8[4718592]{0:T(1024)(128)(4,1)} %bitcast.82), calls=%async_computation | async-start | bytes 8388608
  15.6 10.9 %slice-start.2 = ((s8[4718592]{0:T(1024)(128)(4,1)}), s8[4194304]{0:T(1024)(128)(4,1)S(1)}, s32[]{:S(2)}) async-start(s8[4718592]{0:T(1024)(128)(4,1)} %bitcast.84), calls=%async_computation.2 | async-start | bytes 8388608
  16.4 10.1 %slice-start.1 = ((s8[4718592]{0:T(1024)(128)(4,1)}), s8[524288]{0:T(1024)(128)(4,1)S(1)}, s32[]{:S(2)}) async-start(s8[4718592]{0:T(1024)(128)(4,1)} %bitcast.82), calls=%async_computation.1 | async-start | bytes 1048576
  16.4 10.1 %slice-start.3 = ((s8[4718592]{0:T(1024)(128)(4,1)}), s8[524288]{0:T(1024)(128)(4,1)S(1)}, s32[]{:S(2)}) async-start(s8[4718592]{0:T(1024)(128)(4,1)} %bitcast.84), calls=%async_computation.3 | async-start | bytes 1048576
  16.4 10.1 %copy-start.6 = (bf16[768,768]{1,0:T(8,128)(2,1)S(1)}, bf16[768,768]{1,0:T(8,128)(2,1)}, u32[]{:S(2)}) copy-start(bf16[768,768]{1,0:T(8,128)(2,1)} %refs_3_.4) | copy-start | bytes 3538948
  16.4 10.1 %copy-start.7 = (bf16[1,256,768]{2,1,0:T(8,128)(2,1)S(1)}, bf16[1,256,768]{2,1,0:T(8,128)(2,1)}, u32[]{:S(2)}) copy-start(bf16[1,256,768]{2,1,0:T(8,128)(2,1)} %param.37) | copy-start | bytes 1179652
  24.4 11.5 %collective-permute-start.3 = (bf16[256,768]{1,0:T(8,128)(2,1)S(1)}, bf16[256,768]{1,0:T(8,128)(2,1)S(1)}, u32[]{:S(2)}, u32[]{:S(2)}) collective-permute-start(bf16[256,768]{1,0:T(8,128)(2,1)S(1)} %get-tuple-element.114.refs_1_.refs_5_), channel_id=1, source_target_pairs={{0,2},{1,3},{2,0},{3,1},{4,6},{5,7},{6,4},{7,5},{8,10},{9,11},{10,... | collective-permute-start | bytes 1179656 | tf_op jit(solution)/shard_map/ppermute | solution.py:366
  46.3 3.3 %collective-permute-start.6 = (bf16[1,2,4,240,384]{4,3,2,1,0:T(8,128)(2,1)S(1)}, bf16[1,2,4,240,384]{4,3,2,1,0:T(8,128)(2,1)S(1)}, u32[]{:S(2)}, u32[]{:S(2)}) collective-permute-start(bf16[1,2,4,240,384]{4,3,2,1,0:T(8,128)(2,1)S(1)} %get-tuple-element.134), channel_id=1, source_target_pairs={{0,1},{1,0},{2,3},{3,2},{4,5},{5,4},{6,7},{7,6},{8,9},{9,8},{10,11... | collective-permute-start | bytes 4423688 | tf_op jit(solution)/shard_map/ppermute | solution.py:366
  48.7 3.0 %collective-permute-start.5 = (bf16[1,2,4,192,384]{4,3,2,1,0:T(8,128)(2,1)S(1)}, bf16[1,2,4,192,384]{4,3,2,1,0:T(8,128)(2,1)S(1)}, u32[]{:S(2)}, u32[]{:S(2)}) collective-permute-start(bf16[1,2,4,192,384]{4,3,2,1,0:T(8,128)(2,1)S(1)} %get-tuple-element.126), channel_id=1, source_target_pairs={{0,1},{1,0},{2,3},{3,2},{4,5},{5,4},{6,7},{7,6},{8,9},{9,8},{10,11... | collective-permute-start | bytes 3538952 | tf_op jit(solution)/shard_map/ppermute | solution.py:366
  49.9 21.9 %collective-permute-start.8 = (bf16[4,240,384]{2,1,0:T(8,128)(2,1)S(1)}, bf16[4,240,384]{2,1,0:T(8,128)(2,1)S(1)}, u32[]{:S(2)}, u32[]{:S(2)}) collective-permute-start(bf16[4,240,384]{2,1,0:T(8,128)(2,1)S(1)} %fusion.2), channel_id=1, source_target_pairs={{0,4},{4,0},{8,12},{12,8},{16,20},{20,16},{24,28},{28,24},{1,5},{5... | collective-permute-start | bytes 2211848 | tf_op jit(solution)/shard_map/ppermute | solution.py:366
  51.9 20.0 %collective-permute-start.7 = (bf16[2,2,192,384]{3,2,1,0:T(8,128)(2,1)S(1)}, bf16[2,2,192,384]{3,2,1,0:T(8,128)(2,1)S(1)}, u32[]{:S(2)}, u32[]{:S(2)}) collective-permute-start(bf16[2,2,192,384]{3,2,1,0:T(8,128)(2,1)S(1)} %add_convert_fusion.1), channel_id=1, source_target_pairs={{0,8},{4,12},{8,0},{12,4},{16,24},{20,28},{24,16},{28,20},{1,9},{5... | collective-permute-start | bytes 1769480 | tf_op jit(solution)/shard_map/ppermute | solution.py:366
  71.6 5.5 %collective-permute-start.10 = (bf16[2,2,4,144,384]{4,3,2,1,0:T(8,128)(2,1)S(1)}, bf16[2,2,4,144,384]{4,3,2,1,0:T(8,128)(2,1)S(1)}, u32[]{:S(2)}, u32[]{:S(2)}) collective-permute-start(bf16[2,2,4,144,384]{4,3,2,1,0:T(8,128)(2,1)S(1)} %get-tuple-element.143), channel_id=1, source_target_pairs={{0,1},{1,0},{2,3},{3,2},{4,5},{5,4},{6,7},{7,6},{8,9},{9,8},{10,11... | collective-permute-start | bytes 5308424 | tf_op jit(solution)/shard_map/ppermute | solution.py:366
  74.7 4.9 %collective-permute-start.9 = (bf16[544,768]{1,0:T(8,128)(2,1)S(1)}, bf16[544,768]{1,0:T(8,128)(2,1)S(1)}, u32[]{:S(2)}, u32[]{:S(2)}) collective-permute-start(bf16[544,768]{1,0:T(8,128)(2,1)S(1)} %get-tuple-element.150), channel_id=1, source_target_pairs={{0,1},{1,0},{2,3},{3,2},{4,5},{5,4},{6,7},{7,6},{8,9},{9,8},{10,11... | collective-permute-start | bytes 2506760 | tf_op jit(solution)/shard_map/ppermute | solution.py:366
  75.2 21.8 %collective-permute-start.12 = (bf16[2,192,384]{2,1,0:T(8,128)(2,1)S(1)}, bf16[2,192,384]{2,1,0:T(8,128)(2,1)S(1)}, u32[]{:S(2)}, u32[]{:S(2)}) collective-permute-start(bf16[2,192,384]{2,1,0:T(8,128)(2,1)S(1)} %fusion.15), channel_id=1, source_target_pairs={{0,4},{4,0},{8,12},{12,8},{16,20},{20,16},{24,28},{28,24},{1,5},{5... | collective-permute-start | bytes 884744 | tf_op jit(solution)/shard_map/ppermute | solution.py:366
  76.6 10.3 %collective-permute-start.15 = (bf16[2,240,384]{2,1,0:T(8,128)(2,1)S(1)}, bf16[2,240,384]{2,1,0:T(8,128)(2,1)S(1)}, u32[]{:S(2)}, u32[]{:S(2)}) collective-permute-start(bf16[2,240,384]{2,1,0:T(8,128)(2,1)S(1)} %fusion.3), channel_id=1, source_target_pairs={{0,8},{4,12},{8,0},{12,4},{16,24},{20,28},{24,16},{28,20},{1,9},{5... | collective-permute-start | bytes 1105928 | tf_op jit(solution)/shard_map/ppermute | solution.py:366
  77.2 13.2 %collective-permute-start.13 = (bf16[2,2,144,384]{3,2,1,0:T(8,128)(2,1)S(1)}, bf16[2,2,144,384]{3,2,1,0:T(8,128)(2,1)S(1)}, u32[]{:S(2)}, u32[]{:S(2)}) collective-permute-start(bf16[2,2,144,384]{3,2,1,0:T(8,128)(2,1)S(1)} %fusion.4), channel_id=1, source_target_pairs={{0,2},{1,3},{2,0},{3,1},{4,6},{5,7},{6,4},{7,5},{8,10},{9,11},{10,... | collective-permute-start | bytes 1327112 | tf_op jit(solution)/shard_map/ppermute | solution.py:366
  78.9 14.7 %collective-permute-start.14 = (bf16[2,2,144,384]{3,2,1,0:T(8,128)(2,1)S(1)}, bf16[2,2,144,384]{3,2,1,0:T(8,128)(2,1)S(1)}, u32[]{:S(2)}, u32[]{:S(2)}) collective-permute-start(bf16[2,2,144,384]{3,2,1,0:T(8,128)(2,1)S(1)} %fusion.5), channel_id=1, source_target_pairs={{0,4},{4,0},{8,12},{12,8},{16,20},{20,16},{24,28},{28,24},{1,5},{5... | collective-permute-start | bytes 1327112 | tf_op jit(solution)/shard_map/ppermute | solution.py:366
  79.7 48.2 %collective-permute-start.11 = (bf16[288,768]{1,0:T(8,128)(2,1)S(1)}, bf16[288,768]{1,0:T(8,128)(2,1)S(1)}, u32[]{:S(2)}, u32[]{:S(2)}) collective-permute-start(bf16[288,768]{1,0:T(8,128)(2,1)S(1)} %pad_maximum_fusion), channel_id=1, source_target_pairs={{0,2},{1,3},{2,0},{3,1},{4,6},{5,7},{6,4},{7,5},{8,10},{9,11},{10,... | collective-permute-start | bytes 1327112 | tf_op jit(solution)/shard_map/ppermute | solution.py:366
  87.0 12.6 %collective-permute-start.19 = (bf16[1,240,384]{2,1,0:T(8,128)(2,1)S(1)}, bf16[1,240,384]{2,1,0:T(8,128)(2,1)S(1)}, u32[]{:S(2)}, u32[]{:S(2)}) collective-permute-start(bf16[1,240,384]{2,1,0:T(8,128)(2,1)S(1)} %fusion.14), channel_id=1, source_target_pairs={{0,16},{4,20},{8,24},{12,28},{16,0},{20,4},{24,8},{28,12},{1,17},{... | collective-permute-start | bytes 552968 | tf_op jit(solution)/shard_map/ppermute | solution.py:366
  93.8 6.6 %collective-permute-start.17 = (bf16[2,144,384]{2,1,0:T(8,128)(2,1)S(1)}, bf16[2,144,384]{2,1,0:T(8,128)(2,1)S(1)}, u32[]{:S(2)}, u32[]{:S(2)}) collective-permute-start(bf16[2,144,384]{2,1,0:T(8,128)(2,1)S(1)} %get-tuple-element.196), channel_id=1, source_target_pairs={{0,4},{4,0},{8,12},{12,8},{16,20},{20,16},{24,28},{28,24},{1,5},{5... | collective-permute-start | bytes 663560 | tf_op jit(solution)/shard_map/ppermute | solution.py:366
  95.4 7.8 %collective-permute-start.18 = (bf16[2,144,384]{2,1,0:T(8,128)(2,1)S(1)}, bf16[2,144,384]{2,1,0:T(8,128)(2,1)S(1)}, u32[]{:S(2)}, u32[]{:S(2)}) collective-permute-start(bf16[2,144,384]{2,1,0:T(8,128)(2,1)S(1)} %get-tuple-element.195), channel_id=1, source_target_pairs={{0,2},{1,3},{2,0},{3,1},{4,6},{5,7},{6,4},{7,5},{8,10},{9,11},{10,... | collective-permute-start | bytes 663560 | tf_op jit(solution)/shard_map/ppermute | solution.py:366
  97.0 13.4 %collective-permute-start.16 = (bf16[1,192,384]{2,1,0:T(8,128)(2,1)S(1)}, bf16[1,192,384]{2,1,0:T(8,128)(2,1)S(1)}, u32[]{:S(2)}, u32[]{:S(2)}) collective-permute-start(bf16[1,192,384]{2,1,0:T(8,128)(2,1)S(1)} %fusion.16), channel_id=1, source_target_pairs={{0,16},{4,20},{8,24},{12,28},{16,0},{20,4},{24,8},{28,12},{1,17},{... | collective-permute-start | bytes 442376 | tf_op jit(solution)/shard_map/ppermute | solution.py:366
  99.8 17.7 %collective-permute-start.23 = (bf16[1,240,384]{2,1,0:T(8,128)(2,1)S(1)}, bf16[1,240,384]{2,1,0:T(8,128)(2,1)S(1)}, u32[]{:S(2)}, u32[]{:S(2)}) collective-permute-start(bf16[1,240,384]{2,1,0:T(8,128)(2,1)S(1)} %fusion.12), channel_id=1, source_target_pairs={{0,16},{4,20},{8,24},{12,28},{16,0},{20,4},{24,8},{28,12},{1,17},{... | collective-permute-start | bytes 552968 | tf_op jit(solution)/shard_map/ppermute | solution.py:366
  103.2 12.5 %collective-permute-start.21 = (bf16[2,144,384]{2,1,0:T(8,128)(2,1)S(1)}, bf16[2,144,384]{2,1,0:T(8,128)(2,1)S(1)}, u32[]{:S(2)}, u32[]{:S(2)}) collective-permute-start(bf16[2,144,384]{2,1,0:T(8,128)(2,1)S(1)} %fusion.7), channel_id=1, source_target_pairs={{0,8},{4,12},{8,0},{12,4},{16,24},{20,28},{24,16},{28,20},{1,9},{5... | collective-permute-start | bytes 663560 | tf_op jit(solution)/shard_map/ppermute | solution.py:366
  110.5 14.3 %collective-permute-start.20 = (bf16[1,192,384]{2,1,0:T(8,128)(2,1)S(1)}, bf16[1,192,384]{2,1,0:T(8,128)(2,1)S(1)}, u32[]{:S(2)}, u32[]{:S(2)}) collective-permute-start(bf16[1,192,384]{2,1,0:T(8,128)(2,1)S(1)} %fusion.18), channel_id=1, source_target_pairs={{0,16},{4,20},{8,24},{12,28},{16,0},{20,4},{24,8},{28,12},{1,17},{... | collective-permute-start | bytes 442376 | tf_op jit(solution)/shard_map/ppermute | solution.py:366
  115.8 8.7 %collective-permute-start.22 = (bf16[1,144,384]{2,1,0:T(8,128)(2,1)S(1)}, bf16[1,144,384]{2,1,0:T(8,128)(2,1)S(1)}, u32[]{:S(2)}, u32[]{:S(2)}) collective-permute-start(bf16[1,144,384]{2,1,0:T(8,128)(2,1)S(1)} %fusion.21), channel_id=1, source_target_pairs={{0,16},{4,20},{8,24},{12,28},{16,0},{20,4},{24,8},{28,12},{1,17},{... | collective-permute-start | bytes 331784 | tf_op jit(solution)/shard_map/ppermute | solution.py:366
  117.5 17.0 %collective-permute-start.25 = (bf16[2,240,384]{2,1,0:T(8,128)(2,1)S(1)}, bf16[2,240,384]{2,1,0:T(8,128)(2,1)S(1)}, u32[]{:S(2)}, u32[]{:S(2)}) collective-permute-start(bf16[2,240,384]{2,1,0:T(8,128)(2,1)S(1)} %pad_maximum_fusion.1.refs_1_), channel_id=1, source_target_pairs={{0,8},{4,12},{8,0},{12,4},{16,24},{20,28},{24,16},{28,20},{1,9},{5... | collective-permute-start | bytes 1105928 | tf_op jit(solution)/shard_map/ppermute | solution.py:366
  118.7 15.8 %collective-permute-start.26 = (bf16[2,240,384]{2,1,0:T(8,128)(2,1)S(1)}, bf16[2,240,384]{2,1,0:T(8,128)(2,1)S(1)}, u32[]{:S(2)}, u32[]{:S(2)}) collective-permute-start(bf16[2,240,384]{2,1,0:T(8,128)(2,1)S(1)} %pad_maximum_fusion.1.refs_1_), channel_id=1, source_target_pairs={{0,4},{4,0},{8,12},{12,8},{16,20},{20,16},{24,28},{28,24},{1,5},{5... | collective-permute-start | bytes 1105928 | tf_op jit(solution)/shard_map/ppermute | solution.py:366
  124.6 10.5 %collective-permute-start.24 = (bf16[1,144,384]{2,1,0:T(8,128)(2,1)S(1)}, bf16[1,144,384]{2,1,0:T(8,128)(2,1)S(1)}, u32[]{:S(2)}, u32[]{:S(2)}) collective-permute-start(bf16[1,144,384]{2,1,0:T(8,128)(2,1)S(1)} %fusion.25), channel_id=1, source_target_pairs={{0,16},{4,20},{8,24},{12,28},{16,0},{20,4},{24,8},{28,12},{1,17},{... | collective-permute-start | bytes 331784 | tf_op jit(solution)/shard_map/ppermute | solution.py:366
  124.8 16.1 %collective-permute-start.29 = (bf16[2,192,384]{2,1,0:T(8,128)(2,1)S(1)}, bf16[2,192,384]{2,1,0:T(8,128)(2,1)S(1)}, u32[]{:S(2)}, u32[]{:S(2)}) collective-permute-start(bf16[2,192,384]{2,1,0:T(8,128)(2,1)S(1)} %pad_maximum_fusion.2.refs_1_), channel_id=1, source_target_pairs={{0,8},{4,12},{8,0},{12,4},{16,24},{20,28},{24,16},{28,20},{1,9},{5... | collective-permute-start | bytes 884744 | tf_op jit(solution)/shard_map/ppermute | solution.py:366
  127.9 13.5 %collective-permute-start.30 = (bf16[2,192,384]{2,1,0:T(8,128)(2,1)S(1)}, bf16[2,192,384]{2,1,0:T(8,128)(2,1)S(1)}, u32[]{:S(2)}, u32[]{:S(2)}) collective-permute-start(bf16[2,192,384]{2,1,0:T(8,128)(2,1)S(1)} %pad_maximum_fusion.2.refs_1_), channel_id=1, source_target_pairs={{0,4},{4,0},{8,12},{12,8},{16,20},{20,16},{24,28},{28,24},{1,5},{5... | collective-permute-start | bytes 884744 | tf_op jit(solution)/shard_map/ppermute | solution.py:366
  134.5 16.8 %collective-permute-start.34 = (bf16[2,240,384]{2,1,0:T(8,128)(2,1)S(1)}, bf16[2,240,384]{2,1,0:T(8,128)(2,1)S(1)}, u32[]{:S(2)}, u32[]{:S(2)}) collective-permute-start(bf16[2,240,384]{2,1,0:T(8,128)(2,1)S(1)} %collective-permute-done.25.refs_2_), channel_id=1, source_target_pairs={{0,4},{4,0},{8,12},{12,8},{16,20},{20,16},{24,28},{28,24},{1,5},{5... | collective-permute-start | bytes 1105928 | tf_op jit(solution)/shard_map/ppermute | solution.py:366
  135.1 8.6 %collective-permute-start.27 = (bf16[2,144,384]{2,1,0:T(8,128)(2,1)S(1)}, bf16[2,144,384]{2,1,0:T(8,128)(2,1)S(1)}, u32[]{:S(2)}, u32[]{:S(2)}) collective-permute-start(bf16[2,144,384]{2,1,0:T(8,128)(2,1)S(1)} %pad_maximum_fusion.3.refs_1_), channel_id=1, source_target_pairs={{0,8},{4,12},{8,0},{12,4},{16,24},{20,28},{24,16},{28,20},{1,9},{5... | collective-permute-start | bytes 663560 | tf_op jit(solution)/shard_map/ppermute | solution.py:366
  135.2 13.1 %collective-permute-start.28 = (bf16[2,144,384]{2,1,0:T(8,128)(2,1)S(1)}, bf16[2,144,384]{2,1,0:T(8,128)(2,1)S(1)}, u32[]{:S(2)}, u32[]{:S(2)}) collective-permute-start(bf16[2,144,384]{2,1,0:T(8,128)(2,1)S(1)} %pad_maximum_fusion.3.refs_1_), channel_id=1, source_target_pairs={{0,4},{4,0},{8,12},{12,8},{16,20},{20,16},{24,28},{28,24},{1,5},{5... | collective-permute-start | bytes 663560 | tf_op jit(solution)/shard_map/ppermute | solution.py:366
  140.8 8.0 %collective-permute-start.32 = (f32[16,768]{1,0:T(8,128)S(1)}, f32[16,768]{1,0:T(8,128)S(1)}, u32[]{:S(2)}, u32[]{:S(2)}) collective-permute-start(f32[16,768]{1,0:T(8,128)S(1)} %fusion.31), channel_id=1, source_target_pairs={{0,4},{4,0},{8,12},{12,8},{16,20},{20,16},{24,28},{28,24},{1,5},{5... | collective-permute-start | bytes 147464 | tf_op jit(solution)/shard_map/ppermute | solution.py:366
  148.8 4.8 %collective-permute-start.33 = (f32[16,768]{1,0:T(8,128)S(1)}, f32[16,768]{1,0:T(8,128)S(1)}, u32[]{:S(2)}, u32[]{:S(2)}) collective-permute-start(f32[16,768]{1,0:T(8,128)S(1)} %add.344), channel_id=1, source_target_pairs={{0,8},{4,12},{8,0},{12,4},{16,24},{20,28},{24,16},{28,20},{1,9},{5... | collective-permute-start | bytes 147464 | tf_op jit(solution)/shard_map/ppermute | solution.py:366
  149.3 8.7 %collective-permute-start.35 = (bf16[2,192,384]{2,1,0:T(8,128)(2,1)S(1)}, bf16[2,192,384]{2,1,0:T(8,128)(2,1)S(1)}, u32[]{:S(2)}, u32[]{:S(2)}) collective-permute-start(bf16[2,192,384]{2,1,0:T(8,128)(2,1)S(1)} %collective-permute-done.29.refs_2_), channel_id=1, source_target_pairs={{0,4},{4,0},{8,12},{12,8},{16,20},{20,16},{24,28},{28,24},{1,5},{5... | collective-permute-start | bytes 884744 | tf_op jit(solution)/shard_map/ppermute | solution.py:366
  149.8 11.5 %collective-permute-start.31 = (bf16[2,144,384]{2,1,0:T(8,128)(2,1)S(1)}, bf16[2,144,384]{2,1,0:T(8,128)(2,1)S(1)}, u32[]{:S(2)}, u32[]{:S(2)}) collective-permute-start(bf16[2,144,384]{2,1,0:T(8,128)(2,1)S(1)} %collective-permute-done.27.refs_2_), channel_id=1, source_target_pairs={{0,4},{4,0},{8,12},{12,8},{16,20},{20,16},{24,28},{28,24},{1,5},{5... | collective-permute-start | bytes 663560 | tf_op jit(solution)/shard_map/ppermute | solution.py:366
  153.6 6.4 %collective-permute-start.36 = (f32[16,768]{1,0:T(8,128)S(1)}, f32[16,768]{1,0:T(8,128)S(1)}, u32[]{:S(2)}, u32[]{:S(2)}) collective-permute-start(f32[16,768]{1,0:T(8,128)S(1)} %add.345), channel_id=1, source_target_pairs={{0,16},{4,20},{8,24},{12,28},{16,0},{20,4},{24,8},{28,12},{1,17},{... | collective-permute-start | bytes 147464 | tf_op jit(solution)/shard_map/ppermute | solution.py:366

commit v2 on v1

--- a/solution.py
+++ b/solution.py
@@ -328,37 +328,34 @@
     )(place, d_query, d_key, d_value, sums, *tokens)
 
 
-def assemble_kernel(place_ref, *refs, plan):
-    outs = refs[len(refs) - len(plan) :]
+def assemble_kernel(place_ref, *refs, plan, places):
+    pieces, outs = refs[: len(places)], refs[len(places) :]
     x_own, z_own = place_ref[2], place_ref[3]
-    index = 0
-    for ref in refs[: len(refs) - len(plan)]:
-        for slot in range(ref.shape[0]):
-            relative, column = index % QUARTERS, index // QUARTERS
-            quarter = slot_of(relative) ^ z_own
+    for ref, indices in zip(pieces, places):
+        for at, index in enumerate(indices):
+            quarter = slot_of(index % QUARTERS) ^ z_own
+            column = (index // QUARTERS) ^ x_own
             offset = 0
             for out, (rows, cols) in zip(outs, plan):
                 height = rows // QUARTERS
-                at = pl.ds(pl.multiple_of(quarter * height, 8), height)
+                row = pl.ds(pl.multiple_of(quarter * height, 8), height)
                 for part in range(cols // 2 // LANES):
-                    lanes = pl.ds(
-                        pl.multiple_of((column ^ x_own) * (cols // 2) + part * LANES, 128), LANES
-                    )
-                    out[at, lanes] = ref[slot, offset : offset + height, :].astype(F32)
+                    start = pl.multiple_of(column * (cols // 2) + part * LANES, 128)
+                    out[row, pl.ds(start, LANES)] = ref[at, offset : offset + height, :].astype(F32)
                     offset += height
-            index += 1
 
 
 def assemble(place, pieces, plan, name):
+    places = [indices for _, indices in pieces]
     return pl.pallas_call(
-        lambda *refs: assemble_kernel(*refs, plan=plan),
+        lambda *refs: assemble_kernel(*refs, plan=plan, places=places),
         in_specs=[SMEM_SPEC] + [VMEM_SPEC] * len(pieces),
         out_specs=[VMEM_SPEC] * len(plan),
         out_shape=[jax.ShapeDtypeStruct(shape, F32) for shape in plan],
         compiler_params=pltpu.CompilerParams(vmem_limit_bytes=12 * MIB),
         cost_estimate=cost(0.01),
         name=name,
-    )(place, *pieces)
+    )(place, *[array for array, _ in pieces])
 
 
 def swap(value, axis, mask):
@@ -373,7 +370,7 @@
     return total.astype(BF16)
 
 
-STEPS = "TUCDUCDCUCDTUCDCTUTDTC"
+STEPS = "TUCDUCDTCUTCDTCUDCUTDC"
 
 
 class Order:
@@ -414,16 +411,45 @@
     return piece
 
 
-def gather_dp(order, piece):
+def gather_dp(order, piece, mode):
+    if mode == "xzz":
+        far = exchange(order, [piece], [("dp", 1)])
+        yield
+        both = jnp.concatenate([piece, *order.after(*far)])
+        got = exchange(order, [both], [("dp", 4)])
+        yield
+        four = jnp.concatenate([both, *order.after(*got)])
+        got = exchange(order, [four], [("dp", 2)])
+        yield
+        return [(four, (0, 4, 1, 5)), (*order.after(*got), (2, 6, 3, 7))]
     got = exchange(order, [piece], [("dp", 4)])
     yield
     first = jnp.concatenate([piece, *order.after(*got)])
-    got = exchange(order, [first, first], [("dp", 2), ("dp", 1)])
-    yield
-    second, far_first = order.after(*got)
-    got = exchange(order, [second], [("dp", 1)])
-    yield
-    return [first, second, far_first, *order.after(*got)]
+    if mode == "zxz":
+        far = exchange(order, [first], [("dp", 1)])
+        yield
+        four = jnp.concatenate([first, *order.after(*far)])
+        got = exchange(order, [four], [("dp", 2)])
+        yield
+        return [(four, (0, 1, 4, 5)), (*order.after(*got), (2, 3, 6, 7))]
+    if mode == "zzx split":
+        got = exchange(order, [first, first], [("dp", 2), ("dp", 1)])
+        yield
+        second, far_first = order.after(*got)
+        got = exchange(order, [second], [("dp", 1)])
+        yield
+        return [
+            (first, (0, 1)),
+            (second, (2, 3)),
+            (far_first, (4, 5)),
+            (*order.after(*got), (6, 7)),
+        ]
+    got = exchange(order, [first], [("dp", 2)])
+    yield
+    own = jnp.concatenate([first, *order.after(*got)])
+    got = exchange(order, [own], [("dp", 1)])
+    yield
+    return [(own, (0, 1, 2, 3)), (*order.after(*got), (4, 5, 6, 7))]
 
 
 def columns_first(order, keep, send, seq_masks):
@@ -437,7 +463,7 @@
         yield
         terms = [t[:half] for t in terms] + list(order.after(*got))
     piece = sum_dp_rest(order, summed(terms))
-    return (yield from gather_dp(order, piece))
+    return (yield from gather_dp(order, piece, "zzx split"))
 
 
 def both_first(order, keep, send, seq_masks):
@@ -476,7 +502,7 @@
     yield
     terms = [t[:1] for t in terms] + list(order.after(*got))
     piece = sum_dp_rest(order, summed(terms))
-    return (yield from gather_dp(order, piece))
+    return (yield from gather_dp(order, piece, "zzx"))
 
 
 def halves_first(order, keep, send, seq_masks):
@@ -492,7 +518,7 @@
     yield
     piece = summed([t[:1] for t in terms] + list(order.after(*got)))
     piece = sum_dp_rest(order, piece)
-    return (yield from gather_dp(order, piece))
+    return (yield from gather_dp(order, piece, "zxz"))
 
 
 def token_kernel(dk_ref, dv_ref, wk_ref, wv_ref, small_ref, keep_ref, send_ref, *, n_seq):
@@ -551,14 +577,6 @@
         small = small + order.after(*got)[0]
         step *= 2
     return total, small
-
-
-def finish(chain):
-    try:
-        next(chain)
-    except StopIteration as stop:
-        return stop.value
-    raise ValueError("steps left")
 
 
 VECTORS = ("proj_bias", "ln1_gain", "ln1_bias", "down_bias", "ln2_gain", "ln2_bias")

time: 163 us -> 158 us (0.969)
  waiting for transfers between devices: 54 us -> 50.6 us
  starting transfers between devices: 38.7 us -> 36.8 us
    ppermute x37 -> x35, waiting for transfers between devices: 54 us -> 50.6 us  [swap(): return lax.ppermute(value, axis, [(i, i ^ mask) for i in range(size)])]
    ppermute x37 -> x35, starting transfers between devices: 38.7 us -> 36.8 us  [swap(): return lax.ppermute(value, axis, [(i, i ^ mask) for i in range(size)])]
  transfers between devices with their start and end apart: 37 -> 35, of which waited for: 19 -> 17; matrix products, arithmetic and copies ran while one was open for 4% -> 5% of each run, Pallas kernels for 30% -> 30%
where the time goes in v2:
time: 158 us
  Pallas kernels  60.5 us (38%)
  waiting for transfers between devices  50.6 us (32%)
  starting transfers between devices  36.8 us (23%)
  local copies, waits for them, and re-layouts  4.81 us (3%)
  other arithmetic  2.22 us (1%)
  between operations  1.81 us (1%)
    ppermute x35, waiting for transfers between devices, swap(): return lax.ppermute(value, axis, [(i, i ^ mask) for i in range(size)])  50.6 us
    ppermute x35, starting transfers between devices, swap(): return lax.ppermute(value, axis, [(i, i ^ mask) for i in range(size)])  36.8 us
    pallas_call x2, Pallas kernels, after_attention(): pl.pallas_call(lambda *refs: layer_kernel(*refs, own=own), in_specs=[VMEM...  16.8 us
    pallas_call x1, Pallas kernels, attn_bwd(): pl.pallas_call(lambda *refs: attn_bwd_kernel(*refs, parts=len(keys)), gri...  13.8 us
    pallas_call x1, Pallas kernels, attn_fwd(): pl.pallas_call(lambda *refs: attn_fwd_kernel(*refs, parts=len(keys)), gri...  7.95 us
    pallas_call x3, Pallas kernels, assemble(): pl.pallas_call(lambda *refs: assemble_kernel(*refs, plan=plan, places=pla...  6.31 us
    pallas_call x2, Pallas kernels, half_share_grads(): pl.pallas_call(lambda *refs: half_share_kernel(*refs, plan=plan, low=low)...  4.97 us
    pallas_call x1, Pallas kernels, full_share_grads(): pl.pallas_call(lambda *refs: full_share_kernel(*refs, n_seq=n_seq), in_sp...  4.04 us
  transfers between devices with their start and end apart: 35, of which 17 were waited for; matrix products, arithmetic and copies ran while one was open for 5% of the time, Pallas kernels for 30%

profile of v2, /device:TPU:0, one launch (start us, length us, event | category | flops | bytes accessed | tf_op | source)
XLA Modules:
  0.0 158.2 jit_solution(5807001044850248224)
XLA Ops:
  0.7 3.0 %collective-permute-start = (bf16[256,768]{1,0:T(8,128)(2,1)}, bf16[256,768]{1,0:T(8,128)(2,1)S(1)}, u32[]{:S(2)}, u32[]{:S(2)}) collective-permute-start(bf16[256,768]{1,0:T(8,128)(2,1)} %bitcast.73), channel_id=1, source_target_pairs={{0,2},{1,3},{2,0},{3,1},{4,6},{5,7},{6,4},{7,5},{8,10},{9,11},{10,... | collective-permute-start | bytes 1179656 | tf_op jit(solution)/shard_map/ppermute | solution.py:363
  4.5 0.8 copy.36.refs_2_
  5.3 0.7 constant_dynamic-update-slice_fusion.6
  6.0 0.7 constant_dynamic-update-slice_fusion.5
  6.8 0.7 block_bias.1.refs_1_
  7.6 0.4 copy-done
  8.1 0.4 copy-done.2
  8.5 0.4 copy-done.3
  8.9 1.7 %project_near.1 = (bf16[256,768]{1,0:T(8,128)(2,1)S(1)}, bf16[256,768]{1,0:T(8,128)(2,1)S(1)}, bf16[256,768]{1,0:T(8,128)(2,1)S(1)}, bf16[256,768]{1,0:T(8,128)(2,1)S(1)}, bf16[256,768]{1,0:T(8,128)(2,1)S(1)}) custom-call(bf16[768,768]{1,0:T(8,128)(2,1)S(1)} %copy-done.2, bf16[768,768]{1,0:T(8,128)(2,1)S(1)} %copy-done.3, bf16[768]{0:T(1024)(128)(2,1)S(1)} %copy-done.5, ...), custom_call_target="tpu_custom_call" | custom-call | flops 1100000000 | tf_op jit(solution)/shard_map/project_near/pallas_call | solution.py:92
  10.6 3.3 %collective-permute-done.refs_3_.refs_0_.refs_7_ = bf16[256,768]{1,0:T(8,128)(2,1)S(1)} collective-permute-done((bf16[256,768]{1,0:T(8,128)(2,1)}, bf16[256,768]{1,0:T(8,128)(2,1)S(1)}, u32[]{:S(2)}, u32[]{:S(2)}) %collective-permute-start) | collective-permute-done | bytes 393248 | tf_op jit(solution)/shard_map/ppermute | solution.py:363
  13.9 0.8 project_far.2
  14.7 0.9 collective-permute-done.2.refs_3_.refs_8_
  15.6 0.8 project_far.3
  16.4 8.0 %attn_fwd.1 = (bf16[256,768]{1,0:T(8,128)(2,1)S(1)}, f32[256,768]{1,0:T(8,128)S(1)}) custom-call(bf16[256,768]{1,0:T(8,128)(2,1)S(1)} %get-tuple-element.100.refs_0_, f32[4,1024]{1,0:T(4,128)S(1)} %block_bias.1.refs_1_, bf16[256,768]{1,0:T(8,128)(2,1)S(1)} %get-tuple-element.103.refs_2_.refs_4_, bf16[256,768]{1,0:T(8,128)(2,1)S(1)} %get-tuple-element.104.refs_3_.refs_5_, ...), custom_call_target="tpu_custom_call" | custom-call | flops 11000000512 | tf_op jit(solution)/shard_map/attn_fwd/pallas_call | solution.py:175
  24.4 2.1 %collective-permute-start.3 = (bf16[256,768]{1,0:T(8,128)(2,1)S(1)}, bf16[256,768]{1,0:T(8,128)(2,1)S(1)}, u32[]{:S(2)}, u32[]{:S(2)}) collective-permute-start(bf16[256,768]{1,0:T(8,128)(2,1)S(1)} %get-tuple-element.112.refs_1_.refs_5_), channel_id=1, source_target_pairs={{0,2},{1,3},{2,0},{3,1},{4,6},{5,7},{6,4},{7,5},{8,10},{9,11},{10,... | collective-permute-start | bytes 1179656 | tf_op jit(solution)/shard_map/ppermute | solution.py:363
  26.5 9.1 %layer_own.1 = (bf16[256,768]{1,0:T(8,128)(2,1)S(1)}, bf16[256,3072]{1,0:T(8,128)(2,1)S(1)}, bf16[256,768]{1,0:T(8,128)(2,1)S(1)}, bf16[256,3072]{1,0:T(8,128)(2...) custom-call(bf16[256,768]{1,0:T(8,128)(2,1)S(1)} %bitcast.76, ...), custom_call_target="tpu_custom_call" | custom-call | flops 9900000256 | tf_op jit(solution)/shard_map/layer_own/pallas_call | solution.py:677
  35.9 7.7 %layer_other.1 = (bf16[256,768]{1,0:T(8,128)(2,1)S(1)}, bf16[256,3072]{1,0:T(8,128)(2,1)S(1)}, bf16[256,768]{1,0:T(8,128)(2,1)S(1)}, bf16[256,3072]{1,0:T(8,128)(2,1)S(1)}, bf16[256,768]{1,0:T(8,128)(2,1)S(1)}) custom-call(bf16[256,768]{1,0:T(8,128)(2,1)S(1)} %collective-permute-done.refs_3_.refs_0_.refs_7_, ...), custom_call_target="tpu_custom_call" | custom-call | flops 9900000256 | tf_op jit(solution)/shard_map/layer_other/pallas_call | solution.py:677
  43.6 2.7 %grads_up_proj.1 = (bf16[1,2,4,240,384]{4,3,2,1,0:T(8,128)(2,1)S(1)}, bf16[1,2,4,240,384]{4,3,2,1,0:T(8,128)(2,1)S(1)}) custom-call(s32[4]{0:T(128)S(1)} %pad_add_fusion.refs_0_, bf16[256,768]{1,0:T(8,128)(2,1)S(1)} %get-tuple-element.125.refs_1_, bf16[256,3072]{1,0:T(8,128)(2,1)S(1)} %get-tuple-element.126.refs_2_, ...), custom_call_target="tpu_custom_call" | custom-call | flops 11000000 | tf_op jit(solution)/shard_map/grads_up_proj/pallas_call | solution.py:267
  46.4 2.2 %grads_down.1 = (bf16[1,2,4,192,384]{4,3,2,1,0:T(8,128)(2,1)S(1)}, bf16[1,2,4,192,384]{4,3,2,1,0:T(8,128)(2,1)S(1)}) custom-call(s32[4]{0:T(128)S(1)} %pad_add_fusion.refs_0_, bf16[256,3072]{1,0:T(8,128)(2,1)S(1)} %get-tuple-element.117.refs_1_, bf16[256,768]{1,0:T(8,128)(2,1)S(1)} %get-tuple-element.118.refs_2_, ...), custom_call_target="tpu_custom_call" | custom-call | flops 11000000 | tf_op jit(solution)/shard_map/grads_down/pallas_call | solution.py:267
  48.7 0.6 collective-permute-start.5
  49.2 0.4 collective-permute-done.6
  49.9 1.8 %collective-permute-start.8 = (bf16[4,240,384]{2,1,0:T(8,128)(2,1)S(1)}, bf16[4,240,384]{2,1,0:T(8,128)(2,1)S(1)}, u32[]{:S(2)}, u32[]{:S(2)}) collective-permute-start(bf16[4,240,384]{2,1,0:T(8,128)(2,1)S(1)} %fusion.2), channel_id=1, source_target_pairs={{0,4},{4,0},{8,12},{12,8},{16,20},{20,16},{24,28},{28,24},{1,5},{5... | collective-permute-start | bytes 2211848 | tf_op jit(solution)/shard_map/ppermute | solution.py:363
  51.9 1.9 %collective-permute-start.7 = (bf16[2,2,192,384]{3,2,1,0:T(8,128)(2,1)S(1)}, bf16[2,2,192,384]{3,2,1,0:T(8,128)(2,1)S(1)}, u32[]{:S(2)}, u32[]{:S(2)}) collective-permute-start(bf16[2,2,192,384]{3,2,1,0:T(8,128)(2,1)S(1)} %add_convert_fusion.1), channel_id=1, source_target_pairs={{0,8},{4,12},{8,0},{12,4},{16,24},{20,28},{24,16},{28,20},{1,9},{5... | collective-permute-start | bytes 1769480 | tf_op jit(solution)/shard_map/ppermute | solution.py:363
  53.8 13.8 %attn_bwd.1 = (bf16[256,768]{1,0:T(8,128)(2,1)S(1)}, bf16[1024,768]{1,0:T(8,128)(2,1)S(1)}, bf16[1024,768]{1,0:T(8,128)(2,1)S(1)}) custom-call(bf16[256,768]{1,0:T(8,128)(2,1)S(1)} %get-tuple-element.100.refs_0_, f32[4,1024]{1,0:T(4,128)S(1)} %block_bias.1.refs_1_, bf16[256,768]{1,0:T(8,128)(2,1)S(1)} %get-tuple-element.135.refs_2_, ...), custom_call_target="tpu_custom_call" | custom-call | flops 11000000 | tf_op jit(solution)/shard_map/attn_bwd/pallas_call | solution.py:193
  67.5 4.0 %grads_qkv.1 = (bf16[2,2,4,144,384]{4,3,2,1,0:T(8,128)(2,1)S(1)}, bf16[2,2,4,144,384]{4,3,2,1,0:T(8,128)(2,1)S(1)}, f32[16,768]{1,0:T(8,128)S(1)}) custom-call(s32[4]{0:T(128)S(1)} %pad_add_fusion.refs_0_, bf16[256,768]{1,0:T(8,128)(2,1)S(1)} %get-tuple-element.137.refs_1_, bf16[1024,768]{1,0:T(8,128)(2,1)S(1)} %get-tuple-element.144.refs_2_.refs_0_, ...), custom_call_target="tpu_custom_call" | custom-call | flops 11000000 | tf_op jit(solution)/shard_map/grads_qkv/pallas_call | solution.py:315
  72.0 2.7 %token_terms.1 = (bf16[512,768]{1,0:T(8,128)(2,1)S(1)}, bf16[544,768]{1,0:T(8,128)(2,1)S(1)}) custom-call(bf16[1024,768]{1,0:T(8,128)(2,1)S(1)} %get-tuple-element.144.refs_2_.refs_0_, bf16[1024,768]{1,0:T(8,128)(2,1)S(1)} %get-tuple-element.145.refs_3_.refs_1_, bf16[768,768]{1,0:T(8,128)(2,1)S(1)} %copy-done.2, bf16[768,768]{1,0:T(8,128)(2,1)S(1)} %copy-done.3, ...), custom_call_target="tpu_custom_call" | custom-call | flops 13200000000 | tf_op jit(solution)/shard_map/token_terms/pallas_call | solution.py:539
  74.7 0.5 collective-permute-start.9
  75.2 1.5 collective-permute-start.12
  76.7 0.5 collective-permute-start.15
  77.2 1.6 %collective-permute-start.13 = (bf16[2,2,144,384]{3,2,1,0:T(8,128)(2,1)S(1)}, bf16[2,2,144,384]{3,2,1,0:T(8,128)(2,1)S(1)}, u32[]{:S(2)}, u32[]{:S(2)}) collective-permute-start(bf16[2,2,144,384]{3,2,1,0:T(8,128)(2,1)S(1)} %fusion.4), channel_id=1, source_target_pairs={{0,2},{1,3},{2,0},{3,1},{4,6},{5,7},{6,4},{7,5},{8,10},{9,11},{10,... | collective-permute-start | bytes 1327112 | tf_op jit(solution)/shard_map/ppermute | solution.py:363
  79.0 0.6 collective-permute-start.14
  80.1 6.9 %collective-permute-done.15 = bf16[2,240,384]{2,1,0:T(8,128)(2,1)S(1)} collective-permute-done((bf16[2,240,384]{2,1,0:T(8,128)(2,1)S(1)}, bf16[2,240,384]{2,1,0:T(8,128)(2,1)S(1)}, u32[]{:S(2)}, u32[]{:S(2)}) %collective-permute-start.15) | collective-permute-done | bytes 368672 | tf_op jit(solution)/shard_map/ppermute | solution.py:363
  87.0 2.7 %collective-permute-start.19 = (bf16[1,240,384]{2,1,0:T(8,128)(2,1)S(1)}, bf16[1,240,384]{2,1,0:T(8,128)(2,1)S(1)}, u32[]{:S(2)}, u32[]{:S(2)}) collective-permute-start(bf16[1,240,384]{2,1,0:T(8,128)(2,1)S(1)} %fusion.14), channel_id=1, source_target_pairs={{0,16},{4,20},{8,24},{12,28},{16,0},{20,4},{24,8},{28,12},{1,17},{... | collective-permute-start | bytes 552968 | tf_op jit(solution)/shard_map/ppermute | solution.py:363
  89.7 0.7 collective-permute-done.13
  90.4 3.2 %collective-permute-done.14 = bf16[2,2,144,384]{3,2,1,0:T(8,128)(2,1)S(1)} collective-permute-done((bf16[2,2,144,384]{3,2,1,0:T(8,128)(2,1)S(1)}, bf16[2,2,144,384]{3,2,1,0:T(8,128)(2,1)S(1)}, u32[]{:S(2)}, u32[]{:S(2)}) %collective-permute-start.14) | collective-permute-done | bytes 442400 | tf_op jit(solution)/shard_map/ppermute | solution.py:363
  93.8 1.5 collective-permute-start.17
  95.4 1.6 collective-permute-start.18
  97.0 2.6 %collective-permute-start.16 = (bf16[1,192,384]{2,1,0:T(8,128)(2,1)S(1)}, bf16[1,192,384]{2,1,0:T(8,128)(2,1)S(1)}, u32[]{:S(2)}, u32[]{:S(2)}) collective-permute-start(bf16[1,192,384]{2,1,0:T(8,128)(2,1)S(1)} %fusion.16), channel_id=1, source_target_pairs={{0,16},{4,20},{8,24},{12,28},{16,0},{20,4},{24,8},{28,12},{1,17},{... | collective-permute-start | bytes 442376 | tf_op jit(solution)/shard_map/ppermute | solution.py:363
  99.8 0.4 collective-permute-start.23
  100.5 2.7 %collective-permute-done.18 = bf16[2,144,384]{2,1,0:T(8,128)(2,1)S(1)} collective-permute-done((bf16[2,144,384]{2,1,0:T(8,128)(2,1)S(1)}, bf16[2,144,384]{2,1,0:T(8,128)(2,1)S(1)}, u32[]{:S(2)}, u32[]{:S(2)}) %collective-permute-start.18) | collective-permute-done | bytes 221216 | tf_op jit(solution)/shard_map/ppermute | solution.py:363
  103.2 1.6 %collective-permute-start.20 = (bf16[2,144,384]{2,1,0:T(8,128)(2,1)S(1)}, bf16[2,144,384]{2,1,0:T(8,128)(2,1)S(1)}, u32[]{:S(2)}, u32[]{:S(2)}) collective-permute-start(bf16[2,144,384]{2,1,0:T(8,128)(2,1)S(1)} %fusion.7), channel_id=1, source_target_pairs={{0,8},{4,12},{8,0},{12,4},{16,24},{20,28},{24,16},{28,20},{1,9},{5... | collective-permute-start | bytes 663560 | tf_op jit(solution)/shard_map/ppermute | solution.py:363
  104.9 5.5 %collective-permute-done.16 = bf16[1,192,384]{2,1,0:T(8,128)(2,1)S(1)} collective-permute-done((bf16[1,192,384]{2,1,0:T(8,128)(2,1)S(1)}, bf16[1,192,384]{2,1,0:T(8,128)(2,1)S(1)}, u32[]{:S(2)}, u32[]{:S(2)}) %collective-permute-start.16) | collective-permute-done | bytes 147488 | tf_op jit(solution)/shard_map/ppermute | solution.py:363
  110.6 0.6 collective-permute-start.22
  111.2 4.5 %collective-permute-done.20 = bf16[2,144,384]{2,1,0:T(8,128)(2,1)S(1)} collective-permute-done((bf16[2,144,384]{2,1,0:T(8,128)(2,1)S(1)}, bf16[2,144,384]{2,1,0:T(8,128)(2,1)S(1)}, u32[]{:S(2)}, u32[]{:S(2)}) %collective-permute-start.20) | collective-permute-done | bytes 221216 | tf_op jit(solution)/shard_map/ppermute | solution.py:363
  115.9 1.6 %collective-permute-done.23 = bf16[1,240,384]{2,1,0:T(8,128)(2,1)S(1)} collective-permute-done((bf16[1,240,384]{2,1,0:T(8,128)(2,1)S(1)}, bf16[1,240,384]{2,1,0:T(8,128)(2,1)S(1)}, u32[]{:S(2)}, u32[]{:S(2)}) %collective-permute-start.23) | collective-permute-done | bytes 184352 | tf_op jit(solution)/shard_map/ppermute | solution.py:363
  117.5 1.2 collective-permute-start.29
  118.7 0.6 collective-permute-start.30
  119.3 5.2 %collective-permute-done.21 = bf16[1,144,384]{2,1,0:T(8,128)(2,1)S(1)} collective-permute-done((bf16[1,144,384]{2,1,0:T(8,128)(2,1)S(1)}, bf16[1,144,384]{2,1,0:T(8,128)(2,1)S(1)}, u32[]{:S(2)}, u32[]{:S(2)}) %collective-permute-start.21) | collective-permute-done | bytes 110624 | tf_op jit(solution)/shard_map/ppermute | solution.py:363
  124.8 0.6 collective-permute-start.28
  125.4 3.1 %collective-permute-start.25 = (f32[16,768]{1,0:T(8,128)S(1)}, f32[16,768]{1,0:T(8,128)S(1)}, u32[]{:S(2)}, u32[]{:S(2)}) collective-permute-start(f32[16,768]{1,0:T(8,128)S(1)} %add.343), channel_id=1, source_target_pairs={{0,8},{4,12},{8,0},{12,4},{16,24},{20,28},{24,16},{28,20},{1,9},{5... | collective-permute-start | bytes 147464 | tf_op jit(solution)/shard_map/ppermute | solution.py:363
  128.5 5.3 %collective-permute-done.25 = f32[16,768]{1,0:T(8,128)S(1)} collective-permute-done((f32[16,768]{1,0:T(8,128)S(1)}, f32[16,768]{1,0:T(8,128)S(1)}, u32[]{:S(2)}, u32[]{:S(2)}) %collective-permute-start.25) | collective-permute-done | bytes 49184 | tf_op jit(solution)/shard_map/ppermute | solution.py:363
  134.0 2.1 %collective-permute-start.33 = (bf16[4,192,384]{2,1,0:T(8,128)(2,1)S(1)}, bf16[4,192,384]{2,1,0:T(8,128)(2,1)S(1)}, u32[]{:S(2)}, u32[]{:S(2)}) collective-permute-start(bf16[4,192,384]{2,1,0:T(8,128)(2,1)S(1)} %pad_maximum_fusion.refs_1_), channel_id=1, source_target_pairs={{0,8},{4,12},{8,0},{12,4},{16,24},{20,28},{24,16},{28,20},{1,9},{5... | collective-permute-start | bytes 1769480 | tf_op jit(solution)/shard_map/ppermute | solution.py:363
  136.0 2.0 %collective-permute-start.34 = (f32[16,768]{1,0:T(8,128)S(1)}, f32[16,768]{1,0:T(8,128)S(1)}, u32[]{:S(2)}, u32[]{:S(2)}) collective-permute-start(f32[16,768]{1,0:T(8,128)S(1)} %add.345), channel_id=1, source_target_pairs={{0,16},{4,20},{8,24},{12,28},{16,0},{20,4},{24,8},{28,12},{1,17},{... | collective-permute-start | bytes 147464 | tf_op jit(solution)/shard_map/ppermute | solution.py:363
  138.1 0.5 collective-permute-start.32
  138.6 4.6 %collective-permute-done.27 = bf16[2,144,384]{2,1,0:T(8,128)(2,1)S(1)} collective-permute-done((bf16[2,144,384]{2,1,0:T(8,128)(2,1)S(1)}, bf16[2,144,384]{2,1,0:T(8,128)(2,1)S(1)}, u32[]{:S(2)}, u32[]{:S(2)}) %collective-permute-start.27) | collective-permute-done | bytes 221216 | tf_op jit(solution)/shard_map/ppermute | solution.py:363
  143.3 0.6 collective-permute-start.31
  143.9 1.4 fusion.1
  145.4 4.2 %collective-permute-done.32.refs_4_ = bf16[2,240,384]{2,1,0:T(8,128)(2,1)S(1)} collective-permute-done((bf16[2,240,384]{2,1,0:T(8,128)(2,1)S(1)}, bf16[2,240,384]{2,1,0:T(8,128)(2,1)S(1)}, u32[]{:S(2)}, u32[]{:S(2)}) %collective-permute-start.32) | collective-permute-done | bytes 368672 | tf_op jit(solution)/shard_map/ppermute | solution.py:363
  149.6 2.4 %assemble_U.1 = (f32[192,3072]{1,0:T(8,128)}, f32[192,768]{1,0:T(8,128)}) custom-call(s32[4]{0:T(128)S(1)} %pad_add_fusion.refs_0_, bf16[2,240,384]{2,1,0:T(8,128)(2,1)S(1)} %pad_maximum_fusion.3.refs_1_, bf16[2,240,384]{2,1,0:T(8,128)(2,1)S(1)} %collective-permute-done.29.refs_2_, bf16[2,240,384]{2,1,0:T(8,128)(2,1)S(1)} %collective-permute-done.30.refs_3_, ...), custom_call_target="tpu_custom_call" | custom-call | flops 11000000 | tf_op jit(solution)/shard_map/assemble_U/pallas_call | solution.py:350
  152.0 0.6 slice.395
  152.6 0.7 slice_reduce_fusion
  153.3 2.1 %assemble_D.1 = f32[768,768]{1,0:T(8,128)} custom-call(s32[4]{0:T(128)S(1)} %pad_add_fusion.refs_0_, bf16[4,192,384]{2,1,0:T(8,128)(2,1)S(1)} %pad_maximum_fusion.refs_1_, bf16[4,192,384]{2,1,0:T(8,128)(2,1)S(1)} %collective-permute-done.33.refs_2_), custom_call_target="tpu_custom_call" | custom-call | flops 11000000 | tf_op jit(solution)/shard_map/assemble_D/pallas_call | solution.py:350
  155.4 0.9 collective-permute-done.31.refs_2_
  156.3 1.9 %assemble_C.1 = (f32[192,768]{1,0:T(8,128)}, f32[192,768]{1,0:T(8,128)}, f32[192,768]{1,0:T(8,128)}) custom-call(s32[4]{0:T(128)S(1)} %pad_add_fusion.refs_0_, bf16[4,144,384]{2,1,0:T(8,128)(2,1)S(1)} %pad_maximum_fusion.2.refs_1_, bf16[4,144,384]{2,1,0:T(8,128)(2,1)S(1)} %collective-permute-done.31.refs_2_), custom_call_target="tpu_custom_call" | custom-call | flops 11000000 | tf_op jit(solution)/shard_map/assemble_C/pallas_call | solution.py:350
  (96 shorter events, 4.0 us)
Async XLA Ops:
  0.7 13.2 %collective-permute-start = (bf16[256,768]{1,0:T(8,128)(2,1)}, bf16[256,768]{1,0:T(8,128)(2,1)S(1)}, u32[]{:S(2)}, u32[]{:S(2)}) collective-permute-start(bf16[256,768]{1,0:T(8,128)(2,1)} %bitcast.73), channel_id=1, source_target_pairs={{0,2},{1,3},{2,0},{3,1},{4,6},{5,7},{6,4},{7,5},{8,10},{9,11},{10,... | collective-permute-start | bytes 1179656 | tf_op jit(solution)/shard_map/ppermute | solution.py:363
  3.7 3.9 %collective-permute-start.1 = (bf16[256,768]{1,0:T(8,128)(2,1)}, bf16[256,768]{1,0:T(8,128)(2,1)S(1)}, u32[]{:S(2)}, u32[]{:S(2)}) collective-permute-start(bf16[256,768]{1,0:T(8,128)(2,1)} %bitcast.74), channel_id=1, source_target_pairs={{0,1},{1,0},{2,3},{3,2},{4,5},{5,4},{6,7},{7,6},{8,9},{9,8},{10,11... | collective-permute-start | bytes 1179656 | tf_op jit(solution)/shard_map/ppermute | solution.py:363
  3.7 32.2 %collective-permute-start.4 = (bf16[256,768]{1,0:T(8,128)(2,1)}, bf16[256,768]{1,0:T(8,128)(2,1)S(1)}, u32[]{:S(2)}, u32[]{:S(2)}) collective-permute-start(bf16[256,768]{1,0:T(8,128)(2,1)} %bitcast.86), channel_id=1, source_target_pairs={{0,2},{1,3},{2,0},{3,1},{4,6},{5,7},{6,4},{7,5},{8,10},{9,11},{10,... | collective-permute-start | bytes 1179656 | tf_op jit(solution)/shard_map/ppermute | solution.py:363
  6.7 0.8 copy-start.9
  6.7 0.8 copy-start.10
  6.7 1.3 copy-start
  6.7 1.4 copy-start.1
  6.7 1.8 %copy-start.2 = (bf16[768,768]{1,0:T(8,128)(2,1)S(1)}, bf16[768,768]{1,0:T(8,128)(2,1)}, u32[]{:S(2)}) copy-start(bf16[768,768]{1,0:T(8,128)(2,1)} %refs_2_.8) | copy-start | bytes 3538948
  6.7 2.1 %copy-start.3 = (bf16[768,768]{1,0:T(8,128)(2,1)S(1)}, bf16[768,768]{1,0:T(8,128)(2,1)}, u32[]{:S(2)}) copy-start(bf16[768,768]{1,0:T(8,128)(2,1)} %refs_3_.5) | copy-start | bytes 3538948
  6.8 2.1 %copy-start.4 = (bf16[768]{0:T(1024)(128)(2,1)S(1)}, bf16[768]{0:T(1024)(128)(2,1)}, u32[]{:S(2)}) copy-start(bf16[768]{0:T(1024)(128)(2,1)} %refs_6_.1) | copy-start | bytes 4612
  6.8 2.1 %copy-start.5 = (bf16[768]{0:T(1024)(128)(2,1)S(1)}, bf16[768]{0:T(1024)(128)(2,1)}, u32[]{:S(2)}) copy-start(bf16[768]{0:T(1024)(128)(2,1)} %refs_2_.7) | copy-start | bytes 4612
  7.5 6.3 %copy-start.11 = (bf16[768]{0:T(1024)(128)(2,1)S(1)}, bf16[768]{0:T(1024)(128)(2,1)}, u32[]{:S(2)}) copy-start(bf16[768]{0:T(1024)(128)(2,1)} %param.33) | copy-start | bytes 4612
  7.6 6.3 %copy-start.12 = (bf16[768]{0:T(1024)(128)(2,1)S(1)}, bf16[768]{0:T(1024)(128)(2,1)}, u32[]{:S(2)}) copy-start(bf16[768]{0:T(1024)(128)(2,1)} %param.34) | copy-start | bytes 4612
  7.6 6.3 %copy-start.8 = (bf16[3072]{0:T(1024)(128)(2,1)S(1)}, bf16[3072]{0:T(1024)(128)(2,1)}, u32[]{:S(2)}) copy-start(bf16[3072]{0:T(1024)(128)(2,1)} %param.30) | copy-start | bytes 18436
  13.8 1.7 %collective-permute-start.2 = (bf16[256,768]{1,0:T(8,128)(2,1)S(1)}, bf16[256,768]{1,0:T(8,128)(2,1)S(1)}, u32[]{:S(2)}, u32[]{:S(2)}) collective-permute-start(bf16[256,768]{1,0:T(8,128)(2,1)S(1)} %collective-permute-done.refs_3_.refs_0_.refs_7_), channel_id=1, source_target_pairs={{0,1},{1,0},{2,3},{3,2},{4,5},{5,4},{6,7},{7,6},{8,9},{9,8},{10,11... | collective-permute-start | bytes 1179656 | tf_op jit(solution)/shard_map/ppermute | solution.py:363
  15.6 10.9 %slice-start = ((s8[4718592]{0:T(1024)(128)(4,1)}), s8[4194304]{0:T(1024)(128)(4,1)S(1)}, s32[]{:S(2)}) async-start(s8[4718592]{0:T(1024)(128)(4,1)} %bitcast.82), calls=%async_computation | async-start | bytes 8388608
  15.6 10.9 %slice-start.2 = ((s8[4718592]{0:T(1024)(128)(4,1)}), s8[4194304]{0:T(1024)(128)(4,1)S(1)}, s32[]{:S(2)}) async-start(s8[4718592]{0:T(1024)(128)(4,1)} %bitcast.84), calls=%async_computation.2 | async-start | bytes 8388608
  16.4 10.1 %slice-start.1 = ((s8[4718592]{0:T(1024)(128)(4,1)}), s8[524288]{0:T(1024)(128)(4,1)S(1)}, s32[]{:S(2)}) async-start(s8[4718592]{0:T(1024)(128)(4,1)} %bitcast.82), calls=%async_computation.1 | async-start | bytes 1048576
  16.4 10.1 %slice-start.3 = ((s8[4718592]{0:T(1024)(128)(4,1)}), s8[524288]{0:T(1024)(128)(4,1)S(1)}, s32[]{:S(2)}) async-start(s8[4718592]{0:T(1024)(128)(4,1)} %bitcast.84), calls=%async_computation.3 | async-start | bytes 1048576
  16.4 10.1 %copy-start.6 = (bf16[768,768]{1,0:T(8,128)(2,1)S(1)}, bf16[768,768]{1,0:T(8,128)(2,1)}, u32[]{:S(2)}) copy-start(bf16[768,768]{1,0:T(8,128)(2,1)} %refs_3_.4) | copy-start | bytes 3538948
  16.4 10.1 %copy-start.7 = (bf16[1,256,768]{2,1,0:T(8,128)(2,1)S(1)}, bf16[1,256,768]{2,1,0:T(8,128)(2,1)}, u32[]{:S(2)}) copy-start(bf16[1,256,768]{2,1,0:T(8,128)(2,1)} %param.37) | copy-start | bytes 1179652
  24.4 11.5 %collective-permute-start.3 = (bf16[256,768]{1,0:T(8,128)(2,1)S(1)}, bf16[256,768]{1,0:T(8,128)(2,1)S(1)}, u32[]{:S(2)}, u32[]{:S(2)}) collective-permute-start(bf16[256,768]{1,0:T(8,128)(2,1)S(1)} %get-tuple-element.112.refs_1_.refs_5_), channel_id=1, source_target_pairs={{0,2},{1,3},{2,0},{3,1},{4,6},{5,7},{6,4},{7,5},{8,10},{9,11},{10,... | collective-permute-start | bytes 1179656 | tf_op jit(solution)/shard_map/ppermute | solution.py:363
  46.4 3.3 %collective-permute-start.6 = (bf16[1,2,4,240,384]{4,3,2,1,0:T(8,128)(2,1)S(1)}, bf16[1,2,4,240,384]{4,3,2,1,0:T(8,128)(2,1)S(1)}, u32[]{:S(2)}, u32[]{:S(2)}) collective-permute-start(bf16[1,2,4,240,384]{4,3,2,1,0:T(8,128)(2,1)S(1)} %get-tuple-element.132), channel_id=1, source_target_pairs={{0,1},{1,0},{2,3},{3,2},{4,5},{5,4},{6,7},{7,6},{8,9},{9,8},{10,11... | collective-permute-start | bytes 4423688 | tf_op jit(solution)/shard_map/ppermute | solution.py:363
  48.7 3.0 %collective-permute-start.5 = (bf16[1,2,4,192,384]{4,3,2,1,0:T(8,128)(2,1)S(1)}, bf16[1,2,4,192,384]{4,3,2,1,0:T(8,128)(2,1)S(1)}, u32[]{:S(2)}, u32[]{:S(2)}) collective-permute-start(bf16[1,2,4,192,384]{4,3,2,1,0:T(8,128)(2,1)S(1)} %get-tuple-element.124), channel_id=1, source_target_pairs={{0,1},{1,0},{2,3},{3,2},{4,5},{5,4},{6,7},{7,6},{8,9},{9,8},{10,11... | collective-permute-start | bytes 3538952 | tf_op jit(solution)/shard_map/ppermute | solution.py:363
  49.9 21.8 %collective-permute-start.8 = (bf16[4,240,384]{2,1,0:T(8,128)(2,1)S(1)}, bf16[4,240,384]{2,1,0:T(8,128)(2,1)S(1)}, u32[]{:S(2)}, u32[]{:S(2)}) collective-permute-start(bf16[4,240,384]{2,1,0:T(8,128)(2,1)S(1)} %fusion.2), channel_id=1, source_target_pairs={{0,4},{4,0},{8,12},{12,8},{16,20},{20,16},{24,28},{28,24},{1,5},{5... | collective-permute-start | bytes 2211848 | tf_op jit(solution)/shard_map/ppermute | solution.py:363
  51.9 20.0 %collective-permute-start.7 = (bf16[2,2,192,384]{3,2,1,0:T(8,128)(2,1)S(1)}, bf16[2,2,192,384]{3,2,1,0:T(8,128)(2,1)S(1)}, u32[]{:S(2)}, u32[]{:S(2)}) collective-permute-start(bf16[2,2,192,384]{3,2,1,0:T(8,128)(2,1)S(1)} %add_convert_fusion.1), channel_id=1, source_target_pairs={{0,8},{4,12},{8,0},{12,4},{16,24},{20,28},{24,16},{28,20},{1,9},{5... | collective-permute-start | bytes 1769480 | tf_op jit(solution)/shard_map/ppermute | solution.py:363
  71.6 5.5 %collective-permute-start.10 = (bf16[2,2,4,144,384]{4,3,2,1,0:T(8,128)(2,1)S(1)}, bf16[2,2,4,144,384]{4,3,2,1,0:T(8,128)(2,1)S(1)}, u32[]{:S(2)}, u32[]{:S(2)}) collective-permute-start(bf16[2,2,4,144,384]{4,3,2,1,0:T(8,128)(2,1)S(1)} %get-tuple-element.141), channel_id=1, source_target_pairs={{0,1},{1,0},{2,3},{3,2},{4,5},{5,4},{6,7},{7,6},{8,9},{9,8},{10,11... | collective-permute-start | bytes 5308424 | tf_op jit(solution)/shard_map/ppermute | solution.py:363
  74.7 4.9 %collective-permute-start.9 = (bf16[544,768]{1,0:T(8,128)(2,1)S(1)}, bf16[544,768]{1,0:T(8,128)(2,1)S(1)}, u32[]{:S(2)}, u32[]{:S(2)}) collective-permute-start(bf16[544,768]{1,0:T(8,128)(2,1)S(1)} %get-tuple-element.148), channel_id=1, source_target_pairs={{0,1},{1,0},{2,3},{3,2},{4,5},{5,4},{6,7},{7,6},{8,9},{9,8},{10,11... | collective-permute-start | bytes 2506760 | tf_op jit(solution)/shard_map/ppermute | solution.py:363
  75.2 21.8 %collective-permute-start.12 = (bf16[2,192,384]{2,1,0:T(8,128)(2,1)S(1)}, bf16[2,192,384]{2,1,0:T(8,128)(2,1)S(1)}, u32[]{:S(2)}, u32[]{:S(2)}) collective-permute-start(bf16[2,192,384]{2,1,0:T(8,128)(2,1)S(1)} %fusion.15), channel_id=1, source_target_pairs={{0,4},{4,0},{8,12},{12,8},{16,20},{20,16},{24,28},{28,24},{1,5},{5... | collective-permute-start | bytes 884744 | tf_op jit(solution)/shard_map/ppermute | solution.py:363
  76.7 10.3 %collective-permute-start.15 = (bf16[2,240,384]{2,1,0:T(8,128)(2,1)S(1)}, bf16[2,240,384]{2,1,0:T(8,128)(2,1)S(1)}, u32[]{:S(2)}, u32[]{:S(2)}) collective-permute-start(bf16[2,240,384]{2,1,0:T(8,128)(2,1)S(1)} %fusion.3), channel_id=1, source_target_pairs={{0,8},{4,12},{8,0},{12,4},{16,24},{20,28},{24,16},{28,20},{1,9},{5... | collective-permute-start | bytes 1105928 | tf_op jit(solution)/shard_map/ppermute | solution.py:363
  77.2 13.2 %collective-permute-start.13 = (bf16[2,2,144,384]{3,2,1,0:T(8,128)(2,1)S(1)}, bf16[2,2,144,384]{3,2,1,0:T(8,128)(2,1)S(1)}, u32[]{:S(2)}, u32[]{:S(2)}) collective-permute-start(bf16[2,2,144,384]{3,2,1,0:T(8,128)(2,1)S(1)} %fusion.4), channel_id=1, source_target_pairs={{0,2},{1,3},{2,0},{3,1},{4,6},{5,7},{6,4},{7,5},{8,10},{9,11},{10,... | collective-permute-start | bytes 1327112 | tf_op jit(solution)/shard_map/ppermute | solution.py:363
  79.0 14.7 %collective-permute-start.14 = (bf16[2,2,144,384]{3,2,1,0:T(8,128)(2,1)S(1)}, bf16[2,2,144,384]{3,2,1,0:T(8,128)(2,1)S(1)}, u32[]{:S(2)}, u32[]{:S(2)}) collective-permute-start(bf16[2,2,144,384]{3,2,1,0:T(8,128)(2,1)S(1)} %fusion.5), channel_id=1, source_target_pairs={{0,4},{4,0},{8,12},{12,8},{16,20},{20,16},{24,28},{28,24},{1,5},{5... | collective-permute-start | bytes 1327112 | tf_op jit(solution)/shard_map/ppermute | solution.py:363
  79.7 30.8 %collective-permute-start.11 = (bf16[288,768]{1,0:T(8,128)(2,1)S(1)}, bf16[288,768]{1,0:T(8,128)(2,1)S(1)}, u32[]{:S(2)}, u32[]{:S(2)}) collective-permute-start(bf16[288,768]{1,0:T(8,128)(2,1)S(1)} %pad_maximum_fusion.1), channel_id=1, source_target_pairs={{0,2},{1,3},{2,0},{3,1},{4,6},{5,7},{6,4},{7,5},{8,10},{9,11},{10,... | collective-permute-start | bytes 1327112 | tf_op jit(solution)/shard_map/ppermute | solution.py:363
  87.0 12.6 %collective-permute-start.19 = (bf16[1,240,384]{2,1,0:T(8,128)(2,1)S(1)}, bf16[1,240,384]{2,1,0:T(8,128)(2,1)S(1)}, u32[]{:S(2)}, u32[]{:S(2)}) collective-permute-start(bf16[1,240,384]{2,1,0:T(8,128)(2,1)S(1)} %fusion.14), channel_id=1, source_target_pairs={{0,16},{4,20},{8,24},{12,28},{16,0},{20,4},{24,8},{28,12},{1,17},{... | collective-permute-start | bytes 552968 | tf_op jit(solution)/shard_map/ppermute | solution.py:363
  93.8 6.6 %collective-permute-start.17 = (bf16[2,144,384]{2,1,0:T(8,128)(2,1)S(1)}, bf16[2,144,384]{2,1,0:T(8,128)(2,1)S(1)}, u32[]{:S(2)}, u32[]{:S(2)}) collective-permute-start(bf16[2,144,384]{2,1,0:T(8,128)(2,1)S(1)} %get-tuple-element.192), channel_id=1, source_target_pairs={{0,4},{4,0},{8,12},{12,8},{16,20},{20,16},{24,28},{28,24},{1,5},{5... | collective-permute-start | bytes 663560 | tf_op jit(solution)/shard_map/ppermute | solution.py:363
  95.4 7.8 %collective-permute-start.18 = (bf16[2,144,384]{2,1,0:T(8,128)(2,1)S(1)}, bf16[2,144,384]{2,1,0:T(8,128)(2,1)S(1)}, u32[]{:S(2)}, u32[]{:S(2)}) collective-permute-start(bf16[2,144,384]{2,1,0:T(8,128)(2,1)S(1)} %get-tuple-element.191), channel_id=1, source_target_pairs={{0,2},{1,3},{2,0},{3,1},{4,6},{5,7},{6,4},{7,5},{8,10},{9,11},{10,... | collective-permute-start | bytes 663560 | tf_op jit(solution)/shard_map/ppermute | solution.py:363
  97.0 13.4 %collective-permute-start.16 = (bf16[1,192,384]{2,1,0:T(8,128)(2,1)S(1)}, bf16[1,192,384]{2,1,0:T(8,128)(2,1)S(1)}, u32[]{:S(2)}, u32[]{:S(2)}) collective-permute-start(bf16[1,192,384]{2,1,0:T(8,128)(2,1)S(1)} %fusion.16), channel_id=1, source_target_pairs={{0,16},{4,20},{8,24},{12,28},{16,0},{20,4},{24,8},{28,12},{1,17},{... | collective-permute-start | bytes 442376 | tf_op jit(solution)/shard_map/ppermute | solution.py:363
  99.8 17.7 %collective-permute-start.23 = (bf16[1,240,384]{2,1,0:T(8,128)(2,1)S(1)}, bf16[1,240,384]{2,1,0:T(8,128)(2,1)S(1)}, u32[]{:S(2)}, u32[]{:S(2)}) collective-permute-start(bf16[1,240,384]{2,1,0:T(8,128)(2,1)S(1)} %fusion.12), channel_id=1, source_target_pairs={{0,16},{4,20},{8,24},{12,28},{16,0},{20,4},{24,8},{28,12},{1,17},{... | collective-permute-start | bytes 552968 | tf_op jit(solution)/shard_map/ppermute | solution.py:363
  103.2 12.5 %collective-permute-start.20 = (bf16[2,144,384]{2,1,0:T(8,128)(2,1)S(1)}, bf16[2,144,384]{2,1,0:T(8,128)(2,1)S(1)}, u32[]{:S(2)}, u32[]{:S(2)}) collective-permute-start(bf16[2,144,384]{2,1,0:T(8,128)(2,1)S(1)} %fusion.7), channel_id=1, source_target_pairs={{0,8},{4,12},{8,0},{12,4},{16,24},{20,28},{24,16},{28,20},{1,9},{5... | collective-permute-start | bytes 663560 | tf_op jit(solution)/shard_map/ppermute | solution.py:363
  110.5 14.3 %collective-permute-start.26 = (bf16[1,192,384]{2,1,0:T(8,128)(2,1)S(1)}, bf16[1,192,384]{2,1,0:T(8,128)(2,1)S(1)}, u32[]{:S(2)}, u32[]{:S(2)}) collective-permute-start(bf16[1,192,384]{2,1,0:T(8,128)(2,1)S(1)} %fusion.18), channel_id=1, source_target_pairs={{0,16},{4,20},{8,24},{12,28},{16,0},{20,4},{24,8},{28,12},{1,17},{... | collective-permute-start | bytes 442376 | tf_op jit(solution)/shard_map/ppermute | solution.py:363
  110.6 8.7 %collective-permute-start.22 = (f32[16,768]{1,0:T(8,128)S(1)}, f32[16,768]{1,0:T(8,128)S(1)}, u32[]{:S(2)}, u32[]{:S(2)}) collective-permute-start(f32[16,768]{1,0:T(8,128)S(1)} %fusion.31), channel_id=1, source_target_pairs={{0,4},{4,0},{8,12},{12,8},{16,20},{20,16},{24,28},{28,24},{1,5},{5... | collective-permute-start | bytes 147464 | tf_op jit(solution)/shard_map/ppermute | solution.py:363
  115.8 8.8 %collective-permute-start.21 = (bf16[1,144,384]{2,1,0:T(8,128)(2,1)S(1)}, bf16[1,144,384]{2,1,0:T(8,128)(2,1)S(1)}, u32[]{:S(2)}, u32[]{:S(2)}) collective-permute-start(bf16[1,144,384]{2,1,0:T(8,128)(2,1)S(1)} %fusion.21), channel_id=1, source_target_pairs={{0,16},{4,20},{8,24},{12,28},{16,0},{20,4},{24,8},{28,12},{1,17},{... | collective-permute-start | bytes 331784 | tf_op jit(solution)/shard_map/ppermute | solution.py:363
  117.5 16.4 %collective-permute-start.29 = (bf16[2,240,384]{2,1,0:T(8,128)(2,1)S(1)}, bf16[2,240,384]{2,1,0:T(8,128)(2,1)S(1)}, u32[]{:S(2)}, u32[]{:S(2)}) collective-permute-start(bf16[2,240,384]{2,1,0:T(8,128)(2,1)S(1)} %pad_maximum_fusion.3.refs_1_), channel_id=1, source_target_pairs={{0,8},{4,12},{8,0},{12,4},{16,24},{20,28},{24,16},{28,20},{1,9},{5... | collective-permute-start | bytes 1105928 | tf_op jit(solution)/shard_map/ppermute | solution.py:363
  118.7 15.1 %collective-permute-start.30 = (bf16[2,240,384]{2,1,0:T(8,128)(2,1)S(1)}, bf16[2,240,384]{2,1,0:T(8,128)(2,1)S(1)}, u32[]{:S(2)}, u32[]{:S(2)}) collective-permute-start(bf16[2,240,384]{2,1,0:T(8,128)(2,1)S(1)} %pad_maximum_fusion.3.refs_1_), channel_id=1, source_target_pairs={{0,4},{4,0},{8,12},{12,8},{16,20},{20,16},{24,28},{28,24},{1,5},{5... | collective-permute-start | bytes 1105928 | tf_op jit(solution)/shard_map/ppermute | solution.py:363
  124.6 9.1 %collective-permute-start.24 = (bf16[1,144,384]{2,1,0:T(8,128)(2,1)S(1)}, bf16[1,144,384]{2,1,0:T(8,128)(2,1)S(1)}, u32[]{:S(2)}, u32[]{:S(2)}) collective-permute-start(bf16[1,144,384]{2,1,0:T(8,128)(2,1)S(1)} %fusion.25), channel_id=1, source_target_pairs={{0,16},{4,20},{8,24},{12,28},{16,0},{20,4},{24,8},{28,12},{1,17},{... | collective-permute-start | bytes 331784 | tf_op jit(solution)/shard_map/ppermute | solution.py:363
  124.8 9.1 %collective-permute-start.28 = (bf16[2,192,384]{2,1,0:T(8,128)(2,1)S(1)}, bf16[2,192,384]{2,1,0:T(8,128)(2,1)S(1)}, u32[]{:S(2)}, u32[]{:S(2)}) collective-permute-start(bf16[2,192,384]{2,1,0:T(8,128)(2,1)S(1)} %pad_maximum_fusion.4), channel_id=1, source_target_pairs={{0,4},{4,0},{8,12},{12,8},{16,20},{20,16},{24,28},{28,24},{1,5},{5... | collective-permute-start | bytes 884744 | tf_op jit(solution)/shard_map/ppermute | solution.py:363
  125.4 8.4 %collective-permute-start.25 = (f32[16,768]{1,0:T(8,128)S(1)}, f32[16,768]{1,0:T(8,128)S(1)}, u32[]{:S(2)}, u32[]{:S(2)}) collective-permute-start(f32[16,768]{1,0:T(8,128)S(1)} %add.343), channel_id=1, source_target_pairs={{0,8},{4,12},{8,0},{12,4},{16,24},{20,28},{24,16},{28,20},{1,9},{5... | collective-permute-start | bytes 147464 | tf_op jit(solution)/shard_map/ppermute | solution.py:363
  133.8 9.5 %collective-permute-start.27 = (bf16[2,144,384]{2,1,0:T(8,128)(2,1)S(1)}, bf16[2,144,384]{2,1,0:T(8,128)(2,1)S(1)}, u32[]{:S(2)}, u32[]{:S(2)}) collective-permute-start(bf16[2,144,384]{2,1,0:T(8,128)(2,1)S(1)} %pad_maximum_fusion.5), channel_id=1, source_target_pairs={{0,8},{4,12},{8,0},{12,4},{16,24},{20,28},{24,16},{28,20},{1,9},{5... | collective-permute-start | bytes 663560 | tf_op jit(solution)/shard_map/ppermute | solution.py:363
  134.0 19.3 %collective-permute-start.33 = (bf16[4,192,384]{2,1,0:T(8,128)(2,1)S(1)}, bf16[4,192,384]{2,1,0:T(8,128)(2,1)S(1)}, u32[]{:S(2)}, u32[]{:S(2)}) collective-permute-start(bf16[4,192,384]{2,1,0:T(8,128)(2,1)S(1)} %pad_maximum_fusion.refs_1_), channel_id=1, source_target_pairs={{0,8},{4,12},{8,0},{12,4},{16,24},{20,28},{24,16},{28,20},{1,9},{5... | collective-permute-start | bytes 1769480 | tf_op jit(solution)/shard_map/ppermute | solution.py:363
  136.0 15.9 %collective-permute-start.34 = (f32[16,768]{1,0:T(8,128)S(1)}, f32[16,768]{1,0:T(8,128)S(1)}, u32[]{:S(2)}, u32[]{:S(2)}) collective-permute-start(f32[16,768]{1,0:T(8,128)S(1)} %add.345), channel_id=1, source_target_pairs={{0,16},{4,20},{8,24},{12,28},{16,0},{20,4},{24,8},{28,12},{1,17},{... | collective-permute-start | bytes 147464 | tf_op jit(solution)/shard_map/ppermute | solution.py:363
  138.1 11.5 %collective-permute-start.32 = (bf16[2,240,384]{2,1,0:T(8,128)(2,1)S(1)}, bf16[2,240,384]{2,1,0:T(8,128)(2,1)S(1)}, u32[]{:S(2)}, u32[]{:S(2)}) collective-permute-start(bf16[2,240,384]{2,1,0:T(8,128)(2,1)S(1)} %collective-permute-done.29.refs_2_), channel_id=1, source_target_pairs={{0,4},{4,0},{8,12},{12,8},{16,20},{20,16},{24,28},{28,24},{1,5},{5... | collective-permute-start | bytes 1105928 | tf_op jit(solution)/shard_map/ppermute | solution.py:363
  143.3 13.0 %collective-permute-start.31 = (bf16[4,144,384]{2,1,0:T(8,128)(2,1)S(1)}, bf16[4,144,384]{2,1,0:T(8,128)(2,1)S(1)}, u32[]{:S(2)}, u32[]{:S(2)}) collective-permute-start(bf16[4,144,384]{2,1,0:T(8,128)(2,1)S(1)} %pad_maximum_fusion.2.refs_1_), channel_id=1, source_target_pairs={{0,4},{4,0},{8,12},{12,8},{16,20},{20,16},{24,28},{28,24},{1,5},{5... | collective-permute-start | bytes 1327112 | tf_op jit(solution)/shard_map/ppermute | solution.py:363

commit v3 on v2

--- a/solution.py
+++ b/solution.py
@@ -370,7 +370,7 @@
     return total.astype(BF16)
 
 
-STEPS = "TUCDUCDTCUTCDTCUDCUTDC"
+STEPS = "TUCDUCDTCUTCDCUDTCUTDC"
 
 
 class Order:

time: 158 us -> 157 us (level)
  starting transfers between devices: 36.8 us -> 32.9 us
  waiting for transfers between devices: 50.6 us -> 53.5 us
    ppermute x35, starting transfers between devices: 36.8 us -> 32.9 us  [swap(): return lax.ppermute(value, axis, [(i, i ^ mask) for i in range(size)])]
    ppermute x35, waiting for transfers between devices: 50.6 us -> 53.5 us  [swap(): return lax.ppermute(value, axis, [(i, i ^ mask) for i in range(size)])]
  transfers between devices with their start and end apart: 35 -> 35, of which waited for: 17 -> 18; matrix products, arithmetic and copies ran while one was open for 5% -> 5% of each run, Pallas kernels for 30% -> 31%
where the time goes in v3:
time: 157 us
  Pallas kernels  60.5 us (39%)
  waiting for transfers between devices  53.5 us (34%)
  starting transfers between devices  32.9 us (21%)
  local copies, waits for them, and re-layouts  4.81 us (3%)
  other arithmetic  2.22 us (1%)
  between operations  1.79 us (1%)
    ppermute x35, waiting for transfers between devices, swap(): return lax.ppermute(value, axis, [(i, i ^ mask) for i in range(size)])  53.5 us
    ppermute x35, starting transfers between devices, swap(): return lax.ppermute(value, axis, [(i, i ^ mask) for i in range(size)])  32.9 us
    pallas_call x2, Pallas kernels, after_attention(): pl.pallas_call(lambda *refs: layer_kernel(*refs, own=own), in_specs=[VMEM...  16.8 us
    pallas_call x1, Pallas kernels, attn_bwd(): pl.pallas_call(lambda *refs: attn_bwd_kernel(*refs, parts=len(keys)), gri...  13.8 us
    pallas_call x1, Pallas kernels, attn_fwd(): pl.pallas_call(lambda *refs: attn_fwd_kernel(*refs, parts=len(keys)), gri...  7.95 us
    pallas_call x3, Pallas kernels, assemble(): pl.pallas_call(lambda *refs: assemble_kernel(*refs, plan=plan, places=pla...  6.31 us
    pallas_call x2, Pallas kernels, half_share_grads(): pl.pallas_call(lambda *refs: half_share_kernel(*refs, plan=plan, low=low)...  4.97 us
    pallas_call x1, Pallas kernels, full_share_grads(): pl.pallas_call(lambda *refs: full_share_kernel(*refs, n_seq=n_seq), in_sp...  4.04 us
  transfers between devices with their start and end apart: 35, of which 18 were waited for; matrix products, arithmetic and copies ran while one was open for 5% of the time, Pallas kernels for 31%

profile of v3, /device:TPU:0, one launch (start us, length us, event | category | flops | bytes accessed | tf_op | source)
XLA Modules:
  0.0 157.2 jit_solution(17237645797176924118)
XLA Ops:
  0.7 3.0 %collective-permute-start = (bf16[256,768]{1,0:T(8,128)(2,1)}, bf16[256,768]{1,0:T(8,128)(2,1)S(1)}, u32[]{:S(2)}, u32[]{:S(2)}) collective-permute-start(bf16[256,768]{1,0:T(8,128)(2,1)} %bitcast.73), channel_id=1, source_target_pairs={{0,2},{1,3},{2,0},{3,1},{4,6},{5,7},{6,4},{7,5},{8,10},{9,11},{10,... | collective-permute-start | bytes 1179656 | tf_op jit(solution)/shard_map/ppermute | solution.py:363
  4.5 0.8 copy.36.refs_2_
  5.3 0.7 constant_dynamic-update-slice_fusion.6
  6.0 0.7 constant_dynamic-update-slice_fusion.5
  6.8 0.7 block_bias.1.refs_1_
  7.6 0.4 copy-done
  8.1 0.4 copy-done.2
  8.5 0.4 copy-done.3
  8.9 1.7 %project_near.1 = (bf16[256,768]{1,0:T(8,128)(2,1)S(1)}, bf16[256,768]{1,0:T(8,128)(2,1)S(1)}, bf16[256,768]{1,0:T(8,128)(2,1)S(1)}, bf16[256,768]{1,0:T(8,128)(2,1)S(1)}, bf16[256,768]{1,0:T(8,128)(2,1)S(1)}) custom-call(bf16[768,768]{1,0:T(8,128)(2,1)S(1)} %copy-done.2, bf16[768,768]{1,0:T(8,128)(2,1)S(1)} %copy-done.3, bf16[768]{0:T(1024)(128)(2,1)S(1)} %copy-done.5, ...), custom_call_target="tpu_custom_call" | custom-call | flops 1100000000 | tf_op jit(solution)/shard_map/project_near/pallas_call | solution.py:92
  10.6 3.3 %collective-permute-done.refs_3_.refs_0_.refs_7_ = bf16[256,768]{1,0:T(8,128)(2,1)S(1)} collective-permute-done((bf16[256,768]{1,0:T(8,128)(2,1)}, bf16[256,768]{1,0:T(8,128)(2,1)S(1)}, u32[]{:S(2)}, u32[]{:S(2)}) %collective-permute-start) | collective-permute-done | bytes 393248 | tf_op jit(solution)/shard_map/ppermute | solution.py:363
  13.9 0.8 project_far.2
  14.7 0.9 collective-permute-done.2.refs_3_.refs_8_
  15.6 0.8 project_far.3
  16.4 8.0 %attn_fwd.1 = (bf16[256,768]{1,0:T(8,128)(2,1)S(1)}, f32[256,768]{1,0:T(8,128)S(1)}) custom-call(bf16[256,768]{1,0:T(8,128)(2,1)S(1)} %get-tuple-element.100.refs_0_, f32[4,1024]{1,0:T(4,128)S(1)} %block_bias.1.refs_1_, bf16[256,768]{1,0:T(8,128)(2,1)S(1)} %get-tuple-element.103.refs_2_.refs_4_, bf16[256,768]{1,0:T(8,128)(2,1)S(1)} %get-tuple-element.104.refs_3_.refs_5_, ...), custom_call_target="tpu_custom_call" | custom-call | flops 11000000512 | tf_op jit(solution)/shard_map/attn_fwd/pallas_call | solution.py:175
  24.4 2.1 %collective-permute-start.3 = (bf16[256,768]{1,0:T(8,128)(2,1)S(1)}, bf16[256,768]{1,0:T(8,128)(2,1)S(1)}, u32[]{:S(2)}, u32[]{:S(2)}) collective-permute-start(bf16[256,768]{1,0:T(8,128)(2,1)S(1)} %get-tuple-element.112.refs_1_.refs_5_), channel_id=1, source_target_pairs={{0,2},{1,3},{2,0},{3,1},{4,6},{5,7},{6,4},{7,5},{8,10},{9,11},{10,... | collective-permute-start | bytes 1179656 | tf_op jit(solution)/shard_map/ppermute | solution.py:363
  26.5 9.1 %layer_own.1 = (bf16[256,768]{1,0:T(8,128)(2,1)S(1)}, bf16[256,3072]{1,0:T(8,128)(2,1)S(1)}, bf16[256,768]{1,0:T(8,128)(2,1)S(1)}, bf16[256,3072]{1,0:T(8,128)(2...) custom-call(bf16[256,768]{1,0:T(8,128)(2,1)S(1)} %bitcast.76, ...), custom_call_target="tpu_custom_call" | custom-call | flops 9900000256 | tf_op jit(solution)/shard_map/layer_own/pallas_call | solution.py:677
  35.9 7.7 %layer_other.1 = (bf16[256,768]{1,0:T(8,128)(2,1)S(1)}, bf16[256,3072]{1,0:T(8,128)(2,1)S(1)}, bf16[256,768]{1,0:T(8,128)(2,1)S(1)}, bf16[256,3072]{1,0:T(8,128)(2,1)S(1)}, bf16[256,768]{1,0:T(8,128)(2,1)S(1)}) custom-call(bf16[256,768]{1,0:T(8,128)(2,1)S(1)} %collective-permute-done.refs_3_.refs_0_.refs_7_, ...), custom_call_target="tpu_custom_call" | custom-call | flops 9900000256 | tf_op jit(solution)/shard_map/layer_other/pallas_call | solution.py:677
  43.6 2.7 %grads_up_proj.1 = (bf16[1,2,4,240,384]{4,3,2,1,0:T(8,128)(2,1)S(1)}, bf16[1,2,4,240,384]{4,3,2,1,0:T(8,128)(2,1)S(1)}) custom-call(s32[4]{0:T(128)S(1)} %pad_add_fusion.refs_0_, bf16[256,768]{1,0:T(8,128)(2,1)S(1)} %get-tuple-element.125.refs_1_, bf16[256,3072]{1,0:T(8,128)(2,1)S(1)} %get-tuple-element.126.refs_2_, ...), custom_call_target="tpu_custom_call" | custom-call | flops 11000000 | tf_op jit(solution)/shard_map/grads_up_proj/pallas_call | solution.py:267
  46.4 2.2 %grads_down.1 = (bf16[1,2,4,192,384]{4,3,2,1,0:T(8,128)(2,1)S(1)}, bf16[1,2,4,192,384]{4,3,2,1,0:T(8,128)(2,1)S(1)}) custom-call(s32[4]{0:T(128)S(1)} %pad_add_fusion.refs_0_, bf16[256,3072]{1,0:T(8,128)(2,1)S(1)} %get-tuple-element.117.refs_1_, bf16[256,768]{1,0:T(8,128)(2,1)S(1)} %get-tuple-element.118.refs_2_, ...), custom_call_target="tpu_custom_call" | custom-call | flops 11000000 | tf_op jit(solution)/shard_map/grads_down/pallas_call | solution.py:267
  48.7 0.6 collective-permute-start.5
  49.2 0.4 collective-permute-done.6
  49.9 1.8 %collective-permute-start.8 = (bf16[4,240,384]{2,1,0:T(8,128)(2,1)S(1)}, bf16[4,240,384]{2,1,0:T(8,128)(2,1)S(1)}, u32[]{:S(2)}, u32[]{:S(2)}) collective-permute-start(bf16[4,240,384]{2,1,0:T(8,128)(2,1)S(1)} %fusion.2), channel_id=1, source_target_pairs={{0,4},{4,0},{8,12},{12,8},{16,20},{20,16},{24,28},{28,24},{1,5},{5... | collective-permute-start | bytes 2211848 | tf_op jit(solution)/shard_map/ppermute | solution.py:363
  51.9 1.9 %collective-permute-start.7 = (bf16[2,2,192,384]{3,2,1,0:T(8,128)(2,1)S(1)}, bf16[2,2,192,384]{3,2,1,0:T(8,128)(2,1)S(1)}, u32[]{:S(2)}, u32[]{:S(2)}) collective-permute-start(bf16[2,2,192,384]{3,2,1,0:T(8,128)(2,1)S(1)} %add_convert_fusion.1), channel_id=1, source_target_pairs={{0,8},{4,12},{8,0},{12,4},{16,24},{20,28},{24,16},{28,20},{1,9},{5... | collective-permute-start | bytes 1769480 | tf_op jit(solution)/shard_map/ppermute | solution.py:363
  53.8 13.8 %attn_bwd.1 = (bf16[256,768]{1,0:T(8,128)(2,1)S(1)}, bf16[1024,768]{1,0:T(8,128)(2,1)S(1)}, bf16[1024,768]{1,0:T(8,128)(2,1)S(1)}) custom-call(bf16[256,768]{1,0:T(8,128)(2,1)S(1)} %get-tuple-element.100.refs_0_, f32[4,1024]{1,0:T(4,128)S(1)} %block_bias.1.refs_1_, bf16[256,768]{1,0:T(8,128)(2,1)S(1)} %get-tuple-element.135.refs_2_, ...), custom_call_target="tpu_custom_call" | custom-call | flops 11000000 | tf_op jit(solution)/shard_map/attn_bwd/pallas_call | solution.py:193
  67.5 4.0 %grads_qkv.1 = (bf16[2,2,4,144,384]{4,3,2,1,0:T(8,128)(2,1)S(1)}, bf16[2,2,4,144,384]{4,3,2,1,0:T(8,128)(2,1)S(1)}, f32[16,768]{1,0:T(8,128)S(1)}) custom-call(s32[4]{0:T(128)S(1)} %pad_add_fusion.refs_0_, bf16[256,768]{1,0:T(8,128)(2,1)S(1)} %get-tuple-element.137.refs_1_, bf16[1024,768]{1,0:T(8,128)(2,1)S(1)} %get-tuple-element.144.refs_2_.refs_0_, ...), custom_call_target="tpu_custom_call" | custom-call | flops 11000000 | tf_op jit(solution)/shard_map/grads_qkv/pallas_call | solution.py:315
  72.0 2.7 %token_terms.1 = (bf16[512,768]{1,0:T(8,128)(2,1)S(1)}, bf16[544,768]{1,0:T(8,128)(2,1)S(1)}) custom-call(bf16[1024,768]{1,0:T(8,128)(2,1)S(1)} %get-tuple-element.144.refs_2_.refs_0_, bf16[1024,768]{1,0:T(8,128)(2,1)S(1)} %get-tuple-element.145.refs_3_.refs_1_, bf16[768,768]{1,0:T(8,128)(2,1)S(1)} %copy-done.2, bf16[768,768]{1,0:T(8,128)(2,1)S(1)} %copy-done.3, ...), custom_call_target="tpu_custom_call" | custom-call | flops 13200000000 | tf_op jit(solution)/shard_map/token_terms/pallas_call | solution.py:539
  74.7 0.5 collective-permute-start.9
  75.2 1.5 collective-permute-start.12
  76.7 0.5 collective-permute-start.15
  77.2 1.6 %collective-permute-start.13 = (bf16[2,2,144,384]{3,2,1,0:T(8,128)(2,1)S(1)}, bf16[2,2,144,384]{3,2,1,0:T(8,128)(2,1)S(1)}, u32[]{:S(2)}, u32[]{:S(2)}) collective-permute-start(bf16[2,2,144,384]{3,2,1,0:T(8,128)(2,1)S(1)} %fusion.4), channel_id=1, source_target_pairs={{0,2},{1,3},{2,0},{3,1},{4,6},{5,7},{6,4},{7,5},{8,10},{9,11},{10,... | collective-permute-start | bytes 1327112 | tf_op jit(solution)/shard_map/ppermute | solution.py:363
  79.0 0.6 collective-permute-start.14
  80.1 6.9 %collective-permute-done.15 = bf16[2,240,384]{2,1,0:T(8,128)(2,1)S(1)} collective-permute-done((bf16[2,240,384]{2,1,0:T(8,128)(2,1)S(1)}, bf16[2,240,384]{2,1,0:T(8,128)(2,1)S(1)}, u32[]{:S(2)}, u32[]{:S(2)}) %collective-permute-start.15) | collective-permute-done | bytes 368672 | tf_op jit(solution)/shard_map/ppermute | solution.py:363
  87.0 2.7 %collective-permute-start.19 = (bf16[1,240,384]{2,1,0:T(8,128)(2,1)S(1)}, bf16[1,240,384]{2,1,0:T(8,128)(2,1)S(1)}, u32[]{:S(2)}, u32[]{:S(2)}) collective-permute-start(bf16[1,240,384]{2,1,0:T(8,128)(2,1)S(1)} %fusion.14), channel_id=1, source_target_pairs={{0,16},{4,20},{8,24},{12,28},{16,0},{20,4},{24,8},{28,12},{1,17},{... | collective-permute-start | bytes 552968 | tf_op jit(solution)/shard_map/ppermute | solution.py:363
  89.7 0.7 collective-permute-done.13
  90.4 3.2 %collective-permute-done.14 = bf16[2,2,144,384]{3,2,1,0:T(8,128)(2,1)S(1)} collective-permute-done((bf16[2,2,144,384]{3,2,1,0:T(8,128)(2,1)S(1)}, bf16[2,2,144,384]{3,2,1,0:T(8,128)(2,1)S(1)}, u32[]{:S(2)}, u32[]{:S(2)}) %collective-permute-start.14) | collective-permute-done | bytes 442400 | tf_op jit(solution)/shard_map/ppermute | solution.py:363
  93.8 1.5 collective-permute-start.17
  95.4 1.6 collective-permute-start.18
  97.0 2.6 %collective-permute-start.16 = (bf16[1,192,384]{2,1,0:T(8,128)(2,1)S(1)}, bf16[1,192,384]{2,1,0:T(8,128)(2,1)S(1)}, u32[]{:S(2)}, u32[]{:S(2)}) collective-permute-start(bf16[1,192,384]{2,1,0:T(8,128)(2,1)S(1)} %fusion.16), channel_id=1, source_target_pairs={{0,16},{4,20},{8,24},{12,28},{16,0},{20,4},{24,8},{28,12},{1,17},{... | collective-permute-start | bytes 442376 | tf_op jit(solution)/shard_map/ppermute | solution.py:363
  99.8 0.4 collective-permute-start.23
  100.5 2.7 %collective-permute-done.18 = bf16[2,144,384]{2,1,0:T(8,128)(2,1)S(1)} collective-permute-done((bf16[2,144,384]{2,1,0:T(8,128)(2,1)S(1)}, bf16[2,144,384]{2,1,0:T(8,128)(2,1)S(1)}, u32[]{:S(2)}, u32[]{:S(2)}) %collective-permute-start.18) | collective-permute-done | bytes 221216 | tf_op jit(solution)/shard_map/ppermute | solution.py:363
  103.2 1.6 %collective-permute-start.20 = (bf16[2,144,384]{2,1,0:T(8,128)(2,1)S(1)}, bf16[2,144,384]{2,1,0:T(8,128)(2,1)S(1)}, u32[]{:S(2)}, u32[]{:S(2)}) collective-permute-start(bf16[2,144,384]{2,1,0:T(8,128)(2,1)S(1)} %fusion.7), channel_id=1, source_target_pairs={{0,8},{4,12},{8,0},{12,4},{16,24},{20,28},{24,16},{28,20},{1,9},{5... | collective-permute-start | bytes 663560 | tf_op jit(solution)/shard_map/ppermute | solution.py:363
  104.9 5.5 %collective-permute-done.16 = bf16[1,192,384]{2,1,0:T(8,128)(2,1)S(1)} collective-permute-done((bf16[1,192,384]{2,1,0:T(8,128)(2,1)S(1)}, bf16[1,192,384]{2,1,0:T(8,128)(2,1)S(1)}, u32[]{:S(2)}, u32[]{:S(2)}) %collective-permute-start.16) | collective-permute-done | bytes 147488 | tf_op jit(solution)/shard_map/ppermute | solution.py:363
  110.6 0.6 collective-permute-start.22
  111.2 4.5 %collective-permute-done.20 = bf16[2,144,384]{2,1,0:T(8,128)(2,1)S(1)} collective-permute-done((bf16[2,144,384]{2,1,0:T(8,128)(2,1)S(1)}, bf16[2,144,384]{2,1,0:T(8,128)(2,1)S(1)}, u32[]{:S(2)}, u32[]{:S(2)}) %collective-permute-start.20) | collective-permute-done | bytes 221216 | tf_op jit(solution)/shard_map/ppermute | solution.py:363
  115.9 1.6 %collective-permute-done.23 = bf16[1,240,384]{2,1,0:T(8,128)(2,1)S(1)} collective-permute-done((bf16[1,240,384]{2,1,0:T(8,128)(2,1)S(1)}, bf16[1,240,384]{2,1,0:T(8,128)(2,1)S(1)}, u32[]{:S(2)}, u32[]{:S(2)}) %collective-permute-start.23) | collective-permute-done | bytes 184352 | tf_op jit(solution)/shard_map/ppermute | solution.py:363
  117.5 1.2 collective-permute-start.29
  118.7 0.6 collective-permute-start.30
  119.3 5.2 %collective-permute-done.21 = bf16[1,144,384]{2,1,0:T(8,128)(2,1)S(1)} collective-permute-done((bf16[1,144,384]{2,1,0:T(8,128)(2,1)S(1)}, bf16[1,144,384]{2,1,0:T(8,128)(2,1)S(1)}, u32[]{:S(2)}, u32[]{:S(2)}) %collective-permute-start.21) | collective-permute-done | bytes 110624 | tf_op jit(solution)/shard_map/ppermute | solution.py:363
  124.8 0.6 collective-permute-start.28
  125.4 6.7 %collective-permute-done.24 = bf16[1,144,384]{2,1,0:T(8,128)(2,1)S(1)} collective-permute-done((bf16[1,144,384]{2,1,0:T(8,128)(2,1)S(1)}, bf16[1,144,384]{2,1,0:T(8,128)(2,1)S(1)}, u32[]{:S(2)}, u32[]{:S(2)}) %collective-permute-start.24) | collective-permute-done | bytes 110624 | tf_op jit(solution)/shard_map/ppermute | solution.py:363
  132.2 2.0 %collective-permute-start.27 = (f32[16,768]{1,0:T(8,128)S(1)}, f32[16,768]{1,0:T(8,128)S(1)}, u32[]{:S(2)}, u32[]{:S(2)}) collective-permute-start(f32[16,768]{1,0:T(8,128)S(1)} %add.343), channel_id=1, source_target_pairs={{0,8},{4,12},{8,0},{12,4},{16,24},{20,28},{24,16},{28,20},{1,9},{5... | collective-permute-start | bytes 147464 | tf_op jit(solution)/shard_map/ppermute | solution.py:363
  134.3 1.3 collective-permute-start.33
  135.6 0.5 collective-permute-start.32
  136.1 6.0 %collective-permute-done.27 = f32[16,768]{1,0:T(8,128)S(1)} collective-permute-done((f32[16,768]{1,0:T(8,128)S(1)}, f32[16,768]{1,0:T(8,128)S(1)}, u32[]{:S(2)}, u32[]{:S(2)}) %collective-permute-start.27) | collective-permute-done | bytes 49184 | tf_op jit(solution)/shard_map/ppermute | solution.py:363
  142.3 0.6 collective-permute-start.31
  142.9 1.4 fusion.1
  144.3 1.5 collective-permute-done.32.refs_4_
  145.8 2.4 %assemble_U.1 = (f32[192,3072]{1,0:T(8,128)}, f32[192,768]{1,0:T(8,128)}) custom-call(s32[4]{0:T(128)S(1)} %pad_add_fusion.refs_0_, bf16[2,240,384]{2,1,0:T(8,128)(2,1)S(1)} %pad_maximum_fusion.3.refs_1_, bf16[2,240,384]{2,1,0:T(8,128)(2,1)S(1)} %collective-permute-done.29.refs_2_, bf16[2,240,384]{2,1,0:T(8,128)(2,1)S(1)} %collective-permute-done.30.refs_3_, ...), custom_call_target="tpu_custom_call" | custom-call | flops 11000000 | tf_op jit(solution)/shard_map/assemble_U/pallas_call | solution.py:350
  148.2 2.9 %collective-permute-done.34 = f32[16,768]{1,0:T(8,128)S(1)} collective-permute-done((f32[16,768]{1,0:T(8,128)S(1)}, f32[16,768]{1,0:T(8,128)S(1)}, u32[]{:S(2)}, u32[]{:S(2)}) %collective-permute-start.34) | collective-permute-done | bytes 49184 | tf_op jit(solution)/shard_map/ppermute | solution.py:363
  151.1 0.6 slice.395
  151.7 0.7 slice_reduce_fusion
  152.4 0.9 collective-permute-done.33.refs_2_
  153.3 2.1 %assemble_D.1 = f32[768,768]{1,0:T(8,128)} custom-call(s32[4]{0:T(128)S(1)} %pad_add_fusion.refs_0_, bf16[4,192,384]{2,1,0:T(8,128)(2,1)S(1)} %pad_maximum_fusion.refs_1_, bf16[4,192,384]{2,1,0:T(8,128)(2,1)S(1)} %collective-permute-done.33.refs_2_), custom_call_target="tpu_custom_call" | custom-call | flops 11000000 | tf_op jit(solution)/shard_map/assemble_D/pallas_call | solution.py:350
  155.4 1.9 %assemble_C.1 = (f32[192,768]{1,0:T(8,128)}, f32[192,768]{1,0:T(8,128)}, f32[192,768]{1,0:T(8,128)}) custom-call(s32[4]{0:T(128)S(1)} %pad_add_fusion.refs_0_, bf16[4,144,384]{2,1,0:T(8,128)(2,1)S(1)} %pad_maximum_fusion.2.refs_1_, bf16[4,144,384]{2,1,0:T(8,128)(2,1)S(1)} %collective-permute-done.31.refs_2_), custom_call_target="tpu_custom_call" | custom-call | flops 11000000 | tf_op jit(solution)/shard_map/assemble_C/pallas_call | solution.py:350
  (96 shorter events, 4.1 us)
Async XLA Ops:
  0.7 13.2 %collective-permute-start = (bf16[256,768]{1,0:T(8,128)(2,1)}, bf16[256,768]{1,0:T(8,128)(2,1)S(1)}, u32[]{:S(2)}, u32[]{:S(2)}) collective-permute-start(bf16[256,768]{1,0:T(8,128)(2,1)} %bitcast.73), channel_id=1, source_target_pairs={{0,2},{1,3},{2,0},{3,1},{4,6},{5,7},{6,4},{7,5},{8,10},{9,11},{10,... | collective-permute-start | bytes 1179656 | tf_op jit(solution)/shard_map/ppermute | solution.py:363
  3.7 3.9 %collective-permute-start.1 = (bf16[256,768]{1,0:T(8,128)(2,1)}, bf16[256,768]{1,0:T(8,128)(2,1)S(1)}, u32[]{:S(2)}, u32[]{:S(2)}) collective-permute-start(bf16[256,768]{1,0:T(8,128)(2,1)} %bitcast.74), channel_id=1, source_target_pairs={{0,1},{1,0},{2,3},{3,2},{4,5},{5,4},{6,7},{7,6},{8,9},{9,8},{10,11... | collective-permute-start | bytes 1179656 | tf_op jit(solution)/shard_map/ppermute | solution.py:363
  3.7 32.2 %collective-permute-start.4 = (bf16[256,768]{1,0:T(8,128)(2,1)}, bf16[256,768]{1,0:T(8,128)(2,1)S(1)}, u32[]{:S(2)}, u32[]{:S(2)}) collective-permute-start(bf16[256,768]{1,0:T(8,128)(2,1)} %bitcast.86), channel_id=1, source_target_pairs={{0,2},{1,3},{2,0},{3,1},{4,6},{5,7},{6,4},{7,5},{8,10},{9,11},{10,... | collective-permute-start | bytes 1179656 | tf_op jit(solution)/shard_map/ppermute | solution.py:363
  6.7 0.8 copy-start.9
  6.7 0.8 copy-start.10
  6.7 1.3 copy-start
  6.7 1.4 copy-start.1
  6.7 1.8 %copy-start.2 = (bf16[768,768]{1,0:T(8,128)(2,1)S(1)}, bf16[768,768]{1,0:T(8,128)(2,1)}, u32[]{:S(2)}) copy-start(bf16[768,768]{1,0:T(8,128)(2,1)} %refs_2_.8) | copy-start | bytes 3538948
  6.7 2.1 %copy-start.3 = (bf16[768,768]{1,0:T(8,128)(2,1)S(1)}, bf16[768,768]{1,0:T(8,128)(2,1)}, u32[]{:S(2)}) copy-start(bf16[768,768]{1,0:T(8,128)(2,1)} %refs_3_.5) | copy-start | bytes 3538948
  6.8 2.1 %copy-start.4 = (bf16[768]{0:T(1024)(128)(2,1)S(1)}, bf16[768]{0:T(1024)(128)(2,1)}, u32[]{:S(2)}) copy-start(bf16[768]{0:T(1024)(128)(2,1)} %refs_6_.1) | copy-start | bytes 4612
  6.8 2.1 %copy-start.5 = (bf16[768]{0:T(1024)(128)(2,1)S(1)}, bf16[768]{0:T(1024)(128)(2,1)}, u32[]{:S(2)}) copy-start(bf16[768]{0:T(1024)(128)(2,1)} %refs_2_.7) | copy-start | bytes 4612
  7.5 6.3 %copy-start.11 = (bf16[768]{0:T(1024)(128)(2,1)S(1)}, bf16[768]{0:T(1024)(128)(2,1)}, u32[]{:S(2)}) copy-start(bf16[768]{0:T(1024)(128)(2,1)} %param.33) | copy-start | bytes 4612
  7.6 6.3 %copy-start.12 = (bf16[768]{0:T(1024)(128)(2,1)S(1)}, bf16[768]{0:T(1024)(128)(2,1)}, u32[]{:S(2)}) copy-start(bf16[768]{0:T(1024)(128)(2,1)} %param.34) | copy-start | bytes 4612
  7.6 6.3 %copy-start.8 = (bf16[3072]{0:T(1024)(128)(2,1)S(1)}, bf16[3072]{0:T(1024)(128)(2,1)}, u32[]{:S(2)}) copy-start(bf16[3072]{0:T(1024)(128)(2,1)} %param.30) | copy-start | bytes 18436
  13.8 1.7 %collective-permute-start.2 = (bf16[256,768]{1,0:T(8,128)(2,1)S(1)}, bf16[256,768]{1,0:T(8,128)(2,1)S(1)}, u32[]{:S(2)}, u32[]{:S(2)}) collective-permute-start(bf16[256,768]{1,0:T(8,128)(2,1)S(1)} %collective-permute-done.refs_3_.refs_0_.refs_7_), channel_id=1, source_target_pairs={{0,1},{1,0},{2,3},{3,2},{4,5},{5,4},{6,7},{7,6},{8,9},{9,8},{10,11... | collective-permute-start | bytes 1179656 | tf_op jit(solution)/shard_map/ppermute | solution.py:363
  15.6 10.9 %slice-start = ((s8[4718592]{0:T(1024)(128)(4,1)}), s8[4194304]{0:T(1024)(128)(4,1)S(1)}, s32[]{:S(2)}) async-start(s8[4718592]{0:T(1024)(128)(4,1)} %bitcast.82), calls=%async_computation | async-start | bytes 8388608
  15.6 10.9 %slice-start.2 = ((s8[4718592]{0:T(1024)(128)(4,1)}), s8[4194304]{0:T(1024)(128)(4,1)S(1)}, s32[]{:S(2)}) async-start(s8[4718592]{0:T(1024)(128)(4,1)} %bitcast.84), calls=%async_computation.2 | async-start | bytes 8388608
  16.4 10.1 %slice-start.1 = ((s8[4718592]{0:T(1024)(128)(4,1)}), s8[524288]{0:T(1024)(128)(4,1)S(1)}, s32[]{:S(2)}) async-start(s8[4718592]{0:T(1024)(128)(4,1)} %bitcast.82), calls=%async_computation.1 | async-start | bytes 1048576
  16.4 10.1 %slice-start.3 = ((s8[4718592]{0:T(1024)(128)(4,1)}), s8[524288]{0:T(1024)(128)(4,1)S(1)}, s32[]{:S(2)}) async-start(s8[4718592]{0:T(1024)(128)(4,1)} %bitcast.84), calls=%async_computation.3 | async-start | bytes 1048576
  16.4 10.1 %copy-start.6 = (bf16[768,768]{1,0:T(8,128)(2,1)S(1)}, bf16[768,768]{1,0:T(8,128)(2,1)}, u32[]{:S(2)}) copy-start(bf16[768,768]{1,0:T(8,128)(2,1)} %refs_3_.4) | copy-start | bytes 3538948
  16.4 10.1 %copy-start.7 = (bf16[1,256,768]{2,1,0:T(8,128)(2,1)S(1)}, bf16[1,256,768]{2,1,0:T(8,128)(2,1)}, u32[]{:S(2)}) copy-start(bf16[1,256,768]{2,1,0:T(8,128)(2,1)} %param.37) | copy-start | bytes 1179652
  24.4 11.5 %collective-permute-start.3 = (bf16[256,768]{1,0:T(8,128)(2,1)S(1)}, bf16[256,768]{1,0:T(8,128)(2,1)S(1)}, u32[]{:S(2)}, u32[]{:S(2)}) collective-permute-start(bf16[256,768]{1,0:T(8,128)(2,1)S(1)} %get-tuple-element.112.refs_1_.refs_5_), channel_id=1, source_target_pairs={{0,2},{1,3},{2,0},{3,1},{4,6},{5,7},{6,4},{7,5},{8,10},{9,11},{10,... | collective-permute-start | bytes 1179656 | tf_op jit(solution)/shard_map/ppermute | solution.py:363
  46.4 3.3 %collective-permute-start.6 = (bf16[1,2,4,240,384]{4,3,2,1,0:T(8,128)(2,1)S(1)}, bf16[1,2,4,240,384]{4,3,2,1,0:T(8,128)(2,1)S(1)}, u32[]{:S(2)}, u32[]{:S(2)}) collective-permute-start(bf16[1,2,4,240,384]{4,3,2,1,0:T(8,128)(2,1)S(1)} %get-tuple-element.132), channel_id=1, source_target_pairs={{0,1},{1,0},{2,3},{3,2},{4,5},{5,4},{6,7},{7,6},{8,9},{9,8},{10,11... | collective-permute-start | bytes 4423688 | tf_op jit(solution)/shard_map/ppermute | solution.py:363
  48.7 3.0 %collective-permute-start.5 = (bf16[1,2,4,192,384]{4,3,2,1,0:T(8,128)(2,1)S(1)}, bf16[1,2,4,192,384]{4,3,2,1,0:T(8,128)(2,1)S(1)}, u32[]{:S(2)}, u32[]{:S(2)}) collective-permute-start(bf16[1,2,4,192,384]{4,3,2,1,0:T(8,128)(2,1)S(1)} %get-tuple-element.124), channel_id=1, source_target_pairs={{0,1},{1,0},{2,3},{3,2},{4,5},{5,4},{6,7},{7,6},{8,9},{9,8},{10,11... | collective-permute-start | bytes 3538952 | tf_op jit(solution)/shard_map/ppermute | solution.py:363
  49.9 21.8 %collective-permute-start.8 = (bf16[4,240,384]{2,1,0:T(8,128)(2,1)S(1)}, bf16[4,240,384]{2,1,0:T(8,128)(2,1)S(1)}, u32[]{:S(2)}, u32[]{:S(2)}) collective-permute-start(bf16[4,240,384]{2,1,0:T(8,128)(2,1)S(1)} %fusion.2), channel_id=1, source_target_pairs={{0,4},{4,0},{8,12},{12,8},{16,20},{20,16},{24,28},{28,24},{1,5},{5... | collective-permute-start | bytes 2211848 | tf_op jit(solution)/shard_map/ppermute | solution.py:363
  51.9 20.0 %collective-permute-start.7 = (bf16[2,2,192,384]{3,2,1,0:T(8,128)(2,1)S(1)}, bf16[2,2,192,384]{3,2,1,0:T(8,128)(2,1)S(1)}, u32[]{:S(2)}, u32[]{:S(2)}) collective-permute-start(bf16[2,2,192,384]{3,2,1,0:T(8,128)(2,1)S(1)} %add_convert_fusion.1), channel_id=1, source_target_pairs={{0,8},{4,12},{8,0},{12,4},{16,24},{20,28},{24,16},{28,20},{1,9},{5... | collective-permute-start | bytes 1769480 | tf_op jit(solution)/shard_map/ppermute | solution.py:363
  71.6 5.5 %collective-permute-start.10 = (bf16[2,2,4,144,384]{4,3,2,1,0:T(8,128)(2,1)S(1)}, bf16[2,2,4,144,384]{4,3,2,1,0:T(8,128)(2,1)S(1)}, u32[]{:S(2)}, u32[]{:S(2)}) collective-permute-start(bf16[2,2,4,144,384]{4,3,2,1,0:T(8,128)(2,1)S(1)} %get-tuple-element.141), channel_id=1, source_target_pairs={{0,1},{1,0},{2,3},{3,2},{4,5},{5,4},{6,7},{7,6},{8,9},{9,8},{10,11... | collective-permute-start | bytes 5308424 | tf_op jit(solution)/shard_map/ppermute | solution.py:363
  74.7 4.9 %collective-permute-start.9 = (bf16[544,768]{1,0:T(8,128)(2,1)S(1)}, bf16[544,768]{1,0:T(8,128)(2,1)S(1)}, u32[]{:S(2)}, u32[]{:S(2)}) collective-permute-start(bf16[544,768]{1,0:T(8,128)(2,1)S(1)} %get-tuple-element.148), channel_id=1, source_target_pairs={{0,1},{1,0},{2,3},{3,2},{4,5},{5,4},{6,7},{7,6},{8,9},{9,8},{10,11... | collective-permute-start | bytes 2506760 | tf_op jit(solution)/shard_map/ppermute | solution.py:363
  75.2 21.8 %collective-permute-start.12 = (bf16[2,192,384]{2,1,0:T(8,128)(2,1)S(1)}, bf16[2,192,384]{2,1,0:T(8,128)(2,1)S(1)}, u32[]{:S(2)}, u32[]{:S(2)}) collective-permute-start(bf16[2,192,384]{2,1,0:T(8,128)(2,1)S(1)} %fusion.15), channel_id=1, source_target_pairs={{0,4},{4,0},{8,12},{12,8},{16,20},{20,16},{24,28},{28,24},{1,5},{5... | collective-permute-start | bytes 884744 | tf_op jit(solution)/shard_map/ppermute | solution.py:363
  76.7 10.3 %collective-permute-start.15 = (bf16[2,240,384]{2,1,0:T(8,128)(2,1)S(1)}, bf16[2,240,384]{2,1,0:T(8,128)(2,1)S(1)}, u32[]{:S(2)}, u32[]{:S(2)}) collective-permute-start(bf16[2,240,384]{2,1,0:T(8,128)(2,1)S(1)} %fusion.3), channel_id=1, source_target_pairs={{0,8},{4,12},{8,0},{12,4},{16,24},{20,28},{24,16},{28,20},{1,9},{5... | collective-permute-start | bytes 1105928 | tf_op jit(solution)/shard_map/ppermute | solution.py:363
  77.2 13.2 %collective-permute-start.13 = (bf16[2,2,144,384]{3,2,1,0:T(8,128)(2,1)S(1)}, bf16[2,2,144,384]{3,2,1,0:T(8,128)(2,1)S(1)}, u32[]{:S(2)}, u32[]{:S(2)}) collective-permute-start(bf16[2,2,144,384]{3,2,1,0:T(8,128)(2,1)S(1)} %fusion.4), channel_id=1, source_target_pairs={{0,2},{1,3},{2,0},{3,1},{4,6},{5,7},{6,4},{7,5},{8,10},{9,11},{10,... | collective-permute-start | bytes 1327112 | tf_op jit(solution)/shard_map/ppermute | solution.py:363
  79.0 14.7 %collective-permute-start.14 = (bf16[2,2,144,384]{3,2,1,0:T(8,128)(2,1)S(1)}, bf16[2,2,144,384]{3,2,1,0:T(8,128)(2,1)S(1)}, u32[]{:S(2)}, u32[]{:S(2)}) collective-permute-start(bf16[2,2,144,384]{3,2,1,0:T(8,128)(2,1)S(1)} %fusion.5), channel_id=1, source_target_pairs={{0,4},{4,0},{8,12},{12,8},{16,20},{20,16},{24,28},{28,24},{1,5},{5... | collective-permute-start | bytes 1327112 | tf_op jit(solution)/shard_map/ppermute | solution.py:363
  79.7 30.8 %collective-permute-start.11 = (bf16[288,768]{1,0:T(8,128)(2,1)S(1)}, bf16[288,768]{1,0:T(8,128)(2,1)S(1)}, u32[]{:S(2)}, u32[]{:S(2)}) collective-permute-start(bf16[288,768]{1,0:T(8,128)(2,1)S(1)} %pad_maximum_fusion.1), channel_id=1, source_target_pairs={{0,2},{1,3},{2,0},{3,1},{4,6},{5,7},{6,4},{7,5},{8,10},{9,11},{10,... | collective-permute-start | bytes 1327112 | tf_op jit(solution)/shard_map/ppermute | solution.py:363
  87.0 12.6 %collective-permute-start.19 = (bf16[1,240,384]{2,1,0:T(8,128)(2,1)S(1)}, bf16[1,240,384]{2,1,0:T(8,128)(2,1)S(1)}, u32[]{:S(2)}, u32[]{:S(2)}) collective-permute-start(bf16[1,240,384]{2,1,0:T(8,128)(2,1)S(1)} %fusion.14), channel_id=1, source_target_pairs={{0,16},{4,20},{8,24},{12,28},{16,0},{20,4},{24,8},{28,12},{1,17},{... | collective-permute-start | bytes 552968 | tf_op jit(solution)/shard_map/ppermute | solution.py:363
  93.8 6.6 %collective-permute-start.17 = (bf16[2,144,384]{2,1,0:T(8,128)(2,1)S(1)}, bf16[2,144,384]{2,1,0:T(8,128)(2,1)S(1)}, u32[]{:S(2)}, u32[]{:S(2)}) collective-permute-start(bf16[2,144,384]{2,1,0:T(8,128)(2,1)S(1)} %get-tuple-element.192), channel_id=1, source_target_pairs={{0,4},{4,0},{8,12},{12,8},{16,20},{20,16},{24,28},{28,24},{1,5},{5... | collective-permute-start | bytes 663560 | tf_op jit(solution)/shard_map/ppermute | solution.py:363
  95.4 7.8 %collective-permute-start.18 = (bf16[2,144,384]{2,1,0:T(8,128)(2,1)S(1)}, bf16[2,144,384]{2,1,0:T(8,128)(2,1)S(1)}, u32[]{:S(2)}, u32[]{:S(2)}) collective-permute-start(bf16[2,144,384]{2,1,0:T(8,128)(2,1)S(1)} %get-tuple-element.191), channel_id=1, source_target_pairs={{0,2},{1,3},{2,0},{3,1},{4,6},{5,7},{6,4},{7,5},{8,10},{9,11},{10,... | collective-permute-start | bytes 663560 | tf_op jit(solution)/shard_map/ppermute | solution.py:363
  97.0 13.4 %collective-permute-start.16 = (bf16[1,192,384]{2,1,0:T(8,128)(2,1)S(1)}, bf16[1,192,384]{2,1,0:T(8,128)(2,1)S(1)}, u32[]{:S(2)}, u32[]{:S(2)}) collective-permute-start(bf16[1,192,384]{2,1,0:T(8,128)(2,1)S(1)} %fusion.16), channel_id=1, source_target_pairs={{0,16},{4,20},{8,24},{12,28},{16,0},{20,4},{24,8},{28,12},{1,17},{... | collective-permute-start | bytes 442376 | tf_op jit(solution)/shard_map/ppermute | solution.py:363
  99.8 17.7 %collective-permute-start.23 = (bf16[1,240,384]{2,1,0:T(8,128)(2,1)S(1)}, bf16[1,240,384]{2,1,0:T(8,128)(2,1)S(1)}, u32[]{:S(2)}, u32[]{:S(2)}) collective-permute-start(bf16[1,240,384]{2,1,0:T(8,128)(2,1)S(1)} %fusion.12), channel_id=1, source_target_pairs={{0,16},{4,20},{8,24},{12,28},{16,0},{20,4},{24,8},{28,12},{1,17},{... | collective-permute-start | bytes 552968 | tf_op jit(solution)/shard_map/ppermute | solution.py:363
  103.2 12.5 %collective-permute-start.20 = (bf16[2,144,384]{2,1,0:T(8,128)(2,1)S(1)}, bf16[2,144,384]{2,1,0:T(8,128)(2,1)S(1)}, u32[]{:S(2)}, u32[]{:S(2)}) collective-permute-start(bf16[2,144,384]{2,1,0:T(8,128)(2,1)S(1)} %fusion.7), channel_id=1, source_target_pairs={{0,8},{4,12},{8,0},{12,4},{16,24},{20,28},{24,16},{28,20},{1,9},{5... | collective-permute-start | bytes 663560 | tf_op jit(solution)/shard_map/ppermute | solution.py:363
  110.5 14.3 %collective-permute-start.25 = (bf16[1,192,384]{2,1,0:T(8,128)(2,1)S(1)}, bf16[1,192,384]{2,1,0:T(8,128)(2,1)S(1)}, u32[]{:S(2)}, u32[]{:S(2)}) collective-permute-start(bf16[1,192,384]{2,1,0:T(8,128)(2,1)S(1)} %fusion.18), channel_id=1, source_target_pairs={{0,16},{4,20},{8,24},{12,28},{16,0},{20,4},{24,8},{28,12},{1,17},{... | collective-permute-start | bytes 442376 | tf_op jit(solution)/shard_map/ppermute | solution.py:363
  110.6 8.7 %collective-permute-start.22 = (f32[16,768]{1,0:T(8,128)S(1)}, f32[16,768]{1,0:T(8,128)S(1)}, u32[]{:S(2)}, u32[]{:S(2)}) collective-permute-start(f32[16,768]{1,0:T(8,128)S(1)} %fusion.31), channel_id=1, source_target_pairs={{0,4},{4,0},{8,12},{12,8},{16,20},{20,16},{24,28},{28,24},{1,5},{5... | collective-permute-start | bytes 147464 | tf_op jit(solution)/shard_map/ppermute | solution.py:363
  115.8 8.8 %collective-permute-start.21 = (bf16[1,144,384]{2,1,0:T(8,128)(2,1)S(1)}, bf16[1,144,384]{2,1,0:T(8,128)(2,1)S(1)}, u32[]{:S(2)}, u32[]{:S(2)}) collective-permute-start(bf16[1,144,384]{2,1,0:T(8,128)(2,1)S(1)} %fusion.21), channel_id=1, source_target_pairs={{0,16},{4,20},{8,24},{12,28},{16,0},{20,4},{24,8},{28,12},{1,17},{... | collective-permute-start | bytes 331784 | tf_op jit(solution)/shard_map/ppermute | solution.py:363
  117.5 16.7 %collective-permute-start.29 = (bf16[2,240,384]{2,1,0:T(8,128)(2,1)S(1)}, bf16[2,240,384]{2,1,0:T(8,128)(2,1)S(1)}, u32[]{:S(2)}, u32[]{:S(2)}) collective-permute-start(bf16[2,240,384]{2,1,0:T(8,128)(2,1)S(1)} %pad_maximum_fusion.3.refs_1_), channel_id=1, source_target_pairs={{0,8},{4,12},{8,0},{12,4},{16,24},{20,28},{24,16},{28,20},{1,9},{5... | collective-permute-start | bytes 1105928 | tf_op jit(solution)/shard_map/ppermute | solution.py:363
  118.7 15.5 %collective-permute-start.30 = (bf16[2,240,384]{2,1,0:T(8,128)(2,1)S(1)}, bf16[2,240,384]{2,1,0:T(8,128)(2,1)S(1)}, u32[]{:S(2)}, u32[]{:S(2)}) collective-permute-start(bf16[2,240,384]{2,1,0:T(8,128)(2,1)S(1)} %pad_maximum_fusion.3.refs_1_), channel_id=1, source_target_pairs={{0,4},{4,0},{8,12},{12,8},{16,20},{20,16},{24,28},{28,24},{1,5},{5... | collective-permute-start | bytes 1105928 | tf_op jit(solution)/shard_map/ppermute | solution.py:363
  124.6 7.4 %collective-permute-start.24 = (bf16[1,144,384]{2,1,0:T(8,128)(2,1)S(1)}, bf16[1,144,384]{2,1,0:T(8,128)(2,1)S(1)}, u32[]{:S(2)}, u32[]{:S(2)}) collective-permute-start(bf16[1,144,384]{2,1,0:T(8,128)(2,1)S(1)} %fusion.25), channel_id=1, source_target_pairs={{0,16},{4,20},{8,24},{12,28},{16,0},{20,4},{24,8},{28,12},{1,17},{... | collective-permute-start | bytes 331784 | tf_op jit(solution)/shard_map/ppermute | solution.py:363
  124.8 9.4 %collective-permute-start.28 = (bf16[2,192,384]{2,1,0:T(8,128)(2,1)S(1)}, bf16[2,192,384]{2,1,0:T(8,128)(2,1)S(1)}, u32[]{:S(2)}, u32[]{:S(2)}) collective-permute-start(bf16[2,192,384]{2,1,0:T(8,128)(2,1)S(1)} %pad_maximum_fusion.4), channel_id=1, source_target_pairs={{0,4},{4,0},{8,12},{12,8},{16,20},{20,16},{24,28},{28,24},{1,5},{5... | collective-permute-start | bytes 884744 | tf_op jit(solution)/shard_map/ppermute | solution.py:363
  132.1 10.1 %collective-permute-start.26 = (bf16[2,144,384]{2,1,0:T(8,128)(2,1)S(1)}, bf16[2,144,384]{2,1,0:T(8,128)(2,1)S(1)}, u32[]{:S(2)}, u32[]{:S(2)}) collective-permute-start(bf16[2,144,384]{2,1,0:T(8,128)(2,1)S(1)} %pad_maximum_fusion.5), channel_id=1, source_target_pairs={{0,8},{4,12},{8,0},{12,4},{16,24},{20,28},{24,16},{28,20},{1,9},{5... | collective-permute-start | bytes 663560 | tf_op jit(solution)/shard_map/ppermute | solution.py:363
  132.2 9.9 %collective-permute-start.27 = (f32[16,768]{1,0:T(8,128)S(1)}, f32[16,768]{1,0:T(8,128)S(1)}, u32[]{:S(2)}, u32[]{:S(2)}) collective-permute-start(f32[16,768]{1,0:T(8,128)S(1)} %add.343), channel_id=1, source_target_pairs={{0,8},{4,12},{8,0},{12,4},{16,24},{20,28},{24,16},{28,20},{1,9},{5... | collective-permute-start | bytes 147464 | tf_op jit(solution)/shard_map/ppermute | solution.py:363
  134.3 19.0 %collective-permute-start.33 = (bf16[4,192,384]{2,1,0:T(8,128)(2,1)S(1)}, bf16[4,192,384]{2,1,0:T(8,128)(2,1)S(1)}, u32[]{:S(2)}, u32[]{:S(2)}) collective-permute-start(bf16[4,192,384]{2,1,0:T(8,128)(2,1)S(1)} %pad_maximum_fusion.refs_1_), channel_id=1, source_target_pairs={{0,8},{4,12},{8,0},{12,4},{16,24},{20,28},{24,16},{28,20},{1,9},{5... | collective-permute-start | bytes 1769480 | tf_op jit(solution)/shard_map/ppermute | solution.py:363
  135.6 10.2 %collective-permute-start.32 = (bf16[2,240,384]{2,1,0:T(8,128)(2,1)S(1)}, bf16[2,240,384]{2,1,0:T(8,128)(2,1)S(1)}, u32[]{:S(2)}, u32[]{:S(2)}) collective-permute-start(bf16[2,240,384]{2,1,0:T(8,128)(2,1)S(1)} %collective-permute-done.29.refs_2_), channel_id=1, source_target_pairs={{0,4},{4,0},{8,12},{12,8},{16,20},{20,16},{24,28},{28,24},{1,5},{5... | collective-permute-start | bytes 1105928 | tf_op jit(solution)/shard_map/ppermute | solution.py:363
  142.1 9.0 %collective-permute-start.34 = (f32[16,768]{1,0:T(8,128)S(1)}, f32[16,768]{1,0:T(8,128)S(1)}, u32[]{:S(2)}, u32[]{:S(2)}) collective-permute-start(f32[16,768]{1,0:T(8,128)S(1)} %add.345), channel_id=1, source_target_pairs={{0,16},{4,20},{8,24},{12,28},{16,0},{20,4},{24,8},{28,12},{1,17},{... | collective-permute-start | bytes 147464 | tf_op jit(solution)/shard_map/ppermute | solution.py:363
  142.3 13.1 %collective-permute-start.31 = (bf16[4,144,384]{2,1,0:T(8,128)(2,1)S(1)}, bf16[4,144,384]{2,1,0:T(8,128)(2,1)S(1)}, u32[]{:S(2)}, u32[]{:S(2)}) collective-permute-start(bf16[4,144,384]{2,1,0:T(8,128)(2,1)S(1)} %pad_maximum_fusion.2.refs_1_), channel_id=1, source_target_pairs={{0,4},{4,0},{8,12},{12,8},{16,20},{20,16},{24,28},{28,24},{1,5},{5... | collective-permute-start | bytes 1327112 | tf_op jit(solution)/shard_map/ppermute | solution.py:363
